TPU v7x, 32 devices: a whole 2x2x4 slice. The times are simulated.
32 devices in a mesh: section: 4 (over x, core), sub: 2 (over y), rng: 4 (over z).
Axes of the slice: x: 2, y: 2, z: 4, core: 2. Of those that a mesh axis runs over, the one named last changes fastest.
Arguments:
- echoes: bfloat16 [2, 2, 24, 16384], P(None, 'sub', 'section', 'rng'), may hold values from -6 to 6
- chirp: bfloat16 [2, 2048], replicated, may hold values from -0.25 to 0.25
- steer: bfloat16 [2, 2, 128, 24], P(None, 'sub'), may hold values from -2 to 2
- pulse_order: int32 [2, 24], P('sub'), may hold values from 0 to 23, each once within a row
- band_coef: bfloat16 [5, 2, 2, 2, 128, 16], P(None, 'sub'), may hold values from -2.5 to 2.5
- band_start: int32 [5, 2, 2, 128], P(None, 'sub'), may hold values from 0 to 112
- band_width: int32 [5, 2, 2, 128], P(None, 'sub'), may hold values from 1 to 16
Outputs:
- image: bfloat16 [2, 256, 4, 4096], P(None, 'sub', 'rng', 'section')
Inputs may be any that keep to these rules, and one draw needn't show every extreme that they name: `pulse_order`: each row is a permutation of the 24 aperture positions.
All inputs are finite; a program needn't handle non-finite values.
Results may differ from a plain program's by a relative error of at most 0.0085.
Values may be sent and summed in bfloat16 or wider, within the bound.
No kernel may reach another device: no remote copies, remote signals or barrier semaphores. Data moves between devices by JAX's collectives and lax.ppermute only.
A program may use at most 64 MiB of HBM per device.

v0:
```python
import functools

import jax
import jax.numpy as jnp
from jax import lax
from jax.experimental import pallas as pl
from jax.experimental.pallas import tpu as pltpu
from jax.sharding import PartitionSpec as P

LANE = 128
SUBL = 8
F32 = jnp.float32
BF16 = jnp.bfloat16


def ceil_to(value, unit):
    return -(-value // unit) * unit


def pack_kernel(coef_ref, start_ref, width_ref, steer_ref, order_ref, pack_ref, starts, *, sections, group):
    levels, _, sides, parts, taps, beams = coef_ref.shape
    tap = lax.broadcasted_iota(jnp.int32, (taps, beams), 0)
    row = 0
    for level in range(levels):
        for side in range(sides):
            used = tap < width_ref[level, 0, side : side + 1, :]
            for part in range(parts):
                entries = coef_ref[level, 0, side, part].astype(F32)
                pack_ref[row : row + taps] = jnp.where(used, entries, 0.0).astype(BF16)
                row += taps
    pulses = order_ref.shape[1]
    each = pulses // sections
    position = lax.broadcasted_iota(jnp.int32, (pulses, pulses), 0)
    hit = (position == order_ref[0:1, :]).astype(F32)
    slot = lax.broadcasted_iota(jnp.int32, (sections * group, pulses), 0)
    pulse = lax.broadcasted_iota(jnp.int32, (sections * group, pulses), 1)
    place = jnp.zeros((sections * group, pulses), F32)
    for s in range(sections):
        inside = (pulse >= s * each) & (pulse < (s + 1) * each)
        place = jnp.where(inside & (slot - s * group == pulse - s * each), 1.0, place)
    pick = lax.dot_general(
        place.astype(BF16), hit.astype(BF16), (((1,), (1,)), ((), ())), preferred_element_type=F32
    )
    for part in range(parts):
        chosen = jnp.dot(pick.astype(BF16), steer_ref[part, 0], preferred_element_type=F32)
        pack_ref[row : row + sections * group] = chosen.astype(BF16)
        row += sections * group
    starts[...] = jnp.zeros_like(starts)
    for level in range(levels):
        starts[sides * level : sides * level + sides] = start_ref[level, 0].astype(F32)
    pack_ref[row : row + starts.shape[0]] = starts[...].astype(BF16)


def pack_rows(levels, sides, parts, taps, sections, group):
    return levels * sides * parts * taps + parts * sections * group + ceil_to(levels * sides, 16)


def pack_parameters(coef, start, width, steer, order, sections, group):
    levels, _, sides, parts, taps, beams = coef.shape
    return pl.pallas_call(
        functools.partial(pack_kernel, sections=sections, group=group),
        out_shape=jax.ShapeDtypeStruct((pack_rows(levels, sides, parts, taps, sections, group), beams), BF16),
        scratch_shapes=[pltpu.VMEM((ceil_to(levels * sides, 16), beams), F32)],
        name="pack_parameters",
    )(coef, start, width, steer, order)


def pack_rows_of(real, imag, each):
    group = real.shape[0]
    row = lax.broadcasted_iota(jnp.int32, real.shape, 0)
    return jnp.where(row < each, real, pltpu.roll(imag, each, 0)), group - each


def split_two(value):
    high = value.astype(BF16)
    return high, (value - high.astype(F32)).astype(BF16)


def operator_kernel(index_ref, own_ref, partner_ref, out_ref, weights, *, dims, sections, group, each):
    levels, sides, parts, taps, beams = dims
    width = sections * group
    refs = (own_ref, partner_ref)
    weight_row = levels * sides * parts * taps
    start_row = weight_row + parts * width

    def band(ref, level, side):
        first = ((level * sides + side) * parts) * taps
        tables = [ref[first + p * taps : first + (p + 1) * taps].astype(F32) for p in range(parts)]
        start = ref[start_row : start_row + ceil_to(levels * sides, 16)].astype(F32)
        start = start[level * sides + side : level * sides + side + 1].astype(jnp.int32)
        found = [[], []]
        for c in range(0, beams, SUBL):
            column = lax.broadcasted_iota(jnp.int32, (SUBL, beams), 0) + c
            offset = column - start
            spot = offset & (SUBL - 1)
            for p in range(parts):
                value = jnp.zeros((SUBL, beams), F32)
                for t in range(0, taps, SUBL):
                    got = jnp.take_along_axis(
                        tables[p][t : t + SUBL], spot, axis=0, mode="promise_in_bounds"
                    )
                    value = jnp.where((offset >= t) & (offset < t + SUBL), got, value)
                found[p].append(value)
        return [jnp.concatenate(f, axis=0) for f in found]

    def complex_operand(real, imag):
        top = jnp.concatenate([real, imag], axis=1)
        low = jnp.concatenate([-imag, real], axis=1)
        return jnp.concatenate([top, low], axis=0).astype(BF16)

    section = index_ref[0]
    images = []
    for a in range(2):
        for p in range(parts):
            weights[...] = refs[a][weight_row + p * width : weight_row + (p + 1) * width].astype(F32)
            rows = []
            for j in range(sections):
                at = pl.multiple_of((section ^ j) * group, group)
                rows.append(weights[pl.ds(at, group)])
            images.append(jnp.concatenate(rows, axis=0))
    zero = jnp.zeros((width, 2 * beams), F32)
    own = jnp.concatenate([jnp.concatenate(images[0:2], axis=1), zero], axis=0)
    partner = jnp.concatenate([zero, jnp.concatenate(images[2:4], axis=1)], axis=0)
    for level in range(levels):
        own_high, own_low = split_two(own)
        partner_high, partner_low = split_two(partner)
        own_rows = jnp.concatenate([own_high, own_low], axis=0)
        partner_rows = jnp.concatenate([partner_high, partner_low], axis=0)

        def merged(ref, mine, other):
            product = jnp.dot(
                mine, complex_operand(*band(ref, level, 0)), preferred_element_type=F32
            ) + jnp.dot(other, complex_operand(*band(ref, level, 1)), preferred_element_type=F32)
            return product[: 2 * width] + product[2 * width :]

        following = merged(own_ref, own_rows, partner_rows)
        if level < levels - 1:
            partner = merged(partner_ref, partner_rows, own_rows)
        own = following
    full, left, right = [], [], []
    for j in range(2 * sections):
        real = own[j * group : (j + 1) * group, :beams]
        imag = own[j * group : (j + 1) * group, beams:]
        straight = jnp.concatenate([real, imag], axis=1)
        turned = jnp.concatenate([-imag, real], axis=1)
        lead, moved = pack_rows_of(straight, turned, each)
        row = lax.broadcasted_iota(jnp.int32, lead.shape, 0)
        full.append(lead)
        left.append(jnp.where(row < group // 2, pltpu.roll(turned, group - moved, 0), 0.0))
        right.append(jnp.where(row >= group // 2, pltpu.roll(turned, group // 2 - moved, 0), 0.0))
    pairs = sections // 2
    first_core = section % 2 == 0
    for half, rest in enumerate((left, right)):
        sources = [jnp.concatenate([full[j], rest[j]], axis=0) for j in range(2 * sections)]
        quarters = [jnp.concatenate(sources[q * pairs : (q + 1) * pairs], axis=0) for q in range(4)]
        quarters[1:3] = [
            jnp.where(first_core, quarters[1], quarters[2]),
            jnp.where(first_core, quarters[2], quarters[1]),
        ]
        high, low = split_two(jnp.concatenate(quarters, axis=0).T)
        out_ref[half] = jnp.concatenate([high, low], axis=1)


def fold_operator(section, own, partner, dims, sections, group, each):
    beams = dims[-1]
    width = sections * group
    return pl.pallas_call(
        functools.partial(operator_kernel, dims=dims, sections=sections, group=group, each=each),
        out_shape=jax.ShapeDtypeStruct((2, 2 * beams, 8 * width), BF16),
        in_specs=[
            pl.BlockSpec(memory_space=pltpu.SMEM),
            pl.BlockSpec(memory_space=pltpu.VMEM),
            pl.BlockSpec(memory_space=pltpu.VMEM),
        ],
        scratch_shapes=[pltpu.VMEM((width, beams), F32)],
        compiler_params=pltpu.CompilerParams(vmem_limit_bytes=16 * 1024 * 1024),
        name="fold_operator",
    )(section, own, partner)


def compress_kernel(
    index_ref, echo_ref, halo_ref, chirp_ref, keep_ref, give_ref, rows, even, odd, table, *, sections, group
):
    pulses, _, length = echo_ref.shape
    taps = chirp_ref.shape[1]
    blocks, extra = length // LANE, taps // LANE
    total = blocks + extra
    reverse = LANE - 1 - lax.broadcasted_iota(jnp.int32, (2, LANE), 1)
    below = lax.broadcasted_iota(jnp.int32, (LANE, LANE), 1) <= lax.broadcasted_iota(
        jnp.int32, (LANE, LANE), 0
    )
    before = [jnp.zeros((LANE, LANE), F32)] * 2
    for lag in range(extra + 1):
        if lag < extra:
            piece = chirp_ref[:, lag * LANE : (lag + 1) * LANE].astype(F32)
            piece = jnp.take_along_axis(piece, reverse, axis=1, mode="promise_in_bounds")
            turned = [
                pltpu.roll(
                    jnp.broadcast_to(piece[c : c + 1], (LANE, LANE)), 1, 1, stride=1, stride_axis=0
                )
                for c in range(2)
            ]
        else:
            turned = [jnp.zeros((LANE, LANE), F32)] * 2
        real, imag = [jnp.where(below, turned[c], before[c]) for c in range(2)]
        before = turned
        at = lag * 2 * LANE
        table[at : at + LANE, :LANE] = real.astype(BF16)
        table[at : at + LANE, LANE:] = (-imag).astype(BF16)
        table[at + LANE : at + 2 * LANE, :LANE] = imag.astype(BF16)
        table[at + LANE : at + 2 * LANE, LANE:] = real.astype(BF16)
    rows[...] = jnp.zeros_like(rows)
    for p in range(pulses):
        near = echo_ref[p].astype(F32)
        far = halo_ref[p, :, :taps].astype(F32)
        for c in range(2):
            rows[c * group + p : c * group + p + 1, :length] = near[c : c + 1]
            rows[c * group + p : c * group + p + 1, length:] = far[c : c + 1]
    held = [
        jnp.concatenate(
            [rows[:group, b * LANE : (b + 1) * LANE], rows[group:, b * LANE : (b + 1) * LANE]], axis=1
        )
        for b in range(total)
    ]
    for b in range(0, total, 2):
        even[b * group : (b + 2) * group] = jnp.concatenate(held[b : b + 2], axis=0).astype(BF16)
    for b in range(1, total - 1, 2):
        odd[(b - 1) * group : (b + 1) * group] = jnp.concatenate(held[b : b + 2], axis=0).astype(BF16)
    window = blocks * group
    pieces = []
    for lag in range(extra + 1):
        source, at = (even, lag) if lag % 2 == 0 else (odd, lag - 1)
        pieces.append(source[at * group : at * group + window])
    done = jnp.dot(jnp.concatenate(pieces, axis=1), table[...], preferred_element_type=F32)
    section = index_ref[0]
    chunk = blocks // sections
    for s in range(sections):
        real, imag = [
            jnp.concatenate(
                [
                    done[(s * chunk + b) * group : (s * chunk + b + 1) * group, c * LANE : (c + 1) * LANE]
                    for b in range(chunk)
                ],
                axis=1,
            )
            for c in range(2)
        ]
        middle = chunk * LANE // 2
        lead, moved = pack_rows_of(real, imag, pulses)
        row = lax.broadcasted_iota(jnp.int32, (group, middle), 0)
        rest = jnp.where(
            row < group // 2,
            pltpu.roll(imag[:, :middle], group - moved, 0),
            pltpu.roll(imag[:, middle:], group // 2 - moved, 0),
        )
        stacked = jnp.concatenate([lead[:, :middle], lead[:, middle:], rest], axis=0).astype(BF16)
        slot = section ^ s
        far, other_core = slot // 2, slot % 2
        place = far ^ 1 ^ (section % 2) ^ other_core

        @pl.when(other_core == 0)
        def _():
            keep_ref[place] = stacked

        @pl.when(other_core == 1)
        def _():
            give_ref[place] = stacked


def compress_pulses(section, echo, halo, chirp, sections, group):
    pulses, _, length = echo.shape
    taps = chirp.shape[1]
    blocks, extra = length // LANE, taps // LANE
    total = blocks + extra
    return pl.pallas_call(
        functools.partial(compress_kernel, sections=sections, group=group),
        out_shape=[jax.ShapeDtypeStruct((2, 3 * group, length // sections // 2), BF16)] * 2,
        in_specs=[pl.BlockSpec(memory_space=pltpu.SMEM)] + [pl.BlockSpec(memory_space=pltpu.VMEM)] * 3,
        scratch_shapes=[
            pltpu.VMEM((2 * group, total * LANE), F32),
            pltpu.VMEM((total * group, 2 * LANE), BF16),
            pltpu.VMEM((total * group, 2 * LANE), BF16),
            pltpu.VMEM(((extra + 1) * 2 * LANE, 2 * LANE), BF16),
        ],
        compiler_params=pltpu.CompilerParams(vmem_limit_bytes=24 * 1024 * 1024),
        name="compress_pulses",
    )(section, echo, halo, chirp)


def image_kernel(index_ref, operator_ref, both_ref, *refs, group):
    chunks, (out_ref, parts, sems) = refs[:-3], refs[-3:]
    count, _, tile = parts.shape
    width = both_ref.shape[2]
    near = 1 - index_ref[0] % 2
    held = [both_ref[near]] + [chunk[...] for chunk in chunks]
    held = [value.astype(F32) for value in held]
    copies = []
    for i in range(count):
        half, at = divmod(i * tile, width)
        rows = []
        for value in held:
            for first in range(0, value.shape[0], 3 * group):
                rows.append(value[first + half * group : first + (half + 1) * group, at : at + tile])
                rows.append(value[first + 2 * group : first + 3 * group, at : at + tile])
        pulses = jnp.concatenate(rows, axis=0).astype(BF16)
        result = jnp.dot(
            operator_ref[half], jnp.concatenate([pulses, pulses], axis=0), preferred_element_type=F32
        )
        parts[i] = result.astype(BF16)
        copy = pltpu.make_async_copy(parts.at[i], out_ref.at[:, i * tile : (i + 1) * tile], sems.at[i])
        copy.start()
        copies.append(copy)
    for copy in copies:
        copy.wait()


def form_image(section, operator, both, chunks, group):
    height, half = operator.shape[1], both.shape[2]
    tile = 256 if half % 256 == 0 else half
    count = 2 * half // tile
    return pl.pallas_call(
        functools.partial(image_kernel, group=group),
        out_shape=jax.ShapeDtypeStruct((height, 2 * half), BF16),
        in_specs=[pl.BlockSpec(memory_space=pltpu.SMEM)]
        + [pl.BlockSpec(memory_space=pltpu.VMEM)] * (2 + len(chunks)),
        out_specs=pl.BlockSpec(memory_space=pl.ANY),
        scratch_shapes=[
            pltpu.VMEM((count, height, tile), BF16),
            pltpu.SemaphoreType.DMA((count,)),
        ],
        compiler_params=pltpu.CompilerParams(vmem_limit_bytes=16 * 1024 * 1024),
        name="form_image",
    )(section, operator, both, *chunks)


def swap(value, axis, by):
    count = lax.axis_size(axis)
    return lax.ppermute(value, axis, [(i, i ^ by) for i in range(count)])


def swap_by(value, move):
    sections, subs = lax.axis_size("section"), lax.axis_size("sub")
    pairs = []
    for s in range(sections):
        for a in range(subs):
            to_s, to_a = move(s, a)
            pairs.append((s * subs + a, to_s * subs + to_a))
    return lax.ppermute(value, ("section", "sub"), pairs)


def from_behind(value, axis, by):
    size = lax.axis_size(axis)
    pairs = [(i, i + by) for i in range(size) if 0 <= i + by < size]
    return lax.ppermute(value, axis, pairs)


def on_device(echoes, chirp, steer, pulse_order, band_coef, band_start, band_width):
    sections, subs = lax.axis_size("section"), lax.axis_size("sub")
    pulses_each = echoes.shape[2]
    group = ceil_to(pulses_each, SUBL)
    section = lax.axis_index("section").astype(jnp.int32).reshape(1)
    coef = jnp.swapaxes(band_coef, 4, 5)
    weights = jnp.swapaxes(steer, 2, 3)
    levels, _, sides, parts, taps, beams = coef.shape
    dims = (levels, sides, parts, taps, beams)

    echo = jnp.transpose(echoes[:, 0], (1, 0, 2))
    halo = from_behind(echo, "rng", -1)
    packed = pack_parameters(coef, band_start, band_width, weights, pulse_order, sections, group)
    if subs == 2:
        packed_partner = swap(packed, "sub", 1)
    keep, give = compress_pulses(section, echo, halo, chirp, sections, group)
    both = jnp.concatenate([keep, swap(give, "section", 1)], axis=1)
    far = lax.dynamic_index_in_dim(both, section[0] % 2, 0, keepdims=False)
    if subs != 2:
        near = lax.dynamic_index_in_dim(both, 1 - section[0] % 2, 0, keepdims=False)
        chunks = [near, swap(far, "section", 2)]
        return merge_images(section, chunks, packed, dims, sections, group, pulses_each)
    chunks = [
        swap_by(both[0], lambda s, a: (s, a ^ 1) if s % 2 else (s ^ 2, a)),
        swap_by(both[1], lambda s, a: (s ^ 2, a) if s % 2 else (s, a ^ 1)),
        swap_by(far, lambda s, a: (s ^ 2, a ^ 1)),
    ]
    operator = fold_operator(section, packed, packed_partner, dims, sections, group, pulses_each)
    image = form_image(section, operator, both, chunks, group)
    return image.reshape(2, beams, 1, image.shape[1])


def unpack(chunk, group, each):
    lead = jnp.concatenate([chunk[:group], chunk[group : 2 * group]], axis=1)
    moved, rest = group - each, chunk[2 * group :]
    tail = jnp.concatenate([rest[: each - moved], rest[group // 2 : group // 2 + each - moved]], axis=1)
    return jnp.concatenate([lead, tail], axis=0)


def merge_images(section, chunks, packed, dims, sections, group, each):
    levels, sides, parts, taps, beams = dims
    width = sections * group
    first = levels * sides * parts * taps
    table = packed[first : first + parts * width].reshape(parts, sections, group, beams)
    table = jnp.take(table, section[0] ^ jnp.arange(sections), axis=1)[:, :, :each]
    chunks = [
        unpack(chunk[first : first + 3 * group], group, each)
        for chunk in chunks
        for first in range(0, chunk.shape[0], 3 * group)
    ]
    real, imag = table[0], table[1]
    rows = jnp.concatenate(
        [jnp.concatenate([real, -imag], axis=1), jnp.concatenate([imag, real], axis=1)], axis=2
    )
    image = lax.dot_general(
        rows.reshape(-1, 2 * beams), jnp.concatenate(chunks, axis=0), (((0,), (0,)), ((), ())), preferred_element_type=F32
    ).astype(BF16)
    starts = packed[first + parts * width :].astype(jnp.int32)
    column = jnp.arange(beams, dtype=jnp.int32)
    bits = lax.axis_size("sub").bit_length() - 1
    for level in range(levels):
        partner = swap(image, "sub", 1 << (level % bits))
        operands = []
        for side in range(sides):
            at = (level * sides + side) * parts * taps
            coef = packed[at : at + parts * taps].reshape(parts, taps, beams)
            offset = column[:, None] - starts[level * sides + side][None, :]
            hits = (offset[None] == jnp.arange(taps, dtype=jnp.int32)[:, None, None]).astype(BF16)
            operands.append(jnp.einsum("ptq,tcq->pqc", coef, hits, preferred_element_type=F32).astype(BF16))
        top = jnp.concatenate([operands[0][0], -operands[0][1], operands[1][0], -operands[1][1]], axis=1)
        low = jnp.concatenate([operands[0][1], operands[0][0], operands[1][1], operands[1][0]], axis=1)
        image = jnp.dot(
            jnp.concatenate([top, low], axis=0),
            jnp.concatenate([image, partner], axis=0),
            preferred_element_type=F32,
        ).astype(BF16)
    return image.reshape(2, beams, 1, image.shape[1])


def solution(mesh):
    return jax.shard_map(
        on_device,
        mesh=mesh,
        in_specs=(
            P(None, "sub", "section", "rng"),
            P(),
            P(None, "sub", None, None),
            P("sub", None),
            P(None, "sub", None, None, None, None),
            P(None, "sub", None, None),
            P(None, "sub", None, None),
        ),
        out_specs=P(None, "sub", "rng", "section"),
        check_vma=False,
    )
```

profile of v0, /device:TPU:0, one launch (start us, length us, event | category | flops | bytes accessed | tf_op | source)
XLA Modules:
  0.0 19.1 jit_solution(14748397070982971644)
XLA Ops:
  0.0 1.3 %collective-permute-start.1 = (bf16[6,2,4096]{2,1,0:T(2,128)(2,1)}, bf16[6,2,4096]{2,1,0:T(2,128)(2,1)S(1)}, u32[]{:S(2)}, u32[]{:S(2)}) collective-permute-start(bf16[6,2,4096]{2,1,0:T(2,128)(2,1)} %bitcast.15), channel_id=1, source_target_pairs={{1,0},{2,1},{3,2},{5,4},{6,5},{7,6},{9,8},{10,9},{11,10},{13,12},{... | collective-permute-start | bytes 294920 | tf_op jit(solution)/shard_map/ppermute | solution.py:354
  1.3 0.0 copy-start.1
  1.3 1.9 %pack_parameters.1.own_ref = bf16[400,128]{1,0:T(8,128)(2,1)} custom-call(bf16[5,1,2,2,16,128]{5,4,3,2,1,0:T(8,128)(2,1)} %bitcast.17, s32[5,1,2,128]{3,2,1,0:T(2,128)} %start_ref.1, s32[5,1,2,128]{3,2,1,0:T(2,128)} %width_ref.1, bf16[2,1,24,128]{3,2,1,0:T(8,128)(2,1)} %bitcast.18, s32[1,24]{1,0:T(1,128)} %order_ref.1), custom_call_target="tpu_custom_call" | custom-call | tf_op jit(solution)/shard_map/pack_parameters/pallas_call | solution.py:60
  3.2 3.0 %collective-permute-start = (bf16[400,128]{1,0:T(8,128)(2,1)}, bf16[400,128]{1,0:T(8,128)(2,1)S(1)}, u32[]{:S(2)}, u32[]{:S(2)}) collective-permute-start(bf16[400,128]{1,0:T(8,128)(2,1)} %pack_parameters.1.own_ref), channel_id=1, source_target_pairs={{0,4},{4,0},{1,5},{5,1},{2,6},{6,2},{3,7},{7,3},{8,12},{12,8},{9,1... | collective-permute-start | bytes 307208 | tf_op jit(solution)/shard_map/ppermute | solution.py:338
  6.1 0.0 copy-start.2
  6.1 1.8 %collective-permute-done.1.halo_ref = bf16[6,2,4096]{2,1,0:T(2,128)(2,1)S(1)} collective-permute-done((bf16[6,2,4096]{2,1,0:T(2,128)(2,1)}, bf16[6,2,4096]{2,1,0:T(2,128)(2,1)S(1)}, u32[]{:S(2)}, u32[]{:S(2)}) %collective-permute-start.1) | collective-permute-done | bytes 98336 | tf_op jit(solution)/shard_map/ppermute | solution.py:354
  7.9 0.0 copy-done.1
  7.9 0.0 copy-done.2
  7.9 1.4 %compress_pulses.1 = (bf16[2,24,512]{2,1,0:T(8,128)(2,1)S(1)}, bf16[2,24,512]{2,1,0:T(8,128)(2,1)S(1)}) custom-call(s32[1]{0:T(128)} %bitcast.index_ref, bf16[6,2,4096]{2,1,0:T(2,128)(2,1)S(1)} %bitcast.16, bf16[6,2,4096]{2,1,0:T(2,128)(2,1)S(1)} %collective-permute-done.1.halo_ref, bf16[2,2048]{1,0:T(2,128)(2,1)S(1)} %copy-done.2), custom_call_target="tpu_custom_call" | custom-call | tf_op jit(solution)/shard_map/compress_pulses/pallas_call | solution.py:275
  9.4 0.1 collective-permute-start.2
  9.5 1.2 %collective-permute-done.2 = bf16[2,24,512]{2,1,0:T(8,128)(2,1)S(1)} collective-permute-done((bf16[2,24,512]{2,1,0:T(8,128)(2,1)S(1)}, bf16[2,24,512]{2,1,0:T(8,128)(2,1)S(1)}, u32[]{:S(2)}, u32[]{:S(2)}) %collective-permute-start.2) | collective-permute-done | bytes 49184 | tf_op jit(solution)/shard_map/ppermute | solution.py:338
  10.7 0.0 copy-start
  10.7 2.8 %collective-permute-start.5 = (bf16[48,512]{1,0:T(8,128)(2,1)S(1)}, bf16[48,512]{1,0:T(8,128)(2,1)S(1)}, u32[]{:S(2)}, u32[]{:S(2)}) collective-permute-start(bf16[48,512]{1,0:T(8,128)(2,1)S(1)} %get-tuple-element.9), channel_id=1, source_target_pairs={{0,20},{4,16},{8,28},{12,24},{16,4},{20,0},{24,12},{28,8},{1,21},{... | collective-permute-start | bytes 147464 | tf_op jit(solution)/shard_map/ppermute | solution.py:348
  13.4 0.5 %collective-permute-start.4 = (bf16[48,512]{1,0:T(8,128)(2,1)S(1)}, bf16[48,512]{1,0:T(8,128)(2,1)S(1)}, u32[]{:S(2)}, u32[]{:S(2)}) collective-permute-start(bf16[48,512]{1,0:T(8,128)(2,1)S(1)} %get-tuple-element.10), channel_id=1, source_target_pairs={{0,4},{4,0},{8,24},{12,28},{16,20},{20,16},{24,8},{28,12},{1,5},{5... | collective-permute-start | bytes 147464 | tf_op jit(solution)/shard_map/ppermute | solution.py:348
  14.0 0.3 %collective-permute-start.3 = (bf16[48,512]{1,0:T(8,128)(2,1)S(1)}, bf16[48,512]{1,0:T(8,128)(2,1)S(1)}, u32[]{:S(2)}, u32[]{:S(2)}) collective-permute-start(bf16[48,512]{1,0:T(8,128)(2,1)S(1)} %get-tuple-element.11), channel_id=1, source_target_pairs={{0,16},{4,20},{8,12},{12,8},{16,0},{20,4},{24,28},{28,24},{1,17},{... | collective-permute-start | bytes 147464 | tf_op jit(solution)/shard_map/ppermute | solution.py:348
  14.2 0.0 collective-permute-done.partner_ref
  14.3 0.0 copy-done
  14.3 1.3 %fold_operator.1.operator_ref = bf16[2,256,256]{2,1,0:T(8,128)(2,1)S(1)} custom-call(s32[1]{0:T(128)} %bitcast.index_ref, bf16[400,128]{1,0:T(8,128)(2,1)S(1)} %copy-done, bf16[400,128]{1,0:T(8,128)(2,1)S(1)} %collective-permute-done.partner_ref), custom_call_target="tpu_custom_call" | custom-call | tf_op jit(solution)/shard_map/fold_operator/pallas_call | solution.py:167
  15.6 0.2 collective-permute-done.5.refs_2_
  15.7 1.8 %collective-permute-done.4.refs_1_ = bf16[48,512]{1,0:T(8,128)(2,1)S(1)} collective-permute-done((bf16[48,512]{1,0:T(8,128)(2,1)S(1)}, bf16[48,512]{1,0:T(8,128)(2,1)S(1)}, u32[]{:S(2)}, u32[]{:S(2)}) %collective-permute-start.4) | collective-permute-done | bytes 49184 | tf_op jit(solution)/shard_map/ppermute | solution.py:348
  17.5 0.5 %collective-permute-done.3.refs_0_ = bf16[48,512]{1,0:T(8,128)(2,1)S(1)} collective-permute-done((bf16[48,512]{1,0:T(8,128)(2,1)S(1)}, bf16[48,512]{1,0:T(8,128)(2,1)S(1)}, u32[]{:S(2)}, u32[]{:S(2)}) %collective-permute-start.3) | collective-permute-done | bytes 49184 | tf_op jit(solution)/shard_map/ppermute | solution.py:348
  18.0 1.1 %form_image.1 = bf16[256,1024]{1,0:T(8,128)(2,1)} custom-call(s32[1]{0:T(128)} %bitcast.index_ref, bf16[2,256,256]{2,1,0:T(8,128)(2,1)S(1)} %fold_operator.1.operator_ref, bf16[2,48,512]{2,1,0:T(8,128)(2,1)S(1)} %constant_dynamic-update-slice_fusion.both_ref, bf16[48,512]{1,0:T(8,128)(2,1)S(1)} %collective-permute-done.3.refs_0_, ...), custom_call_target="tpu_custom_call" | custom-call | tf_op jit(solution)/shard_map/form_image/pallas_call | solution.py:321
  (3 shorter events, 0.0 us)
Async XLA Ops:
  0.0 7.9 %collective-permute-start.1 = (bf16[6,2,4096]{2,1,0:T(2,128)(2,1)}, bf16[6,2,4096]{2,1,0:T(2,128)(2,1)S(1)}, u32[]{:S(2)}, u32[]{:S(2)}) collective-permute-start(bf16[6,2,4096]{2,1,0:T(2,128)(2,1)} %bitcast.15), channel_id=1, source_target_pairs={{1,0},{2,1},{3,2},{5,4},{6,5},{7,6},{9,8},{10,9},{11,10},{13,12},{... | collective-permute-start | bytes 294920 | tf_op jit(solution)/shard_map/ppermute | solution.py:354
  1.3 6.6 %copy-start.1 = (bf16[2,1,6,4096]{3,0,2,1:T(2,128)(2,1)S(1)}, bf16[2,1,6,4096]{3,0,2,1:T(2,128)(2,1)}, u32[]{:S(2)}) copy-start(bf16[2,1,6,4096]{3,0,2,1:T(2,128)(2,1)} %param.7) | copy-start | bytes 294916
  3.2 11.1 %collective-permute-start = (bf16[400,128]{1,0:T(8,128)(2,1)}, bf16[400,128]{1,0:T(8,128)(2,1)S(1)}, u32[]{:S(2)}, u32[]{:S(2)}) collective-permute-start(bf16[400,128]{1,0:T(8,128)(2,1)} %pack_parameters.1.own_ref), channel_id=1, source_target_pairs={{0,4},{4,0},{1,5},{5,1},{2,6},{6,2},{3,7},{7,3},{8,12},{12,8},{9,1... | collective-permute-start | bytes 307208 | tf_op jit(solution)/shard_map/ppermute | solution.py:338
  6.1 1.8 %copy-start.2 = (bf16[2,2048]{1,0:T(2,128)(2,1)S(1)}, bf16[2,2048]{1,0:T(2,128)(2,1)}, u32[]{:S(2)}) copy-start(bf16[2,2048]{1,0:T(2,128)(2,1)} %chirp_ref.1) | copy-start | bytes 24580
  9.4 1.3 %collective-permute-start.2 = (bf16[2,24,512]{2,1,0:T(8,128)(2,1)S(1)}, bf16[2,24,512]{2,1,0:T(8,128)(2,1)S(1)}, u32[]{:S(2)}, u32[]{:S(2)}) collective-permute-start(bf16[2,24,512]{2,1,0:T(8,128)(2,1)S(1)} %get-tuple-element.8), channel_id=1, source_target_pairs={{0,8},{8,0},{16,24},{24,16},{1,9},{9,1},{17,25},{25,17},{2,10},{10... | collective-permute-start | bytes 147464 | tf_op jit(solution)/shard_map/ppermute | solution.py:338
  10.7 3.6 %copy-start = (bf16[400,128]{1,0:T(8,128)(2,1)S(1)}, bf16[400,128]{1,0:T(8,128)(2,1)}, u32[]{:S(2)}) copy-start(bf16[400,128]{1,0:T(8,128)(2,1)} %pack_parameters.1.own_ref) | copy-start | bytes 307204
  10.7 5.1 %collective-permute-start.5 = (bf16[48,512]{1,0:T(8,128)(2,1)S(1)}, bf16[48,512]{1,0:T(8,128)(2,1)S(1)}, u32[]{:S(2)}, u32[]{:S(2)}) collective-permute-start(bf16[48,512]{1,0:T(8,128)(2,1)S(1)} %get-tuple-element.9), channel_id=1, source_target_pairs={{0,20},{4,16},{8,28},{12,24},{16,4},{20,0},{24,12},{28,8},{1,21},{... | collective-permute-start | bytes 147464 | tf_op jit(solution)/shard_map/ppermute | solution.py:348
  13.4 4.1 %collective-permute-start.4 = (bf16[48,512]{1,0:T(8,128)(2,1)S(1)}, bf16[48,512]{1,0:T(8,128)(2,1)S(1)}, u32[]{:S(2)}, u32[]{:S(2)}) collective-permute-start(bf16[48,512]{1,0:T(8,128)(2,1)S(1)} %get-tuple-element.10), channel_id=1, source_target_pairs={{0,4},{4,0},{8,24},{12,28},{16,20},{20,16},{24,8},{28,12},{1,5},{5... | collective-permute-start | bytes 147464 | tf_op jit(solution)/shard_map/ppermute | solution.py:348
  14.0 4.1 %collective-permute-start.3 = (bf16[48,512]{1,0:T(8,128)(2,1)S(1)}, bf16[48,512]{1,0:T(8,128)(2,1)S(1)}, u32[]{:S(2)}, u32[]{:S(2)}) collective-permute-start(bf16[48,512]{1,0:T(8,128)(2,1)S(1)} %get-tuple-element.11), channel_id=1, source_target_pairs={{0,16},{4,20},{8,12},{12,8},{16,0},{20,4},{24,28},{28,24},{1,17},{... | collective-permute-start | bytes 147464 | tf_op jit(solution)/shard_map/ppermute | solution.py:348
where the time goes:
time: 19.3 us; the launch traced here: 19.1 us
  starting transfers between devices  7.87 us (41%)
  Pallas kernels  5.68 us (29%)
  waiting for transfers between devices  5.46 us (28%)
    ppermute x3, starting transfers between devices, swap_by(): return lax.ppermute(value, ('section', 'sub'), pairs)  3.55 us
    ppermute x2, starting transfers between devices, swap(): return lax.ppermute(value, axis, [(i, i ^ by) for i in range(count)])  3.04 us
    ppermute x3, waiting for transfers between devices, swap_by(): return lax.ppermute(value, ('section', 'sub'), pairs)  2.46 us
    pallas_call x1, Pallas kernels, pack_parameters(): pl.pallas_call(functools.partial(pack_kernel, sections=sections, group=gr...  1.85 us
    ppermute x1, waiting for transfers between devices, from_behind(): return lax.ppermute(value, axis, pairs)  1.79 us
    pallas_call x1, Pallas kernels, compress_pulses(): pl.pallas_call(functools.partial(compress_kernel, sections=sections, grou...  1.44 us
    pallas_call x1, Pallas kernels, fold_operator(): pl.pallas_call(functools.partial(operator_kernel, dims=dims, sections=sec...  1.32 us
    ppermute x1, starting transfers between devices, from_behind(): return lax.ppermute(value, axis, pairs)  1.28 us
  transfers between devices with their start and end apart: 6, of which 5 were waited for; matrix products, arithmetic and copies ran while one was open for 0% of the time, Pallas kernels for 24%

commit v1 on v0

--- a/solution.py
+++ b/solution.py
@@ -178,13 +178,52 @@
     )(section, own, partner)
 
 
-def compress_kernel(
-    index_ref, echo_ref, halo_ref, chirp_ref, keep_ref, give_ref, rows, even, odd, table, *, sections, group
-):
+def correlate(rows, even, odd, table, blocks, group):
+    extra = table.shape[0] // (2 * LANE) - 1
+    total = blocks + extra
+    held = [
+        jnp.concatenate(
+            [rows[:group, b * LANE : (b + 1) * LANE], rows[group:, b * LANE : (b + 1) * LANE]], axis=1
+        )
+        for b in range(total)
+    ]
+    for b in range(0, total, 2):
+        even[b * group : (b + 2) * group] = jnp.concatenate(held[b : b + 2], axis=0).astype(BF16)
+    for b in range(1, total - 1, 2):
+        odd[(b - 1) * group : (b + 1) * group] = jnp.concatenate(held[b : b + 2], axis=0).astype(BF16)
+    window = blocks * group
+    pieces = []
+    for lag in range(extra + 1):
+        source, at = (even, lag) if lag % 2 == 0 else (odd, lag - 1)
+        pieces.append(source[at * group : at * group + window])
+    return jnp.dot(jnp.concatenate(pieces, axis=1), table[...], preferred_element_type=F32)
+
+
+def as_chunk(done, s, chunk, group, each):
+    real, imag = [
+        jnp.concatenate(
+            [
+                done[(s * chunk + b) * group : (s * chunk + b + 1) * group, c * LANE : (c + 1) * LANE]
+                for b in range(chunk)
+            ],
+            axis=1,
+        )
+        for c in range(2)
+    ]
+    middle = chunk * LANE // 2
+    lead, moved = pack_rows_of(real, imag, each)
+    row = lax.broadcasted_iota(jnp.int32, (group, middle), 0)
+    rest = jnp.where(
+        row < group // 2,
+        pltpu.roll(imag[:, :middle], group - moved, 0),
+        pltpu.roll(imag[:, middle:], group // 2 - moved, 0),
+    )
+    return jnp.concatenate([lead[:, :middle], lead[:, middle:], rest], axis=0).astype(BF16)
+
+
+def begin_kernel(echo_ref, chirp_ref, early_ref, late_ref, table, rows, even, odd, *, group):
     pulses, _, length = echo_ref.shape
-    taps = chirp_ref.shape[1]
-    blocks, extra = length // LANE, taps // LANE
-    total = blocks + extra
+    extra = chirp_ref.shape[1] // LANE
     reverse = LANE - 1 - lax.broadcasted_iota(jnp.int32, (2, LANE), 1)
     below = lax.broadcasted_iota(jnp.int32, (LANE, LANE), 1) <= lax.broadcasted_iota(
         jnp.int32, (LANE, LANE), 0
@@ -212,51 +251,33 @@
     rows[...] = jnp.zeros_like(rows)
     for p in range(pulses):
         near = echo_ref[p].astype(F32)
+        for c in range(2):
+            rows[c * group + p : c * group + p + 1, :] = near[c : c + 1]
+    late_ref[...] = rows[:, length - late_ref.shape[1] :]
+    done = correlate(rows, even, odd, table, length // LANE - extra, group)
+    for s in range(early_ref.shape[0]):
+        early_ref[s] = as_chunk(done, s, 2 * early_ref.shape[2] // LANE, group, pulses)
+
+
+def finish_kernel(index_ref, early_ref, late_ref, halo_ref, table, keep_ref, give_ref, rows, even, odd, *, group):
+    pulses = halo_ref.shape[0]
+    span = late_ref.shape[1]
+    taps = rows.shape[1] - span
+    rows[:, :span] = late_ref[...]
+    rows[:, span:] = jnp.zeros((2 * group, taps), F32)
+    for p in range(pulses):
         far = halo_ref[p, :, :taps].astype(F32)
         for c in range(2):
-            rows[c * group + p : c * group + p + 1, :length] = near[c : c + 1]
-            rows[c * group + p : c * group + p + 1, length:] = far[c : c + 1]
-    held = [
-        jnp.concatenate(
-            [rows[:group, b * LANE : (b + 1) * LANE], rows[group:, b * LANE : (b + 1) * LANE]], axis=1
-        )
-        for b in range(total)
-    ]
-    for b in range(0, total, 2):
-        even[b * group : (b + 2) * group] = jnp.concatenate(held[b : b + 2], axis=0).astype(BF16)
-    for b in range(1, total - 1, 2):
-        odd[(b - 1) * group : (b + 1) * group] = jnp.concatenate(held[b : b + 2], axis=0).astype(BF16)
-    window = blocks * group
-    pieces = []
-    for lag in range(extra + 1):
-        source, at = (even, lag) if lag % 2 == 0 else (odd, lag - 1)
-        pieces.append(source[at * group : at * group + window])
-    done = jnp.dot(jnp.concatenate(pieces, axis=1), table[...], preferred_element_type=F32)
+            rows[c * group + p : c * group + p + 1, span:] = far[c : c + 1]
+    done = correlate(rows, even, odd, table, span // LANE, group)
+    ready = early_ref.shape[0]
+    chunk = 2 * early_ref.shape[2]
     section = index_ref[0]
-    chunk = blocks // sections
-    for s in range(sections):
-        real, imag = [
-            jnp.concatenate(
-                [
-                    done[(s * chunk + b) * group : (s * chunk + b + 1) * group, c * LANE : (c + 1) * LANE]
-                    for b in range(chunk)
-                ],
-                axis=1,
-            )
-            for c in range(2)
-        ]
-        middle = chunk * LANE // 2
-        lead, moved = pack_rows_of(real, imag, pulses)
-        row = lax.broadcasted_iota(jnp.int32, (group, middle), 0)
-        rest = jnp.where(
-            row < group // 2,
-            pltpu.roll(imag[:, :middle], group - moved, 0),
-            pltpu.roll(imag[:, middle:], group // 2 - moved, 0),
-        )
-        stacked = jnp.concatenate([lead[:, :middle], lead[:, middle:], rest], axis=0).astype(BF16)
+    for s in range(ready + span // chunk):
+        stacked = early_ref[s] if s < ready else as_chunk(done, s - ready, chunk // LANE, group, pulses)
         slot = section ^ s
-        far, other_core = slot // 2, slot % 2
-        place = far ^ 1 ^ (section % 2) ^ other_core
+        far_chunk, other_core = slot // 2, slot % 2
+        place = far_chunk ^ 1 ^ (section % 2) ^ other_core
 
         @pl.when(other_core == 0)
         def _():
@@ -267,24 +288,42 @@
             give_ref[place] = stacked
 
 
-def compress_pulses(section, echo, halo, chirp, sections, group):
-    pulses, _, length = echo.shape
+def row_scratch(blocks, group):
+    return [
+        pltpu.VMEM((2 * group, blocks * LANE), F32),
+        pltpu.VMEM((blocks * group, 2 * LANE), BF16),
+        pltpu.VMEM((blocks * group, 2 * LANE), BF16),
+    ]
+
+
+def begin_compression(echo, chirp, sections, group):
+    _, _, length = echo.shape
     taps = chirp.shape[1]
-    blocks, extra = length // LANE, taps // LANE
-    total = blocks + extra
+    chunk = length // sections
+    early = (length - taps) // chunk
     return pl.pallas_call(
-        functools.partial(compress_kernel, sections=sections, group=group),
-        out_shape=[jax.ShapeDtypeStruct((2, 3 * group, length // sections // 2), BF16)] * 2,
-        in_specs=[pl.BlockSpec(memory_space=pltpu.SMEM)] + [pl.BlockSpec(memory_space=pltpu.VMEM)] * 3,
-        scratch_shapes=[
-            pltpu.VMEM((2 * group, total * LANE), F32),
-            pltpu.VMEM((total * group, 2 * LANE), BF16),
-            pltpu.VMEM((total * group, 2 * LANE), BF16),
-            pltpu.VMEM(((extra + 1) * 2 * LANE, 2 * LANE), BF16),
-        ],
+        functools.partial(begin_kernel, group=group),
+        out_shape=(
+            jax.ShapeDtypeStruct((early, 3 * group, chunk // 2), BF16),
+            jax.ShapeDtypeStruct((2 * group, length - early * chunk), F32),
+            jax.ShapeDtypeStruct(((taps // LANE + 1) * 2 * LANE, 2 * LANE), BF16),
+        ),
+        scratch_shapes=row_scratch(length // LANE, group),
         compiler_params=pltpu.CompilerParams(vmem_limit_bytes=24 * 1024 * 1024),
-        name="compress_pulses",
-    )(section, echo, halo, chirp)
+        name="begin_compression",
+    )(echo, chirp)
+
+
+def finish_compression(section, early, late, halo, table, group):
+    blocks = late.shape[1] // LANE + table.shape[0] // (2 * LANE) - 1
+    return pl.pallas_call(
+        functools.partial(finish_kernel, group=group),
+        out_shape=[jax.ShapeDtypeStruct((2, *early.shape[1:]), BF16)] * 2,
+        in_specs=[pl.BlockSpec(memory_space=pltpu.SMEM)] + [pl.BlockSpec(memory_space=pltpu.VMEM)] * 4,
+        scratch_shapes=row_scratch(blocks, group),
+        compiler_params=pltpu.CompilerParams(vmem_limit_bytes=24 * 1024 * 1024),
+        name="finish_compression",
+    )(section, early, late, halo, table)
 
 
 def image_kernel(index_ref, operator_ref, both_ref, *refs, group):
@@ -369,7 +408,8 @@
     packed = pack_parameters(coef, band_start, band_width, weights, pulse_order, sections, group)
     if subs == 2:
         packed_partner = swap(packed, "sub", 1)
-    keep, give = compress_pulses(section, echo, halo, chirp, sections, group)
+    early, late, table = begin_compression(echo, chirp, sections, group)
+    keep, give = finish_compression(section, early, late, halo, table, group)
     both = jnp.concatenate([keep, swap(give, "section", 1)], axis=1)
     far = lax.dynamic_index_in_dim(both, section[0] % 2, 0, keepdims=False)
     if subs != 2:

time: 19.3 us -> 19.4 us (level)
  waiting for transfers between devices: 5.46 us -> 3.81 us
  local copies, waits for them, and re-layouts: 0.03 us -> 1.61 us
    ppermute x1, waiting for transfers between devices: 1.79 us -> 0.01 us  [from_behind(): return lax.ppermute(value, axis, pairs)]
    unnamed x7, local copies, waits for them, and re-layouts: 0.02 us -> 1.6 us
    pallas_call x1 -> x2, Pallas kernels: 1.44 us -> 1.56 us  [the longest x1 1.04 us: begin_compression(): pl.pallas_call(functools.partial(begin_kernel, group=group), out_shape=(j...]
  transfers between devices with their start and end apart: 6 -> 6, of which waited for: 5 -> 3; matrix products, arithmetic and copies ran while one was open for 0% -> 0% of each run, Pallas kernels for 24% -> 25%
where the time goes in v1:
time: 19.4 us; the launch traced here: 19.1 us
  starting transfers between devices  7.87 us (41%)
  Pallas kernels  5.76 us (30%)
  waiting for transfers between devices  3.81 us (20%)
  local copies, waits for them, and re-layouts  1.61 us (8%)
    ppermute x3, starting transfers between devices, swap_by(): return lax.ppermute(value, ('section', 'sub'), pairs)  3.55 us
    ppermute x2, starting transfers between devices, swap(): return lax.ppermute(value, axis, [(i, i ^ by) for i in range(count)])  3.04 us
    ppermute x3, waiting for transfers between devices, swap_by(): return lax.ppermute(value, ('section', 'sub'), pairs)  2.6 us
    pallas_call x1, Pallas kernels, pack_parameters(): pl.pallas_call(functools.partial(pack_kernel, sections=sections, group=gr...  1.82 us
    unnamed x7, local copies, waits for them, and re-layouts  1.6 us
    pallas_call x1, Pallas kernels, fold_operator(): pl.pallas_call(functools.partial(operator_kernel, dims=dims, sections=sec...  1.32 us
    ppermute x1, starting transfers between devices, from_behind(): return lax.ppermute(value, axis, pairs)  1.28 us
    ppermute x2, waiting for transfers between devices, swap(): return lax.ppermute(value, axis, [(i, i ^ by) for i in range(count)])  1.21 us
  transfers between devices with their start and end apart: 6, of which 3 were waited for; matrix products, arithmetic and copies ran while one was open for 0% of the time, Pallas kernels for 25%

profile of v1, /device:TPU:0, one launch (start us, length us, event | category | flops | bytes accessed | tf_op | source)
XLA Modules:
  0.0 19.1 jit_solution(1580024689231400342)
XLA Ops:
  0.0 1.3 %collective-permute-start.1 = (bf16[6,2,4096]{2,1,0:T(2,128)(2,1)}, bf16[6,2,4096]{2,1,0:T(2,128)(2,1)S(1)}, u32[]{:S(2)}, u32[]{:S(2)}) collective-permute-start(bf16[6,2,4096]{2,1,0:T(2,128)(2,1)} %bitcast.15), channel_id=1, source_target_pairs={{1,0},{2,1},{3,2},{5,4},{6,5},{7,6},{9,8},{10,9},{11,10},{13,12},{... | collective-permute-start | bytes 294920 | tf_op jit(solution)/shard_map/ppermute | solution.py:393
  1.3 1.8 %pack_parameters.1.own_ref = bf16[400,128]{1,0:T(8,128)(2,1)} custom-call(bf16[5,1,2,2,16,128]{5,4,3,2,1,0:T(8,128)(2,1)} %bitcast.17, s32[5,1,2,128]{3,2,1,0:T(2,128)} %start_ref.1, s32[5,1,2,128]{3,2,1,0:T(2,128)} %width_ref.1, bf16[2,1,24,128]{3,2,1,0:T(8,128)(2,1)} %bitcast.18, s32[1,24]{1,0:T(1,128)} %order_ref.1), custom_call_target="tpu_custom_call" | custom-call | tf_op jit(solution)/shard_map/pack_parameters/pallas_call | solution.py:60
  3.1 0.0 copy-start
  3.1 3.0 %collective-permute-start = (bf16[400,128]{1,0:T(8,128)(2,1)}, bf16[400,128]{1,0:T(8,128)(2,1)S(1)}, u32[]{:S(2)}, u32[]{:S(2)}) collective-permute-start(bf16[400,128]{1,0:T(8,128)(2,1)} %pack_parameters.1.own_ref), channel_id=1, source_target_pairs={{0,4},{4,0},{1,5},{5,1},{2,6},{6,2},{3,7},{7,3},{8,12},{12,8},{9,1... | collective-permute-start | bytes 307208 | tf_op jit(solution)/shard_map/ppermute | solution.py:377
  6.1 0.0 copy-start.1
  6.1 0.9 %copy-done.1 = bf16[2,1,6,4096]{3,0,2,1:T(2,128)(2,1)S(1)} copy-done((bf16[2,1,6,4096]{3,0,2,1:T(2,128)(2,1)S(1)}, bf16[2,1,6,4096]{3,0,2,1:T(2,128)(2,1)}, u32[]{:S(2)}) %copy-start.1) | copy-done | bytes 98328
  7.0 0.0 copy-start.2
  7.0 0.7 %copy-done.2 = bf16[2,2048]{1,0:T(2,128)(2,1)S(1)} copy-done((bf16[2,2048]{1,0:T(2,128)(2,1)S(1)}, bf16[2,2048]{1,0:T(2,128)(2,1)}, u32[]{:S(2)}) %copy-start.2) | copy-done | bytes 8216
  7.7 1.0 %begin_compression.1 = (bf16[2,24,512]{2,1,0:T(8,128)(2,1)S(1)}, f32[16,2048]{1,0:T(8,128)S(1)}, bf16[4352,256]{1,0:T(8,128)(2,1)S(1)}) custom-call(bf16[6,2,4096]{2,1,0:T(2,128)(2,1)S(1)} %bitcast.16, bf16[2,2048]{1,0:T(2,128)(2,1)S(1)} %copy-done.2), custom_call_target="tpu_custom_call" | custom-call | tf_op jit(solution)/shard_map/begin_compression/pallas_call | solution.py:304
  8.7 0.0 collective-permute-done.1.halo_ref
  8.7 0.5 %finish_compression.1 = (bf16[2,24,512]{2,1,0:T(8,128)(2,1)S(1)}, bf16[2,24,512]{2,1,0:T(8,128)(2,1)S(1)}) custom-call(s32[1]{0:T(128)} %bitcast.index_ref, bf16[2,24,512]{2,1,0:T(8,128)(2,1)S(1)} %get-tuple-element.10.early_ref, f32[16,2048]{1,0:T(8,128)S(1)} %get-tuple-element.11.late_ref, bf16[6,2,4096]{2,1,0:T(2,128)(2,1)S(1)} %collective-permute-done.1.halo_ref, ...), custom_call_target="tpu_custom_call" | custom-call | tf_op jit(solution)/shard_map/finish_compression/pallas_call | solution.py:319
  9.3 0.1 collective-permute-start.2
  9.4 1.2 %collective-permute-done.2 = bf16[2,24,512]{2,1,0:T(8,128)(2,1)S(1)} collective-permute-done((bf16[2,24,512]{2,1,0:T(8,128)(2,1)S(1)}, bf16[2,24,512]{2,1,0:T(8,128)(2,1)S(1)}, u32[]{:S(2)}, u32[]{:S(2)}) %collective-permute-start.2) | collective-permute-done | bytes 49184 | tf_op jit(solution)/shard_map/ppermute | solution.py:377
  10.6 1.5 %collective-permute-start.3 = (bf16[48,512]{1,0:T(8,128)(2,1)S(1)}, bf16[48,512]{1,0:T(8,128)(2,1)S(1)}, u32[]{:S(2)}, u32[]{:S(2)}) collective-permute-start(bf16[48,512]{1,0:T(8,128)(2,1)S(1)} %get-tuple-element.17), channel_id=1, source_target_pairs={{0,16},{4,20},{8,12},{12,8},{16,0},{20,4},{24,28},{28,24},{1,17},{... | collective-permute-start | bytes 147464 | tf_op jit(solution)/shard_map/ppermute | solution.py:387
  12.1 1.0 %collective-permute-start.4 = (bf16[48,512]{1,0:T(8,128)(2,1)S(1)}, bf16[48,512]{1,0:T(8,128)(2,1)S(1)}, u32[]{:S(2)}, u32[]{:S(2)}) collective-permute-start(bf16[48,512]{1,0:T(8,128)(2,1)S(1)} %get-tuple-element.16), channel_id=1, source_target_pairs={{0,4},{4,0},{8,24},{12,28},{16,20},{20,16},{24,8},{28,12},{1,5},{5... | collective-permute-start | bytes 147464 | tf_op jit(solution)/shard_map/ppermute | solution.py:387
  13.1 1.1 %collective-permute-start.5 = (bf16[48,512]{1,0:T(8,128)(2,1)S(1)}, bf16[48,512]{1,0:T(8,128)(2,1)S(1)}, u32[]{:S(2)}, u32[]{:S(2)}) collective-permute-start(bf16[48,512]{1,0:T(8,128)(2,1)S(1)} %get-tuple-element.15), channel_id=1, source_target_pairs={{0,20},{4,16},{8,28},{12,24},{16,4},{20,0},{24,12},{28,8},{1,21},{... | collective-permute-start | bytes 147464 | tf_op jit(solution)/shard_map/ppermute | solution.py:387
  14.1 0.0 collective-permute-done.partner_ref
  14.1 0.0 copy-done
  14.1 1.3 %fold_operator.1.operator_ref = bf16[2,256,256]{2,1,0:T(8,128)(2,1)S(1)} custom-call(s32[1]{0:T(128)} %bitcast.index_ref, bf16[400,128]{1,0:T(8,128)(2,1)S(1)} %copy-done, bf16[400,128]{1,0:T(8,128)(2,1)S(1)} %collective-permute-done.partner_ref), custom_call_target="tpu_custom_call" | custom-call | tf_op jit(solution)/shard_map/fold_operator/pallas_call | solution.py:167
  15.5 0.0 collective-permute-done.3.refs_0_
  15.5 0.8 %collective-permute-done.4.refs_1_ = bf16[48,512]{1,0:T(8,128)(2,1)S(1)} collective-permute-done((bf16[48,512]{1,0:T(8,128)(2,1)S(1)}, bf16[48,512]{1,0:T(8,128)(2,1)S(1)}, u32[]{:S(2)}, u32[]{:S(2)}) %collective-permute-start.4) | collective-permute-done | bytes 49184 | tf_op jit(solution)/shard_map/ppermute | solution.py:387
  16.2 1.8 %collective-permute-done.5.refs_2_ = bf16[48,512]{1,0:T(8,128)(2,1)S(1)} collective-permute-done((bf16[48,512]{1,0:T(8,128)(2,1)S(1)}, bf16[48,512]{1,0:T(8,128)(2,1)S(1)}, u32[]{:S(2)}, u32[]{:S(2)}) %collective-permute-start.5) | collective-permute-done | bytes 49184 | tf_op jit(solution)/shard_map/ppermute | solution.py:387
  18.1 1.1 %form_image.1 = bf16[256,1024]{1,0:T(8,128)(2,1)} custom-call(s32[1]{0:T(128)} %bitcast.index_ref, bf16[2,256,256]{2,1,0:T(8,128)(2,1)S(1)} %fold_operator.1.operator_ref, bf16[2,48,512]{2,1,0:T(8,128)(2,1)S(1)} %constant_dynamic-update-slice_fusion.both_ref, bf16[48,512]{1,0:T(8,128)(2,1)S(1)} %collective-permute-done.3.refs_0_, ...), custom_call_target="tpu_custom_call" | custom-call | tf_op jit(solution)/shard_map/form_image/pallas_call | solution.py:360
  (3 shorter events, 0.0 us)
Async XLA Ops:
  0.0 8.7 %collective-permute-start.1 = (bf16[6,2,4096]{2,1,0:T(2,128)(2,1)}, bf16[6,2,4096]{2,1,0:T(2,128)(2,1)S(1)}, u32[]{:S(2)}, u32[]{:S(2)}) collective-permute-start(bf16[6,2,4096]{2,1,0:T(2,128)(2,1)} %bitcast.15), channel_id=1, source_target_pairs={{1,0},{2,1},{3,2},{5,4},{6,5},{7,6},{9,8},{10,9},{11,10},{13,12},{... | collective-permute-start | bytes 294920 | tf_op jit(solution)/shard_map/ppermute | solution.py:393
  3.1 11.0 %copy-start = (bf16[400,128]{1,0:T(8,128)(2,1)S(1)}, bf16[400,128]{1,0:T(8,128)(2,1)}, u32[]{:S(2)}) copy-start(bf16[400,128]{1,0:T(8,128)(2,1)} %pack_parameters.1.own_ref) | copy-start | bytes 307204
  3.1 11.0 %collective-permute-start = (bf16[400,128]{1,0:T(8,128)(2,1)}, bf16[400,128]{1,0:T(8,128)(2,1)S(1)}, u32[]{:S(2)}, u32[]{:S(2)}) collective-permute-start(bf16[400,128]{1,0:T(8,128)(2,1)} %pack_parameters.1.own_ref), channel_id=1, source_target_pairs={{0,4},{4,0},{1,5},{5,1},{2,6},{6,2},{3,7},{7,3},{8,12},{12,8},{9,1... | collective-permute-start | bytes 307208 | tf_op jit(solution)/shard_map/ppermute | solution.py:377
  6.1 0.9 %copy-start.1 = (bf16[2,1,6,4096]{3,0,2,1:T(2,128)(2,1)S(1)}, bf16[2,1,6,4096]{3,0,2,1:T(2,128)(2,1)}, u32[]{:S(2)}) copy-start(bf16[2,1,6,4096]{3,0,2,1:T(2,128)(2,1)} %param.7) | copy-start | bytes 294916
  7.0 0.7 %copy-start.2 = (bf16[2,2048]{1,0:T(2,128)(2,1)S(1)}, bf16[2,2048]{1,0:T(2,128)(2,1)}, u32[]{:S(2)}) copy-start(bf16[2,2048]{1,0:T(2,128)(2,1)} %chirp_ref.1) | copy-start | bytes 24580
  9.3 1.3 %collective-permute-start.2 = (bf16[2,24,512]{2,1,0:T(8,128)(2,1)S(1)}, bf16[2,24,512]{2,1,0:T(8,128)(2,1)S(1)}, u32[]{:S(2)}, u32[]{:S(2)}) collective-permute-start(bf16[2,24,512]{2,1,0:T(8,128)(2,1)S(1)} %get-tuple-element.14), channel_id=1, source_target_pairs={{0,8},{8,0},{16,24},{24,16},{1,9},{9,1},{17,25},{25,17},{2,10},{10... | collective-permute-start | bytes 147464 | tf_op jit(solution)/shard_map/ppermute | solution.py:377
  10.6 4.9 %collective-permute-start.3 = (bf16[48,512]{1,0:T(8,128)(2,1)S(1)}, bf16[48,512]{1,0:T(8,128)(2,1)S(1)}, u32[]{:S(2)}, u32[]{:S(2)}) collective-permute-start(bf16[48,512]{1,0:T(8,128)(2,1)S(1)} %get-tuple-element.17), channel_id=1, source_target_pairs={{0,16},{4,20},{8,12},{12,8},{16,0},{20,4},{24,28},{28,24},{1,17},{... | collective-permute-start | bytes 147464 | tf_op jit(solution)/shard_map/ppermute | solution.py:387
  12.1 4.1 %collective-permute-start.4 = (bf16[48,512]{1,0:T(8,128)(2,1)S(1)}, bf16[48,512]{1,0:T(8,128)(2,1)S(1)}, u32[]{:S(2)}, u32[]{:S(2)}) collective-permute-start(bf16[48,512]{1,0:T(8,128)(2,1)S(1)} %get-tuple-element.16), channel_id=1, source_target_pairs={{0,4},{4,0},{8,24},{12,28},{16,20},{20,16},{24,8},{28,12},{1,5},{5... | collective-permute-start | bytes 147464 | tf_op jit(solution)/shard_map/ppermute | solution.py:387
  13.1 5.0 %collective-permute-start.5 = (bf16[48,512]{1,0:T(8,128)(2,1)S(1)}, bf16[48,512]{1,0:T(8,128)(2,1)S(1)}, u32[]{:S(2)}, u32[]{:S(2)}) collective-permute-start(bf16[48,512]{1,0:T(8,128)(2,1)S(1)} %get-tuple-element.15), channel_id=1, source_target_pairs={{0,20},{4,16},{8,28},{12,24},{16,4},{20,0},{24,12},{28,8},{1,21},{... | collective-permute-start | bytes 147464 | tf_op jit(solution)/shard_map/ppermute | solution.py:387

commit v2 on v1

--- a/solution.py
+++ b/solution.py
@@ -11,6 +11,10 @@
 SUBL = 8
 F32 = jnp.float32
 BF16 = jnp.bfloat16
+
+
+def cost(macs, moved):
+    return pl.CostEstimate(flops=2 * macs, bytes_accessed=moved, transcendentals=0)
 
 
 def ceil_to(value, unit):
@@ -61,6 +65,7 @@
         functools.partial(pack_kernel, sections=sections, group=group),
         out_shape=jax.ShapeDtypeStruct((pack_rows(levels, sides, parts, taps, sections, group), beams), BF16),
         scratch_shapes=[pltpu.VMEM((ceil_to(levels * sides, 16), beams), F32)],
+        cost_estimate=cost(0, 6 << 20),
         name="pack_parameters",
     )(coef, start, width, steer, order)
 
@@ -162,7 +167,7 @@
 
 
 def fold_operator(section, own, partner, dims, sections, group, each):
-    beams = dims[-1]
+    levels, beams = dims[0], dims[-1]
     width = sections * group
     return pl.pallas_call(
         functools.partial(operator_kernel, dims=dims, sections=sections, group=group, each=each),
@@ -174,6 +179,7 @@
         ],
         scratch_shapes=[pltpu.VMEM((width, beams), F32)],
         compiler_params=pltpu.CompilerParams(vmem_limit_bytes=16 * 1024 * 1024),
+        cost_estimate=cost(levels * 2 * 16 * width * beams * beams, 4 << 20),
         name="fold_operator",
     )(section, own, partner)
 
@@ -288,6 +294,11 @@
             give_ref[place] = stacked
 
 
+def pulses_macs(echo, taps):
+    pulses, _, length = echo.shape
+    return 4 * pulses * length * taps
+
+
 def row_scratch(blocks, group):
     return [
         pltpu.VMEM((2 * group, blocks * LANE), F32),
@@ -310,6 +321,7 @@
         ),
         scratch_shapes=row_scratch(length // LANE, group),
         compiler_params=pltpu.CompilerParams(vmem_limit_bytes=24 * 1024 * 1024),
+        cost_estimate=cost(pulses_macs(echo, taps) // 2, 4 << 20),
         name="begin_compression",
     )(echo, chirp)
 
@@ -322,6 +334,7 @@
         in_specs=[pl.BlockSpec(memory_space=pltpu.SMEM)] + [pl.BlockSpec(memory_space=pltpu.VMEM)] * 4,
         scratch_shapes=row_scratch(blocks, group),
         compiler_params=pltpu.CompilerParams(vmem_limit_bytes=24 * 1024 * 1024),
+        cost_estimate=cost(pulses_macs(halo, halo.shape[2] // 2) // 2, 2 << 20),
         name="finish_compression",
     )(section, early, late, halo, table)
 
@@ -368,6 +381,7 @@
             pltpu.SemaphoreType.DMA((count,)),
         ],
         compiler_params=pltpu.CompilerParams(vmem_limit_bytes=16 * 1024 * 1024),
+        cost_estimate=cost(height * height * 2 * half, 4 << 20),
         name="form_image",
     )(section, operator, both, *chunks)
 

time: 19.4 us -> 19.4 us (level)
  no operation moved by 1% of the time
where the time goes in v2:
time: 19.4 us; the launch traced here: 19.1 us
  starting transfers between devices  7.87 us (41%)
  Pallas kernels  5.76 us (30%)
  waiting for transfers between devices  3.81 us (20%)
  local copies, waits for them, and re-layouts  1.61 us (8%)
    ppermute x3, starting transfers between devices, swap_by(): return lax.ppermute(value, ('section', 'sub'), pairs)  3.55 us
    ppermute x2, starting transfers between devices, swap(): return lax.ppermute(value, axis, [(i, i ^ by) for i in range(count)])  3.04 us
    ppermute x3, waiting for transfers between devices, swap_by(): return lax.ppermute(value, ('section', 'sub'), pairs)  2.6 us
    pallas_call x1, Pallas kernels, pack_parameters(): pl.pallas_call(functools.partial(pack_kernel, sections=sections, group=gr...  1.82 us
    unnamed x7, local copies, waits for them, and re-layouts  1.6 us
    pallas_call x1, Pallas kernels, fold_operator(): pl.pallas_call(functools.partial(operator_kernel, dims=dims, sections=sec...  1.32 us
    ppermute x1, starting transfers between devices, from_behind(): return lax.ppermute(value, axis, pairs)  1.28 us
    ppermute x2, waiting for transfers between devices, swap(): return lax.ppermute(value, axis, [(i, i ^ by) for i in range(count)])  1.21 us
  transfers between devices with their start and end apart: 6, of which 3 were waited for; matrix products, arithmetic and copies ran while one was open for 0% of the time, Pallas kernels for 25%

profile of v2, /device:TPU:0, one launch (start us, length us, event | category | flops | bytes accessed | tf_op | source)
XLA Modules:
  0.0 19.1 jit_solution(13341592238796783290)
XLA Ops:
  0.0 1.3 %collective-permute-start.1 = (bf16[6,2,4096]{2,1,0:T(2,128)(2,1)}, bf16[6,2,4096]{2,1,0:T(2,128)(2,1)S(1)}, u32[]{:S(2)}, u32[]{:S(2)}) collective-permute-start(bf16[6,2,4096]{2,1,0:T(2,128)(2,1)} %bitcast.15), channel_id=1, source_target_pairs={{1,0},{2,1},{3,2},{5,4},{6,5},{7,6},{9,8},{10,9},{11,10},{13,12},{... | collective-permute-start | bytes 294920 | tf_op jit(solution)/shard_map/ppermute | solution.py:407
  1.3 1.8 %pack_parameters.1.own_ref = bf16[400,128]{1,0:T(8,128)(2,1)} custom-call(bf16[5,1,2,2,16,128]{5,4,3,2,1,0:T(8,128)(2,1)} %bitcast.17, s32[5,1,2,128]{3,2,1,0:T(2,128)} %start_ref.1, s32[5,1,2,128]{3,2,1,0:T(2,128)} %width_ref.1, bf16[2,1,24,128]{3,2,1,0:T(8,128)(2,1)} %bitcast.18, s32[1,24]{1,0:T(1,128)} %order_ref.1), custom_call_target="tpu_custom_call" | custom-call | bytes 6291456 | tf_op jit(solution)/shard_map/pack_parameters/pallas_call | solution.py:64
  3.1 0.0 copy-start
  3.1 3.0 %collective-permute-start = (bf16[400,128]{1,0:T(8,128)(2,1)}, bf16[400,128]{1,0:T(8,128)(2,1)S(1)}, u32[]{:S(2)}, u32[]{:S(2)}) collective-permute-start(bf16[400,128]{1,0:T(8,128)(2,1)} %pack_parameters.1.own_ref), channel_id=1, source_target_pairs={{0,4},{4,0},{1,5},{5,1},{2,6},{6,2},{3,7},{7,3},{8,12},{12,8},{9,1... | collective-permute-start | bytes 307208 | tf_op jit(solution)/shard_map/ppermute | solution.py:391
  6.1 0.0 copy-start.1
  6.1 0.9 %copy-done.1 = bf16[2,1,6,4096]{3,0,2,1:T(2,128)(2,1)S(1)} copy-done((bf16[2,1,6,4096]{3,0,2,1:T(2,128)(2,1)S(1)}, bf16[2,1,6,4096]{3,0,2,1:T(2,128)(2,1)}, u32[]{:S(2)}) %copy-start.1) | copy-done | bytes 98328
  7.0 0.0 copy-start.2
  7.0 0.7 %copy-done.2 = bf16[2,2048]{1,0:T(2,128)(2,1)S(1)} copy-done((bf16[2,2048]{1,0:T(2,128)(2,1)S(1)}, bf16[2,2048]{1,0:T(2,128)(2,1)}, u32[]{:S(2)}) %copy-start.2) | copy-done | bytes 8216
  7.7 1.0 %begin_compression.1 = (bf16[2,24,512]{2,1,0:T(8,128)(2,1)S(1)}, f32[16,2048]{1,0:T(8,128)S(1)}, bf16[4352,256]{1,0:T(8,128)(2,1)S(1)}) custom-call(bf16[6,2,4096]{2,1,0:T(2,128)(2,1)S(1)} %bitcast.16, bf16[2,2048]{1,0:T(2,128)(2,1)S(1)} %copy-done.2), custom_call_target="tpu_custom_call" | custom-call | flops 201326592 | bytes 4194304 | tf_op jit(solution)/shard_map/begin_compression/pallas_call | solution.py:315
  8.7 0.0 collective-permute-done.1.halo_ref
  8.7 0.5 %finish_compression.1 = (bf16[2,24,512]{2,1,0:T(8,128)(2,1)S(1)}, bf16[2,24,512]{2,1,0:T(8,128)(2,1)S(1)}) custom-call(s32[1]{0:T(128)} %bitcast.index_ref, bf16[2,24,512]{2,1,0:T(8,128)(2,1)S(1)} %get-tuple-element.10.early_ref, f32[16,2048]{1,0:T(8,128)S(1)} %get-tuple-element.11.late_ref, bf16[6,2,4096]{2,1,0:T(2,128)(2,1)S(1)} %collective-permute-done.1.halo_ref, ...), custom_call_target="tpu_custom_call" | custom-call | flops 201326592 | bytes 2097152 | tf_op jit(solution)/shard_map/finish_compression/pallas_call | solution.py:331
  9.2 0.1 collective-permute-start.2
  9.3 1.2 %collective-permute-done.2 = bf16[2,24,512]{2,1,0:T(8,128)(2,1)S(1)} collective-permute-done((bf16[2,24,512]{2,1,0:T(8,128)(2,1)S(1)}, bf16[2,24,512]{2,1,0:T(8,128)(2,1)S(1)}, u32[]{:S(2)}, u32[]{:S(2)}) %collective-permute-start.2) | collective-permute-done | bytes 49184 | tf_op jit(solution)/shard_map/ppermute | solution.py:391
  10.6 1.6 %collective-permute-start.3 = (bf16[48,512]{1,0:T(8,128)(2,1)S(1)}, bf16[48,512]{1,0:T(8,128)(2,1)S(1)}, u32[]{:S(2)}, u32[]{:S(2)}) collective-permute-start(bf16[48,512]{1,0:T(8,128)(2,1)S(1)} %get-tuple-element.17), channel_id=1, source_target_pairs={{0,16},{4,20},{8,12},{12,8},{16,0},{20,4},{24,28},{28,24},{1,17},{... | collective-permute-start | bytes 147464 | tf_op jit(solution)/shard_map/ppermute | solution.py:401
  12.1 0.9 %collective-permute-start.4 = (bf16[48,512]{1,0:T(8,128)(2,1)S(1)}, bf16[48,512]{1,0:T(8,128)(2,1)S(1)}, u32[]{:S(2)}, u32[]{:S(2)}) collective-permute-start(bf16[48,512]{1,0:T(8,128)(2,1)S(1)} %get-tuple-element.16), channel_id=1, source_target_pairs={{0,4},{4,0},{8,24},{12,28},{16,20},{20,16},{24,8},{28,12},{1,5},{5... | collective-permute-start | bytes 147464 | tf_op jit(solution)/shard_map/ppermute | solution.py:401
  13.1 1.1 %collective-permute-start.5 = (bf16[48,512]{1,0:T(8,128)(2,1)S(1)}, bf16[48,512]{1,0:T(8,128)(2,1)S(1)}, u32[]{:S(2)}, u32[]{:S(2)}) collective-permute-start(bf16[48,512]{1,0:T(8,128)(2,1)S(1)} %get-tuple-element.15), channel_id=1, source_target_pairs={{0,20},{4,16},{8,28},{12,24},{16,4},{20,0},{24,12},{28,8},{1,21},{... | collective-permute-start | bytes 147464 | tf_op jit(solution)/shard_map/ppermute | solution.py:401
  14.1 0.0 collective-permute-done.partner_ref
  14.1 0.0 copy-done
  14.1 1.3 %fold_operator.1.operator_ref = bf16[2,256,256]{2,1,0:T(8,128)(2,1)S(1)} custom-call(s32[1]{0:T(128)} %bitcast.index_ref, bf16[400,128]{1,0:T(8,128)(2,1)S(1)} %copy-done, bf16[400,128]{1,0:T(8,128)(2,1)S(1)} %collective-permute-done.partner_ref), custom_call_target="tpu_custom_call" | custom-call | flops 167772160 | bytes 4194304 | tf_op jit(solution)/shard_map/fold_operator/pallas_call | solution.py:172
  15.5 0.0 collective-permute-done.3.refs_0_
  15.5 0.8 %collective-permute-done.4.refs_1_ = bf16[48,512]{1,0:T(8,128)(2,1)S(1)} collective-permute-done((bf16[48,512]{1,0:T(8,128)(2,1)S(1)}, bf16[48,512]{1,0:T(8,128)(2,1)S(1)}, u32[]{:S(2)}, u32[]{:S(2)}) %collective-permute-start.4) | collective-permute-done | bytes 49184 | tf_op jit(solution)/shard_map/ppermute | solution.py:401
  16.2 1.8 %collective-permute-done.5.refs_2_ = bf16[48,512]{1,0:T(8,128)(2,1)S(1)} collective-permute-done((bf16[48,512]{1,0:T(8,128)(2,1)S(1)}, bf16[48,512]{1,0:T(8,128)(2,1)S(1)}, u32[]{:S(2)}, u32[]{:S(2)}) %collective-permute-start.5) | collective-permute-done | bytes 49184 | tf_op jit(solution)/shard_map/ppermute | solution.py:401
  18.1 1.1 %form_image.1 = bf16[256,1024]{1,0:T(8,128)(2,1)} custom-call(s32[1]{0:T(128)} %bitcast.index_ref, bf16[2,256,256]{2,1,0:T(8,128)(2,1)S(1)} %fold_operator.1.operator_ref, bf16[2,48,512]{2,1,0:T(8,128)(2,1)S(1)} %constant_dynamic-update-slice_fusion.both_ref, bf16[48,512]{1,0:T(8,128)(2,1)S(1)} %collective-permute-done.3.refs_0_, ...), custom_call_target="tpu_custom_call" | custom-call | flops 134217728 | bytes 4194304 | tf_op jit(solution)/shard_map/form_image/pallas_call | solution.py:373
  (3 shorter events, 0.0 us)
Async XLA Ops:
  0.0 8.7 %collective-permute-start.1 = (bf16[6,2,4096]{2,1,0:T(2,128)(2,1)}, bf16[6,2,4096]{2,1,0:T(2,128)(2,1)S(1)}, u32[]{:S(2)}, u32[]{:S(2)}) collective-permute-start(bf16[6,2,4096]{2,1,0:T(2,128)(2,1)} %bitcast.15), channel_id=1, source_target_pairs={{1,0},{2,1},{3,2},{5,4},{6,5},{7,6},{9,8},{10,9},{11,10},{13,12},{... | collective-permute-start | bytes 294920 | tf_op jit(solution)/shard_map/ppermute | solution.py:407
  3.1 11.0 %copy-start = (bf16[400,128]{1,0:T(8,128)(2,1)S(1)}, bf16[400,128]{1,0:T(8,128)(2,1)}, u32[]{:S(2)}) copy-start(bf16[400,128]{1,0:T(8,128)(2,1)} %pack_parameters.1.own_ref) | copy-start | bytes 307204
  3.1 11.0 %collective-permute-start = (bf16[400,128]{1,0:T(8,128)(2,1)}, bf16[400,128]{1,0:T(8,128)(2,1)S(1)}, u32[]{:S(2)}, u32[]{:S(2)}) collective-permute-start(bf16[400,128]{1,0:T(8,128)(2,1)} %pack_parameters.1.own_ref), channel_id=1, source_target_pairs={{0,4},{4,0},{1,5},{5,1},{2,6},{6,2},{3,7},{7,3},{8,12},{12,8},{9,1... | collective-permute-start | bytes 307208 | tf_op jit(solution)/shard_map/ppermute | solution.py:391
  6.1 0.9 %copy-start.1 = (bf16[2,1,6,4096]{3,0,2,1:T(2,128)(2,1)S(1)}, bf16[2,1,6,4096]{3,0,2,1:T(2,128)(2,1)}, u32[]{:S(2)}) copy-start(bf16[2,1,6,4096]{3,0,2,1:T(2,128)(2,1)} %param.7) | copy-start | bytes 294916
  7.0 0.7 %copy-start.2 = (bf16[2,2048]{1,0:T(2,128)(2,1)S(1)}, bf16[2,2048]{1,0:T(2,128)(2,1)}, u32[]{:S(2)}) copy-start(bf16[2,2048]{1,0:T(2,128)(2,1)} %chirp_ref.1) | copy-start | bytes 24580
  9.2 1.3 %collective-permute-start.2 = (bf16[2,24,512]{2,1,0:T(8,128)(2,1)S(1)}, bf16[2,24,512]{2,1,0:T(8,128)(2,1)S(1)}, u32[]{:S(2)}, u32[]{:S(2)}) collective-permute-start(bf16[2,24,512]{2,1,0:T(8,128)(2,1)S(1)} %get-tuple-element.14), channel_id=1, source_target_pairs={{0,8},{8,0},{16,24},{24,16},{1,9},{9,1},{17,25},{25,17},{2,10},{10... | collective-permute-start | bytes 147464 | tf_op jit(solution)/shard_map/ppermute | solution.py:391
  10.6 4.9 %collective-permute-start.3 = (bf16[48,512]{1,0:T(8,128)(2,1)S(1)}, bf16[48,512]{1,0:T(8,128)(2,1)S(1)}, u32[]{:S(2)}, u32[]{:S(2)}) collective-permute-start(bf16[48,512]{1,0:T(8,128)(2,1)S(1)} %get-tuple-element.17), channel_id=1, source_target_pairs={{0,16},{4,20},{8,12},{12,8},{16,0},{20,4},{24,28},{28,24},{1,17},{... | collective-permute-start | bytes 147464 | tf_op jit(solution)/shard_map/ppermute | solution.py:401
  12.1 4.1 %collective-permute-start.4 = (bf16[48,512]{1,0:T(8,128)(2,1)S(1)}, bf16[48,512]{1,0:T(8,128)(2,1)S(1)}, u32[]{:S(2)}, u32[]{:S(2)}) collective-permute-start(bf16[48,512]{1,0:T(8,128)(2,1)S(1)} %get-tuple-element.16), channel_id=1, source_target_pairs={{0,4},{4,0},{8,24},{12,28},{16,20},{20,16},{24,8},{28,12},{1,5},{5... | collective-permute-start | bytes 147464 | tf_op jit(solution)/shard_map/ppermute | solution.py:401
  13.1 5.0 %collective-permute-start.5 = (bf16[48,512]{1,0:T(8,128)(2,1)S(1)}, bf16[48,512]{1,0:T(8,128)(2,1)S(1)}, u32[]{:S(2)}, u32[]{:S(2)}) collective-permute-start(bf16[48,512]{1,0:T(8,128)(2,1)S(1)} %get-tuple-element.15), channel_id=1, source_target_pairs={{0,20},{4,16},{8,28},{12,24},{16,4},{20,0},{24,12},{28,8},{1,21},{... | collective-permute-start | bytes 147464 | tf_op jit(solution)/shard_map/ppermute | solution.py:401

commit v3 on v1

--- a/solution.py
+++ b/solution.py
@@ -17,7 +17,18 @@
     return -(-value // unit) * unit
 
 
-def pack_kernel(coef_ref, start_ref, width_ref, steer_ref, order_ref, pack_ref, starts, *, sections, group):
+def prepare_kernel(*refs, sections, group):
+    sources, (echo_out, chirp_out, pack_ref), scratch = refs[:7], refs[7:10], refs[10:]
+    coef_ref, start_ref, width_ref, steer_ref, order_ref, starts, sems = scratch
+    targets = (coef_ref, start_ref, width_ref, steer_ref, order_ref, chirp_out, echo_out)
+    loads = [
+        pltpu.make_async_copy(source, target, sems.at[i])
+        for i, (source, target) in enumerate(zip(sources, targets))
+    ]
+    for load in loads:
+        load.start()
+    for load in loads:
+        load.wait()
     levels, _, sides, parts, taps, beams = coef_ref.shape
     tap = lax.broadcasted_iota(jnp.int32, (taps, beams), 0)
     row = 0
@@ -55,14 +66,22 @@
     return levels * sides * parts * taps + parts * sections * group + ceil_to(levels * sides, 16)
 
 
-def pack_parameters(coef, start, width, steer, order, sections, group):
+def prepare(echo, chirp, coef, start, width, steer, order, sections, group):
     levels, _, sides, parts, taps, beams = coef.shape
+    sources = (coef, start, width, steer, order, chirp, echo)
     return pl.pallas_call(
-        functools.partial(pack_kernel, sections=sections, group=group),
-        out_shape=jax.ShapeDtypeStruct((pack_rows(levels, sides, parts, taps, sections, group), beams), BF16),
-        scratch_shapes=[pltpu.VMEM((ceil_to(levels * sides, 16), beams), F32)],
-        name="pack_parameters",
-    )(coef, start, width, steer, order)
+        functools.partial(prepare_kernel, sections=sections, group=group),
+        out_shape=(
+            jax.ShapeDtypeStruct(echo.shape, BF16),
+            jax.ShapeDtypeStruct(chirp.shape, BF16),
+            jax.ShapeDtypeStruct((pack_rows(levels, sides, parts, taps, sections, group), beams), BF16),
+        ),
+        in_specs=[pl.BlockSpec(memory_space=pl.ANY)] * len(sources),
+        scratch_shapes=[pltpu.VMEM(x.shape, x.dtype) for x in sources[:5]]
+        + [pltpu.VMEM((ceil_to(levels * sides, 16), beams), F32), pltpu.SemaphoreType.DMA((len(sources),))],
+        compiler_params=pltpu.CompilerParams(vmem_limit_bytes=16 * 1024 * 1024),
+        name="prepare",
+    )(*[pltpu.with_memory_space_constraint(x, pltpu.HBM) for x in sources])
 
 
 def pack_rows_of(real, imag, each):
@@ -405,7 +424,9 @@
 
     echo = jnp.transpose(echoes[:, 0], (1, 0, 2))
     halo = from_behind(echo, "rng", -1)
-    packed = pack_parameters(coef, band_start, band_width, weights, pulse_order, sections, group)
+    echo, chirp, packed = prepare(
+        echo, chirp, coef, band_start, band_width, weights, pulse_order, sections, group
+    )
     if subs == 2:
         packed_partner = swap(packed, "sub", 1)
     early, late, table = begin_compression(echo, chirp, sections, group)

time: 19.4 us -> 19.3 us (level)
  waiting for transfers between devices: 3.81 us -> 5.84 us
  local copies, waits for them, and re-layouts: 1.61 us -> 0.02 us
  Pallas kernels: 5.76 us -> 5.29 us
    unnamed x7 -> x1, local copies, waits for them, and re-layouts: 1.6 us -> 0.01 us
    ppermute x1, waiting for transfers between devices: 0.01 us -> 1.2 us  [from_behind(): return lax.ppermute(value, axis, pairs)]
    ppermute x3, waiting for transfers between devices: 2.6 us -> 3.44 us  [swap_by(): return lax.ppermute(value, ('section', 'sub'), pairs)]
    pallas_call x1, Pallas kernels: 1.82 us -> 1.35 us  [prepare(): pl.pallas_call(functools.partial(prepare_kernel, sections=sections, group...]
  transfers between devices with their start and end apart: 6 -> 6, of which waited for: 3 -> 4; matrix products, arithmetic and copies ran while one was open for 0% -> 0% of each run, Pallas kernels for 25% -> 22%
where the time goes in v3:
time: 19.3 us; the launch traced here: 19.2 us
  starting transfers between devices  7.94 us (41%)
  waiting for transfers between devices  5.84 us (30%)
  Pallas kernels  5.29 us (27%)
    ppermute x3, starting transfers between devices, swap_by(): return lax.ppermute(value, ('section', 'sub'), pairs)  3.55 us
    ppermute x3, waiting for transfers between devices, swap_by(): return lax.ppermute(value, ('section', 'sub'), pairs)  3.44 us
    ppermute x2, starting transfers between devices, swap(): return lax.ppermute(value, axis, [(i, i ^ by) for i in range(count)])  3.1 us
    pallas_call x1, Pallas kernels, prepare(): pl.pallas_call(functools.partial(prepare_kernel, sections=sections, group...  1.35 us
    pallas_call x1, Pallas kernels, fold_operator(): pl.pallas_call(functools.partial(operator_kernel, dims=dims, sections=sec...  1.32 us
    ppermute x1, starting transfers between devices, from_behind(): return lax.ppermute(value, axis, pairs)  1.28 us
    ppermute x2, waiting for transfers between devices, swap(): return lax.ppermute(value, axis, [(i, i ^ by) for i in range(count)])  1.21 us
    ppermute x1, waiting for transfers between devices, from_behind(): return lax.ppermute(value, axis, pairs)  1.2 us
  transfers between devices with their start and end apart: 6, of which 4 were waited for; matrix products, arithmetic and copies ran while one was open for 0% of the time, Pallas kernels for 22%

profile of v3, /device:TPU:0, one launch (start us, length us, event | category | flops | bytes accessed | tf_op | source)
XLA Modules:
  0.0 19.2 jit_solution(5411005916242657716)
XLA Ops:
  0.0 1.3 %collective-permute-start.1 = (bf16[6,2,4096]{2,1,0:T(2,128)(2,1)}, bf16[6,2,4096]{2,1,0:T(2,128)(2,1)S(1)}, u32[]{:S(2)}, u32[]{:S(2)}) collective-permute-start(bf16[6,2,4096]{2,1,0:T(2,128)(2,1)} %bitcast.15), channel_id=1, source_target_pairs={{1,0},{2,1},{3,2},{5,4},{6,5},{7,6},{9,8},{10,9},{11,10},{13,12},{... | collective-permute-start | bytes 294920 | tf_op jit(solution)/shard_map/ppermute | solution.py:412
  1.3 1.3 %prepare.1 = (bf16[6,2,4096]{2,1,0:T(2,128)(2,1)S(1)}, bf16[2,2048]{1,0:T(2,128)(2,1)S(1)}, bf16[400,128]{1,0:T(8,128)(2,1)S(1)}) custom-call(bf16[5,1,2,2,16,128]{5,4,3,2,1,0:T(8,128)(2,1)} %bitcast.17, s32[5,1,2,128]{3,2,1,0:T(2,128)} %refs_1_.1, s32[5,1,2,128]{3,2,1,0:T(2,128)} %refs_2_.1, bf16[2,1,24,128]{3,2,1,0:T(8,128)(2,1)} %bitcast.18, ...), custom_call_target="tpu_custom_call" | custom-call | tf_op jit(solution)/shard_map/prepare/pallas_call | solution.py:72
  2.6 3.0 %collective-permute-start = (bf16[400,128]{1,0:T(8,128)(2,1)S(1)}, bf16[400,128]{1,0:T(8,128)(2,1)S(1)}, u32[]{:S(2)}, u32[]{:S(2)}) collective-permute-start(bf16[400,128]{1,0:T(8,128)(2,1)S(1)} %get-tuple-element.13.own_ref), channel_id=1, source_target_pairs={{0,4},{4,0},{1,5},{5,1},{2,6},{6,2},{3,7},{7,3},{8,12},{12,8},{9,1... | collective-permute-start | bytes 307208 | tf_op jit(solution)/shard_map/ppermute | solution.py:396
  5.7 1.0 %begin_compression.1 = (bf16[2,24,512]{2,1,0:T(8,128)(2,1)S(1)}, f32[16,2048]{1,0:T(8,128)S(1)}, bf16[4352,256]{1,0:T(8,128)(2,1)S(1)}) custom-call(bf16[6,2,4096]{2,1,0:T(2,128)(2,1)S(1)} %get-tuple-element.14.echo_ref, bf16[2,2048]{1,0:T(2,128)(2,1)S(1)} %get-tuple-element.15.chirp_ref), custom_call_target="tpu_custom_call" | custom-call | tf_op jit(solution)/shard_map/begin_compression/pallas_call | solution.py:323
  6.7 1.2 %collective-permute-done.1.halo_ref = bf16[6,2,4096]{2,1,0:T(2,128)(2,1)S(1)} collective-permute-done((bf16[6,2,4096]{2,1,0:T(2,128)(2,1)}, bf16[6,2,4096]{2,1,0:T(2,128)(2,1)S(1)}, u32[]{:S(2)}, u32[]{:S(2)}) %collective-permute-start.1) | collective-permute-done | bytes 98336 | tf_op jit(solution)/shard_map/ppermute | solution.py:412
  7.9 0.5 %finish_compression.1 = (bf16[2,24,512]{2,1,0:T(8,128)(2,1)S(1)}, bf16[2,24,512]{2,1,0:T(8,128)(2,1)S(1)}) custom-call(s32[1]{0:T(128)} %bitcast.index_ref, bf16[2,24,512]{2,1,0:T(8,128)(2,1)S(1)} %get-tuple-element.16.early_ref, f32[16,2048]{1,0:T(8,128)S(1)} %get-tuple-element.17.late_ref, bf16[6,2,4096]{2,1,0:T(2,128)(2,1)S(1)} %collective-permute-done.1.halo_ref, ...), custom_call_target="tpu_custom_call" | custom-call | tf_op jit(solution)/shard_map/finish_compression/pallas_call | solution.py:338
  8.4 0.1 collective-permute-start.2
  8.5 1.2 %collective-permute-done.2 = bf16[2,24,512]{2,1,0:T(8,128)(2,1)S(1)} collective-permute-done((bf16[2,24,512]{2,1,0:T(8,128)(2,1)S(1)}, bf16[2,24,512]{2,1,0:T(8,128)(2,1)S(1)}, u32[]{:S(2)}, u32[]{:S(2)}) %collective-permute-start.2) | collective-permute-done | bytes 49184 | tf_op jit(solution)/shard_map/ppermute | solution.py:396
  9.8 1.8 %collective-permute-start.3 = (bf16[48,512]{1,0:T(8,128)(2,1)S(1)}, bf16[48,512]{1,0:T(8,128)(2,1)S(1)}, u32[]{:S(2)}, u32[]{:S(2)}) collective-permute-start(bf16[48,512]{1,0:T(8,128)(2,1)S(1)} %get-tuple-element.23), channel_id=1, source_target_pairs={{0,16},{4,20},{8,12},{12,8},{16,0},{20,4},{24,28},{28,24},{1,17},{... | collective-permute-start | bytes 147464 | tf_op jit(solution)/shard_map/ppermute | solution.py:406
  11.6 1.5 %collective-permute-start.4 = (bf16[48,512]{1,0:T(8,128)(2,1)S(1)}, bf16[48,512]{1,0:T(8,128)(2,1)S(1)}, u32[]{:S(2)}, u32[]{:S(2)}) collective-permute-start(bf16[48,512]{1,0:T(8,128)(2,1)S(1)} %get-tuple-element.22), channel_id=1, source_target_pairs={{0,4},{4,0},{8,24},{12,28},{16,20},{20,16},{24,8},{28,12},{1,5},{5... | collective-permute-start | bytes 147464 | tf_op jit(solution)/shard_map/ppermute | solution.py:406
  13.1 0.2 %collective-permute-start.5 = (bf16[48,512]{1,0:T(8,128)(2,1)S(1)}, bf16[48,512]{1,0:T(8,128)(2,1)S(1)}, u32[]{:S(2)}, u32[]{:S(2)}) collective-permute-start(bf16[48,512]{1,0:T(8,128)(2,1)S(1)} %get-tuple-element.21), channel_id=1, source_target_pairs={{0,20},{4,16},{8,28},{12,24},{16,4},{20,0},{24,12},{28,8},{1,21},{... | collective-permute-start | bytes 147464 | tf_op jit(solution)/shard_map/ppermute | solution.py:406
  13.3 0.0 collective-permute-done.partner_ref
  13.3 1.3 %fold_operator.1.operator_ref = bf16[2,256,256]{2,1,0:T(8,128)(2,1)S(1)} custom-call(s32[1]{0:T(128)} %bitcast.index_ref, bf16[400,128]{1,0:T(8,128)(2,1)S(1)} %get-tuple-element.13.own_ref, bf16[400,128]{1,0:T(8,128)(2,1)S(1)} %collective-permute-done.partner_ref), custom_call_target="tpu_custom_call" | custom-call | tf_op jit(solution)/shard_map/fold_operator/pallas_call | solution.py:186
  14.6 0.0 collective-permute-done.3.refs_0_
  14.7 1.0 %collective-permute-done.4.refs_1_ = bf16[48,512]{1,0:T(8,128)(2,1)S(1)} collective-permute-done((bf16[48,512]{1,0:T(8,128)(2,1)S(1)}, bf16[48,512]{1,0:T(8,128)(2,1)S(1)}, u32[]{:S(2)}, u32[]{:S(2)}) %collective-permute-start.4) | collective-permute-done | bytes 49184 | tf_op jit(solution)/shard_map/ppermute | solution.py:406
  15.7 2.4 %collective-permute-done.5.refs_2_ = bf16[48,512]{1,0:T(8,128)(2,1)S(1)} collective-permute-done((bf16[48,512]{1,0:T(8,128)(2,1)S(1)}, bf16[48,512]{1,0:T(8,128)(2,1)S(1)}, u32[]{:S(2)}, u32[]{:S(2)}) %collective-permute-start.5) | collective-permute-done | bytes 49184 | tf_op jit(solution)/shard_map/ppermute | solution.py:406
  18.1 1.1 %form_image.1 = bf16[256,1024]{1,0:T(8,128)(2,1)} custom-call(s32[1]{0:T(128)} %bitcast.index_ref, bf16[2,256,256]{2,1,0:T(8,128)(2,1)S(1)} %fold_operator.1.operator_ref, bf16[2,48,512]{2,1,0:T(8,128)(2,1)S(1)} %constant_dynamic-update-slice_fusion.both_ref, bf16[48,512]{1,0:T(8,128)(2,1)S(1)} %collective-permute-done.3.refs_0_, ...), custom_call_target="tpu_custom_call" | custom-call | tf_op jit(solution)/shard_map/form_image/pallas_call | solution.py:379
  (3 shorter events, 0.0 us)
Async XLA Ops:
  0.0 7.9 %collective-permute-start.1 = (bf16[6,2,4096]{2,1,0:T(2,128)(2,1)}, bf16[6,2,4096]{2,1,0:T(2,128)(2,1)S(1)}, u32[]{:S(2)}, u32[]{:S(2)}) collective-permute-start(bf16[6,2,4096]{2,1,0:T(2,128)(2,1)} %bitcast.15), channel_id=1, source_target_pairs={{1,0},{2,1},{3,2},{5,4},{6,5},{7,6},{9,8},{10,9},{11,10},{13,12},{... | collective-permute-start | bytes 294920 | tf_op jit(solution)/shard_map/ppermute | solution.py:412
  2.6 10.7 %collective-permute-start = (bf16[400,128]{1,0:T(8,128)(2,1)S(1)}, bf16[400,128]{1,0:T(8,128)(2,1)S(1)}, u32[]{:S(2)}, u32[]{:S(2)}) collective-permute-start(bf16[400,128]{1,0:T(8,128)(2,1)S(1)} %get-tuple-element.13.own_ref), channel_id=1, source_target_pairs={{0,4},{4,0},{1,5},{5,1},{2,6},{6,2},{3,7},{7,3},{8,12},{12,8},{9,1... | collective-permute-start | bytes 307208 | tf_op jit(solution)/shard_map/ppermute | solution.py:396
  8.4 1.3 %collective-permute-start.2 = (bf16[2,24,512]{2,1,0:T(8,128)(2,1)S(1)}, bf16[2,24,512]{2,1,0:T(8,128)(2,1)S(1)}, u32[]{:S(2)}, u32[]{:S(2)}) collective-permute-start(bf16[2,24,512]{2,1,0:T(8,128)(2,1)S(1)} %get-tuple-element.20), channel_id=1, source_target_pairs={{0,8},{8,0},{16,24},{24,16},{1,9},{9,1},{17,25},{25,17},{2,10},{10... | collective-permute-start | bytes 147464 | tf_op jit(solution)/shard_map/ppermute | solution.py:396
  9.8 4.9 %collective-permute-start.3 = (bf16[48,512]{1,0:T(8,128)(2,1)S(1)}, bf16[48,512]{1,0:T(8,128)(2,1)S(1)}, u32[]{:S(2)}, u32[]{:S(2)}) collective-permute-start(bf16[48,512]{1,0:T(8,128)(2,1)S(1)} %get-tuple-element.23), channel_id=1, source_target_pairs={{0,16},{4,20},{8,12},{12,8},{16,0},{20,4},{24,28},{28,24},{1,17},{... | collective-permute-start | bytes 147464 | tf_op jit(solution)/shard_map/ppermute | solution.py:406
  11.6 4.1 %collective-permute-start.4 = (bf16[48,512]{1,0:T(8,128)(2,1)S(1)}, bf16[48,512]{1,0:T(8,128)(2,1)S(1)}, u32[]{:S(2)}, u32[]{:S(2)}) collective-permute-start(bf16[48,512]{1,0:T(8,128)(2,1)S(1)} %get-tuple-element.22), channel_id=1, source_target_pairs={{0,4},{4,0},{8,24},{12,28},{16,20},{20,16},{24,8},{28,12},{1,5},{5... | collective-permute-start | bytes 147464 | tf_op jit(solution)/shard_map/ppermute | solution.py:406
  13.1 5.0 %collective-permute-start.5 = (bf16[48,512]{1,0:T(8,128)(2,1)S(1)}, bf16[48,512]{1,0:T(8,128)(2,1)S(1)}, u32[]{:S(2)}, u32[]{:S(2)}) collective-permute-start(bf16[48,512]{1,0:T(8,128)(2,1)S(1)} %get-tuple-element.21), channel_id=1, source_target_pairs={{0,20},{4,16},{8,28},{12,24},{16,4},{20,0},{24,12},{28,8},{1,21},{... | collective-permute-start | bytes 147464 | tf_op jit(solution)/shard_map/ppermute | solution.py:406

commit v4 on v3

--- a/solution.py
+++ b/solution.py
@@ -172,7 +172,9 @@
     for half, rest in enumerate((left, right)):
         sources = [jnp.concatenate([full[j], rest[j]], axis=0) for j in range(2 * sections)]
         quarters = [jnp.concatenate(sources[q * pairs : (q + 1) * pairs], axis=0) for q in range(4)]
-        quarters[1:3] = [
+        quarters = [
+            quarters[0],
+            quarters[3],
             jnp.where(first_core, quarters[1], quarters[2]),
             jnp.where(first_core, quarters[2], quarters[1]),
         ]
@@ -285,7 +287,7 @@
     rows[:, :span] = late_ref[...]
     rows[:, span:] = jnp.zeros((2 * group, taps), F32)
     for p in range(pulses):
-        far = halo_ref[p, :, :taps].astype(F32)
+        far = jnp.where(index_ref[1] != 0, halo_ref[p, :, :taps].astype(F32), 0.0)
         for c in range(2):
             rows[c * group + p : c * group + p + 1, span:] = far[c : c + 1]
     done = correlate(rows, even, odd, table, span // LANE, group)
@@ -333,7 +335,7 @@
     )(echo, chirp)
 
 
-def finish_compression(section, early, late, halo, table, group):
+def finish_compression(place, early, late, halo, table, group):
     blocks = late.shape[1] // LANE + table.shape[0] // (2 * LANE) - 1
     return pl.pallas_call(
         functools.partial(finish_kernel, group=group),
@@ -342,7 +344,7 @@
         scratch_shapes=row_scratch(blocks, group),
         compiler_params=pltpu.CompilerParams(vmem_limit_bytes=24 * 1024 * 1024),
         name="finish_compression",
-    )(section, early, late, halo, table)
+    )(place, early, late, halo, table)
 
 
 def image_kernel(index_ref, operator_ref, both_ref, *refs, group):
@@ -406,10 +408,16 @@
     return lax.ppermute(value, ("section", "sub"), pairs)
 
 
-def from_behind(value, axis, by):
-    size = lax.axis_size(axis)
-    pairs = [(i, i + by) for i in range(size) if 0 <= i + by < size]
-    return lax.ppermute(value, axis, pairs)
+def from_next(value):
+    sections, others, count = lax.axis_size("section"), lax.axis_size("sub"), lax.axis_size("rng")
+    pairs = []
+    for s in range(sections):
+        for a in range(others):
+            first = (s * others + a) * count
+            pairs += [(first + i, first + i - 1) for i in range(1, count)]
+            if s:
+                pairs.append((first, first + count - 1))
+    return lax.ppermute(value, ("section", "sub", "rng"), pairs)
 
 
 def on_device(echoes, chirp, steer, pulse_order, band_coef, band_start, band_width):
@@ -423,14 +431,16 @@
     dims = (levels, sides, parts, taps, beams)
 
     echo = jnp.transpose(echoes[:, 0], (1, 0, 2))
-    halo = from_behind(echo, "rng", -1)
+    halo = from_next(echo)
+    has_next = (lax.axis_index("rng") < lax.axis_size("rng") - 1).astype(jnp.int32)
     echo, chirp, packed = prepare(
         echo, chirp, coef, band_start, band_width, weights, pulse_order, sections, group
     )
     if subs == 2:
         packed_partner = swap(packed, "sub", 1)
     early, late, table = begin_compression(echo, chirp, sections, group)
-    keep, give = finish_compression(section, early, late, halo, table, group)
+    place = jnp.stack([section[0], has_next])
+    keep, give = finish_compression(place, early, late, halo, table, group)
     both = jnp.concatenate([keep, swap(give, "section", 1)], axis=1)
     far = lax.dynamic_index_in_dim(both, section[0] % 2, 0, keepdims=False)
     if subs != 2:
@@ -438,9 +448,9 @@
         chunks = [near, swap(far, "section", 2)]
         return merge_images(section, chunks, packed, dims, sections, group, pulses_each)
     chunks = [
+        swap_by(far, lambda s, a: (s ^ 2, a ^ 1)),
         swap_by(both[0], lambda s, a: (s, a ^ 1) if s % 2 else (s ^ 2, a)),
         swap_by(both[1], lambda s, a: (s ^ 2, a) if s % 2 else (s, a ^ 1)),
-        swap_by(far, lambda s, a: (s ^ 2, a ^ 1)),
     ]
     operator = fold_operator(section, packed, packed_partner, dims, sections, group, pulses_each)
     image = form_image(section, operator, both, chunks, group)

time: 19.3 us -> 20.6 us (1.067)
  starting transfers between devices: 7.94 us -> 10.8 us
  waiting for transfers between devices: 5.84 us -> 3.6 us
  Pallas kernels: 5.29 us -> 5.82 us
    ppermute x2, starting transfers between devices: 3.1 us -> 5.47 us  [swap(): return lax.ppermute(value, axis, [(i, i ^ by) for i in range(count)])]
    ppermute x3, waiting for transfers between devices: 3.44 us -> 1.6 us  [swap_by(): return lax.ppermute(value, ('section', 'sub'), pairs)]
    ppermute x3, starting transfers between devices: 3.55 us -> 4.1 us  [swap_by(): return lax.ppermute(value, ('section', 'sub'), pairs)]
    pallas_call x1, Pallas kernels: 0.52 us -> 1.05 us  [finish_compression(): pl.pallas_call(functools.partial(finish_kernel, group=group), out_shape=[...]
    ppermute x2, waiting for transfers between devices: 1.21 us -> 0.88 us  [swap(): return lax.ppermute(value, axis, [(i, i ^ by) for i in range(count)])]
  transfers between devices with their start and end apart: 6 -> 6, of which waited for: 4 -> 3; matrix products, arithmetic and copies ran while one was open for 0% -> 0% of each run, Pallas kernels for 22% -> 23%
where the time goes in v4:
time: 20.6 us; the launch traced here: 20.4 us
  starting transfers between devices  10.8 us (52%)
  Pallas kernels  5.82 us (28%)
  waiting for transfers between devices  3.6 us (17%)
    ppermute x2, starting transfers between devices, swap(): return lax.ppermute(value, axis, [(i, i ^ by) for i in range(count)])  5.47 us
    ppermute x3, starting transfers between devices, swap_by(): return lax.ppermute(value, ('section', 'sub'), pairs)  4.1 us
    ppermute x3, waiting for transfers between devices, swap_by(): return lax.ppermute(value, ('section', 'sub'), pairs)  1.6 us
    pallas_call x1, Pallas kernels, prepare(): pl.pallas_call(functools.partial(prepare_kernel, sections=sections, group...  1.35 us
    pallas_call x1, Pallas kernels, fold_operator(): pl.pallas_call(functools.partial(operator_kernel, dims=dims, sections=sec...  1.32 us
    ppermute x1, starting transfers between devices, from_next(): return lax.ppermute(value, ('section', 'sub', 'rng'), pairs)  1.28 us
    ppermute x1, waiting for transfers between devices, from_next(): return lax.ppermute(value, ('section', 'sub', 'rng'), pairs)  1.12 us
    pallas_call x1, Pallas kernels, form_image(): pl.pallas_call(functools.partial(image_kernel, group=group), out_shape=ja...  1.06 us
  transfers between devices with their start and end apart: 6, of which 3 were waited for; matrix products, arithmetic and copies ran while one was open for 0% of the time, Pallas kernels for 23%

profile of v4, /device:TPU:0, one launch (start us, length us, event | category | flops | bytes accessed | tf_op | source)
XLA Modules:
  0.0 20.4 jit_solution(11495079142269625315)
XLA Ops:
  0.0 1.3 %collective-permute-start.1 = (bf16[6,2,4096]{2,1,0:T(2,128)(2,1)}, bf16[6,2,4096]{2,1,0:T(2,128)(2,1)S(1)}, u32[]{:S(2)}, u32[]{:S(2)}) collective-permute-start(bf16[6,2,4096]{2,1,0:T(2,128)(2,1)} %bitcast.16), channel_id=1, source_target_pairs={{1,0},{2,1},{3,2},{5,4},{6,5},{7,6},{9,8},{10,9},{11,10},{8,11},{1... | collective-permute-start | bytes 294920 | tf_op jit(solution)/shard_map/ppermute | solution.py:420
  1.3 1.3 %prepare.1 = (bf16[6,2,4096]{2,1,0:T(2,128)(2,1)S(1)}, bf16[2,2048]{1,0:T(2,128)(2,1)S(1)}, bf16[400,128]{1,0:T(8,128)(2,1)S(1)}) custom-call(bf16[5,1,2,2,16,128]{5,4,3,2,1,0:T(8,128)(2,1)} %bitcast.18, s32[5,1,2,128]{3,2,1,0:T(2,128)} %refs_1_.1, s32[5,1,2,128]{3,2,1,0:T(2,128)} %refs_2_.1, bf16[2,1,24,128]{3,2,1,0:T(8,128)(2,1)} %bitcast.19, ...), custom_call_target="tpu_custom_call" | custom-call | tf_op jit(solution)/shard_map/prepare/pallas_call | solution.py:72
  2.6 3.0 %collective-permute-start = (bf16[400,128]{1,0:T(8,128)(2,1)S(1)}, bf16[400,128]{1,0:T(8,128)(2,1)S(1)}, u32[]{:S(2)}, u32[]{:S(2)}) collective-permute-start(bf16[400,128]{1,0:T(8,128)(2,1)S(1)} %get-tuple-element.13.own_ref), channel_id=1, source_target_pairs={{0,4},{4,0},{1,5},{5,1},{2,6},{6,2},{3,7},{7,3},{8,12},{12,8},{9,1... | collective-permute-start | bytes 307208 | tf_op jit(solution)/shard_map/ppermute | solution.py:398
  5.7 1.0 %begin_compression.1 = (bf16[2,24,512]{2,1,0:T(8,128)(2,1)S(1)}, f32[16,2048]{1,0:T(8,128)S(1)}, bf16[4352,256]{1,0:T(8,128)(2,1)S(1)}) custom-call(bf16[6,2,4096]{2,1,0:T(2,128)(2,1)S(1)} %get-tuple-element.14.echo_ref, bf16[2,2048]{1,0:T(2,128)(2,1)S(1)} %get-tuple-element.15.chirp_ref), custom_call_target="tpu_custom_call" | custom-call | tf_op jit(solution)/shard_map/begin_compression/pallas_call | solution.py:325
  6.7 0.1 pad_add_fusion.index_ref
  6.8 1.1 %collective-permute-done.1.halo_ref = bf16[6,2,4096]{2,1,0:T(2,128)(2,1)S(1)} collective-permute-done((bf16[6,2,4096]{2,1,0:T(2,128)(2,1)}, bf16[6,2,4096]{2,1,0:T(2,128)(2,1)S(1)}, u32[]{:S(2)}, u32[]{:S(2)}) %collective-permute-start.1) | collective-permute-done | bytes 98336 | tf_op jit(solution)/shard_map/ppermute | solution.py:420
  7.9 1.1 %finish_compression.1 = (bf16[2,24,512]{2,1,0:T(8,128)(2,1)S(1)}, bf16[2,24,512]{2,1,0:T(8,128)(2,1)S(1)}) custom-call(s32[2]{0:T(128)S(1)} %pad_add_fusion.index_ref, bf16[2,24,512]{2,1,0:T(8,128)(2,1)S(1)} %get-tuple-element.16.early_ref, f32[16,2048]{1,0:T(8,128)S(1)} %get-tuple-element.17.late_ref, ...), custom_call_target="tpu_custom_call" | custom-call | tf_op jit(solution)/shard_map/finish_compression/pallas_call | solution.py:340
  9.0 2.4 %collective-permute-start.2 = (bf16[2,24,512]{2,1,0:T(8,128)(2,1)S(1)}, bf16[2,24,512]{2,1,0:T(8,128)(2,1)S(1)}, u32[]{:S(2)}, u32[]{:S(2)}) collective-permute-start(bf16[2,24,512]{2,1,0:T(8,128)(2,1)S(1)} %get-tuple-element.20), channel_id=1, source_target_pairs={{0,8},{8,0},{16,24},{24,16},{1,9},{9,1},{17,25},{25,17},{2,10},{10... | collective-permute-start | bytes 147464 | tf_op jit(solution)/shard_map/ppermute | solution.py:398
  11.4 0.9 %collective-permute-done.2 = bf16[2,24,512]{2,1,0:T(8,128)(2,1)S(1)} collective-permute-done((bf16[2,24,512]{2,1,0:T(8,128)(2,1)S(1)}, bf16[2,24,512]{2,1,0:T(8,128)(2,1)S(1)}, u32[]{:S(2)}, u32[]{:S(2)}) %collective-permute-start.2) | collective-permute-done | bytes 49184 | tf_op jit(solution)/shard_map/ppermute | solution.py:398
  12.3 2.6 %collective-permute-start.3 = (bf16[48,512]{1,0:T(8,128)(2,1)S(1)}, bf16[48,512]{1,0:T(8,128)(2,1)S(1)}, u32[]{:S(2)}, u32[]{:S(2)}) collective-permute-start(bf16[48,512]{1,0:T(8,128)(2,1)S(1)} %get-tuple-element.23), channel_id=1, source_target_pairs={{0,20},{4,16},{8,28},{12,24},{16,4},{20,0},{24,12},{28,8},{1,21},{... | collective-permute-start | bytes 147464 | tf_op jit(solution)/shard_map/ppermute | solution.py:408
  14.9 0.1 collective-permute-start.4
  15.0 1.4 %collective-permute-start.5 = (bf16[48,512]{1,0:T(8,128)(2,1)S(1)}, bf16[48,512]{1,0:T(8,128)(2,1)S(1)}, u32[]{:S(2)}, u32[]{:S(2)}) collective-permute-start(bf16[48,512]{1,0:T(8,128)(2,1)S(1)} %get-tuple-element.21), channel_id=1, source_target_pairs={{0,4},{4,0},{8,24},{12,28},{16,20},{20,16},{24,8},{28,12},{1,5},{5... | collective-permute-start | bytes 147464 | tf_op jit(solution)/shard_map/ppermute | solution.py:408
  16.4 0.0 collective-permute-done.partner_ref
  16.4 1.3 %fold_operator.1.operator_ref = bf16[2,256,256]{2,1,0:T(8,128)(2,1)S(1)} custom-call(s32[1]{0:T(128)} %bitcast.index_ref, bf16[400,128]{1,0:T(8,128)(2,1)S(1)} %get-tuple-element.13.own_ref, bf16[400,128]{1,0:T(8,128)(2,1)S(1)} %collective-permute-done.partner_ref), custom_call_target="tpu_custom_call" | custom-call | tf_op jit(solution)/shard_map/fold_operator/pallas_call | solution.py:188
  17.8 0.0 collective-permute-done.3.refs_0_
  17.8 1.6 %collective-permute-done.4.refs_1_ = bf16[48,512]{1,0:T(8,128)(2,1)S(1)} collective-permute-done((bf16[48,512]{1,0:T(8,128)(2,1)S(1)}, bf16[48,512]{1,0:T(8,128)(2,1)S(1)}, u32[]{:S(2)}, u32[]{:S(2)}) %collective-permute-start.4) | collective-permute-done | bytes 49184 | tf_op jit(solution)/shard_map/ppermute | solution.py:408
  19.4 0.0 collective-permute-done.5.refs_2_
  19.4 1.1 %form_image.1 = bf16[256,1024]{1,0:T(8,128)(2,1)} custom-call(s32[1]{0:T(128)} %bitcast.index_ref, bf16[2,256,256]{2,1,0:T(8,128)(2,1)S(1)} %fold_operator.1.operator_ref, bf16[2,48,512]{2,1,0:T(8,128)(2,1)S(1)} %constant_dynamic-update-slice_fusion.both_ref, bf16[48,512]{1,0:T(8,128)(2,1)S(1)} %collective-permute-done.3.refs_0_, ...), custom_call_target="tpu_custom_call" | custom-call | tf_op jit(solution)/shard_map/form_image/pallas_call | solution.py:381
  (3 shorter events, 0.0 us)
Async XLA Ops:
  0.0 7.9 %collective-permute-start.1 = (bf16[6,2,4096]{2,1,0:T(2,128)(2,1)}, bf16[6,2,4096]{2,1,0:T(2,128)(2,1)S(1)}, u32[]{:S(2)}, u32[]{:S(2)}) collective-permute-start(bf16[6,2,4096]{2,1,0:T(2,128)(2,1)} %bitcast.16), channel_id=1, source_target_pairs={{1,0},{2,1},{3,2},{5,4},{6,5},{7,6},{9,8},{10,9},{11,10},{8,11},{1... | collective-permute-start | bytes 294920 | tf_op jit(solution)/shard_map/ppermute | solution.py:420
  2.6 13.8 %collective-permute-start = (bf16[400,128]{1,0:T(8,128)(2,1)S(1)}, bf16[400,128]{1,0:T(8,128)(2,1)S(1)}, u32[]{:S(2)}, u32[]{:S(2)}) collective-permute-start(bf16[400,128]{1,0:T(8,128)(2,1)S(1)} %get-tuple-element.13.own_ref), channel_id=1, source_target_pairs={{0,4},{4,0},{1,5},{5,1},{2,6},{6,2},{3,7},{7,3},{8,12},{12,8},{9,1... | collective-permute-start | bytes 307208 | tf_op jit(solution)/shard_map/ppermute | solution.py:398
  9.0 3.3 %collective-permute-start.2 = (bf16[2,24,512]{2,1,0:T(8,128)(2,1)S(1)}, bf16[2,24,512]{2,1,0:T(8,128)(2,1)S(1)}, u32[]{:S(2)}, u32[]{:S(2)}) collective-permute-start(bf16[2,24,512]{2,1,0:T(8,128)(2,1)S(1)} %get-tuple-element.20), channel_id=1, source_target_pairs={{0,8},{8,0},{16,24},{24,16},{1,9},{9,1},{17,25},{25,17},{2,10},{10... | collective-permute-start | bytes 147464 | tf_op jit(solution)/shard_map/ppermute | solution.py:398
  12.3 5.4 %collective-permute-start.3 = (bf16[48,512]{1,0:T(8,128)(2,1)S(1)}, bf16[48,512]{1,0:T(8,128)(2,1)S(1)}, u32[]{:S(2)}, u32[]{:S(2)}) collective-permute-start(bf16[48,512]{1,0:T(8,128)(2,1)S(1)} %get-tuple-element.23), channel_id=1, source_target_pairs={{0,20},{4,16},{8,28},{12,24},{16,4},{20,0},{24,12},{28,8},{1,21},{... | collective-permute-start | bytes 147464 | tf_op jit(solution)/shard_map/ppermute | solution.py:408
  14.9 4.5 %collective-permute-start.4 = (bf16[48,512]{1,0:T(8,128)(2,1)S(1)}, bf16[48,512]{1,0:T(8,128)(2,1)S(1)}, u32[]{:S(2)}, u32[]{:S(2)}) collective-permute-start(bf16[48,512]{1,0:T(8,128)(2,1)S(1)} %get-tuple-element.22), channel_id=1, source_target_pairs={{0,16},{4,20},{8,12},{12,8},{16,0},{20,4},{24,28},{28,24},{1,17},{... | collective-permute-start | bytes 147464 | tf_op jit(solution)/shard_map/ppermute | solution.py:408
  15.0 4.3 %collective-permute-start.5 = (bf16[48,512]{1,0:T(8,128)(2,1)S(1)}, bf16[48,512]{1,0:T(8,128)(2,1)S(1)}, u32[]{:S(2)}, u32[]{:S(2)}) collective-permute-start(bf16[48,512]{1,0:T(8,128)(2,1)S(1)} %get-tuple-element.21), channel_id=1, source_target_pairs={{0,4},{4,0},{8,24},{12,28},{16,20},{20,16},{24,8},{28,12},{1,5},{5... | collective-permute-start | bytes 147464 | tf_op jit(solution)/shard_map/ppermute | solution.py:408

commit v5 on v4

--- a/solution.py
+++ b/solution.py
@@ -18,9 +18,9 @@
 
 
 def prepare_kernel(*refs, sections, group):
-    sources, (echo_out, chirp_out, pack_ref), scratch = refs[:7], refs[7:10], refs[10:]
+    sources, (echo_out, rim_ref, chirp_out, pack_ref), scratch = refs[:7], refs[7:11], refs[11:]
     coef_ref, start_ref, width_ref, steer_ref, order_ref, starts, sems = scratch
-    targets = (coef_ref, start_ref, width_ref, steer_ref, order_ref, chirp_out, echo_out)
+    targets = (echo_out, coef_ref, start_ref, width_ref, steer_ref, order_ref, chirp_out)
     loads = [
         pltpu.make_async_copy(source, target, sems.at[i])
         for i, (source, target) in enumerate(zip(sources, targets))
@@ -29,6 +29,7 @@
         load.start()
     for load in loads:
         load.wait()
+    rim_ref[...] = echo_out[:, :, : rim_ref.shape[2]]
     levels, _, sides, parts, taps, beams = coef_ref.shape
     tap = lax.broadcasted_iota(jnp.int32, (taps, beams), 0)
     row = 0
@@ -68,16 +69,17 @@
 
 def prepare(echo, chirp, coef, start, width, steer, order, sections, group):
     levels, _, sides, parts, taps, beams = coef.shape
-    sources = (coef, start, width, steer, order, chirp, echo)
+    sources = (echo, coef, start, width, steer, order, chirp)
     return pl.pallas_call(
         functools.partial(prepare_kernel, sections=sections, group=group),
         out_shape=(
             jax.ShapeDtypeStruct(echo.shape, BF16),
+            jax.ShapeDtypeStruct((*echo.shape[:2], chirp.shape[1]), BF16),
             jax.ShapeDtypeStruct(chirp.shape, BF16),
             jax.ShapeDtypeStruct((pack_rows(levels, sides, parts, taps, sections, group), beams), BF16),
         ),
         in_specs=[pl.BlockSpec(memory_space=pl.ANY)] * len(sources),
-        scratch_shapes=[pltpu.VMEM(x.shape, x.dtype) for x in sources[:5]]
+        scratch_shapes=[pltpu.VMEM(x.shape, x.dtype) for x in sources[1:6]]
         + [pltpu.VMEM((ceil_to(levels * sides, 16), beams), F32), pltpu.SemaphoreType.DMA((len(sources),))],
         compiler_params=pltpu.CompilerParams(vmem_limit_bytes=16 * 1024 * 1024),
         name="prepare",
@@ -283,18 +285,20 @@
 def finish_kernel(index_ref, early_ref, late_ref, halo_ref, table, keep_ref, give_ref, rows, even, odd, *, group):
     pulses = halo_ref.shape[0]
     span = late_ref.shape[1]
-    taps = rows.shape[1] - span
+    taps = halo_ref.shape[2]
+    ready = early_ref.shape[0]
+    chunk = 2 * early_ref.shape[2]
+    sections = ready + span // chunk
+    section = lax.rem(index_ref[0], sections)
+    has_next = index_ref[0] >= sections
     rows[:, :span] = late_ref[...]
     rows[:, span:] = jnp.zeros((2 * group, taps), F32)
     for p in range(pulses):
-        far = jnp.where(index_ref[1] != 0, halo_ref[p, :, :taps].astype(F32), 0.0)
+        far = jnp.where(has_next, halo_ref[p].astype(F32), 0.0)
         for c in range(2):
             rows[c * group + p : c * group + p + 1, span:] = far[c : c + 1]
     done = correlate(rows, even, odd, table, span // LANE, group)
-    ready = early_ref.shape[0]
-    chunk = 2 * early_ref.shape[2]
-    section = index_ref[0]
-    for s in range(ready + span // chunk):
+    for s in range(sections):
         stacked = early_ref[s] if s < ready else as_chunk(done, s - ready, chunk // LANE, group, pulses)
         slot = section ^ s
         far_chunk, other_core = slot // 2, slot % 2
@@ -408,16 +412,9 @@
     return lax.ppermute(value, ("section", "sub"), pairs)
 
 
-def from_next(value):
-    sections, others, count = lax.axis_size("section"), lax.axis_size("sub"), lax.axis_size("rng")
-    pairs = []
-    for s in range(sections):
-        for a in range(others):
-            first = (s * others + a) * count
-            pairs += [(first + i, first + i - 1) for i in range(1, count)]
-            if s:
-                pairs.append((first, first + count - 1))
-    return lax.ppermute(value, ("section", "sub", "rng"), pairs)
+def from_next(value, axis):
+    count = lax.axis_size(axis)
+    return lax.ppermute(value, axis, [(i, (i - 1) % count) for i in range(count)])
 
 
 def on_device(echoes, chirp, steer, pulse_order, band_coef, band_start, band_width):
@@ -431,15 +428,15 @@
     dims = (levels, sides, parts, taps, beams)
 
     echo = jnp.transpose(echoes[:, 0], (1, 0, 2))
-    halo = from_next(echo)
-    has_next = (lax.axis_index("rng") < lax.axis_size("rng") - 1).astype(jnp.int32)
-    echo, chirp, packed = prepare(
+    echo, rim, chirp, packed = prepare(
         echo, chirp, coef, band_start, band_width, weights, pulse_order, sections, group
     )
+    halo = from_next(rim, "rng")
+    has_next = (lax.axis_index("rng") < lax.axis_size("rng") - 1).astype(jnp.int32)
     if subs == 2:
         packed_partner = swap(packed, "sub", 1)
     early, late, table = begin_compression(echo, chirp, sections, group)
-    place = jnp.stack([section[0], has_next])
+    place = section + sections * has_next
     keep, give = finish_compression(place, early, late, halo, table, group)
     both = jnp.concatenate([keep, swap(give, "section", 1)], axis=1)
     far = lax.dynamic_index_in_dim(both, section[0] % 2, 0, keepdims=False)

time: 20.6 us -> 18.3 us (0.89)
  waiting for transfers between devices: 3.6 us -> 2.62 us
  Pallas kernels: 5.82 us -> 5.21 us
  starting transfers between devices: 10.8 us -> 10.2 us
    ppermute x2, starting transfers between devices: 5.47 us -> 1.59 us  [swap(): return lax.ppermute(value, axis, [(i, i ^ by) for i in range(count)])]
    ppermute x1, starting transfers between devices: 1.28 us -> 5.1 us  [from_next(): lax.ppermute(value, axis, [(i, (i - 1) % count) for i in range(count)])]
    ppermute x1, waiting for transfers between devices: 1.12 us -> 0.01 us  [from_next(): lax.ppermute(value, axis, [(i, (i - 1) % count) for i in range(count)])]
    pallas_call x1, Pallas kernels: 1.05 us -> 0.51 us  [finish_compression(): pl.pallas_call(functools.partial(finish_kernel, group=group), out_shape=[...]
    ppermute x3, starting transfers between devices: 4.1 us -> 3.55 us  [swap_by(): return lax.ppermute(value, ('section', 'sub'), pairs)]
    ppermute x2, waiting for transfers between devices: 0.88 us -> 1.21 us  [swap(): return lax.ppermute(value, axis, [(i, i ^ by) for i in range(count)])]
  transfers between devices with their start and end apart: 6 -> 6, of which waited for: 3 -> 3; matrix products, arithmetic and copies ran while one was open for 0% -> 0% of each run, Pallas kernels for 23% -> 16%
where the time goes in v5:
time: 18.3 us; the launch traced here: 18.2 us
  starting transfers between devices  10.2 us (56%)
  Pallas kernels  5.21 us (28%)
  waiting for transfers between devices  2.62 us (14%)
    ppermute x1, starting transfers between devices, from_next(): lax.ppermute(value, axis, [(i, (i - 1) % count) for i in range(count)])  5.1 us
    ppermute x3, starting transfers between devices, swap_by(): return lax.ppermute(value, ('section', 'sub'), pairs)  3.55 us
    ppermute x2, starting transfers between devices, swap(): return lax.ppermute(value, axis, [(i, i ^ by) for i in range(count)])  1.59 us
    ppermute x3, waiting for transfers between devices, swap_by(): return lax.ppermute(value, ('section', 'sub'), pairs)  1.41 us
    pallas_call x1, Pallas kernels, fold_operator(): pl.pallas_call(functools.partial(operator_kernel, dims=dims, sections=sec...  1.32 us
    pallas_call x1, Pallas kernels, prepare(): pl.pallas_call(functools.partial(prepare_kernel, sections=sections, group...  1.27 us
    ppermute x2, waiting for transfers between devices, swap(): return lax.ppermute(value, axis, [(i, i ^ by) for i in range(count)])  1.21 us
    pallas_call x1, Pallas kernels, form_image(): pl.pallas_call(functools.partial(image_kernel, group=group), out_shape=ja...  1.06 us
  transfers between devices with their start and end apart: 6, of which 3 were waited for; matrix products, arithmetic and copies ran while one was open for 0% of the time, Pallas kernels for 16%

profile of v5, /device:TPU:0, one launch (start us, length us, event | category | flops | bytes accessed | tf_op | source)
XLA Modules:
  0.0 18.2 jit_solution(688721530565667700)
XLA Ops:
  0.0 1.3 %prepare.1 = (bf16[6,2,4096]{2,1,0:T(2,128)(2,1)S(1)}, bf16[6,2,2048]{2,1,0:T(2,128)(2,1)S(1)}, bf16[2,2048]{1,0:T(2,128)(2,1)S(1)}, bf16[400,128]{1,0:T(8,128)(2,1)S(1)}) custom-call(bf16[6,2,4096]{2,1,0:T(2,128)(2,1)} %bitcast.16, bf16[5,1,2,2,16,128]{5,4,3,2,1,0:T(8,128)(2,1)} %bitcast.17, s32[5,1,2,128]{3,2,1,0:T(2,128)} %refs_2_.1, ...), custom_call_target="tpu_custom_call" | custom-call | tf_op jit(solution)/shard_map/prepare/pallas_call | solution.py:73
  1.3 5.1 %collective-permute-start.1 = (bf16[6,2,2048]{2,1,0:T(2,128)(2,1)S(1)}, bf16[6,2,2048]{2,1,0:T(2,128)(2,1)S(1)}, u32[]{:S(2)}, u32[]{:S(2)}) collective-permute-start(bf16[6,2,2048]{2,1,0:T(2,128)(2,1)S(1)} %get-tuple-element.19), channel_id=1, source_target_pairs={{0,3},{1,0},{2,1},{3,2},{4,7},{5,4},{6,5},{7,6},{8,11},{9,8},{10,9... | collective-permute-start | bytes 147464 | tf_op jit(solution)/shard_map/ppermute | solution.py:417
  6.4 1.5 %collective-permute-start = (bf16[400,128]{1,0:T(8,128)(2,1)S(1)}, bf16[400,128]{1,0:T(8,128)(2,1)S(1)}, u32[]{:S(2)}, u32[]{:S(2)}) collective-permute-start(bf16[400,128]{1,0:T(8,128)(2,1)S(1)} %get-tuple-element.14.own_ref), channel_id=1, source_target_pairs={{0,4},{4,0},{1,5},{5,1},{2,6},{6,2},{3,7},{7,3},{8,12},{12,8},{9,1... | collective-permute-start | bytes 307208 | tf_op jit(solution)/shard_map/ppermute | solution.py:402
  7.9 1.0 %begin_compression.1 = (bf16[2,24,512]{2,1,0:T(8,128)(2,1)S(1)}, f32[16,2048]{1,0:T(8,128)S(1)}, bf16[4352,256]{1,0:T(8,128)(2,1)S(1)}) custom-call(bf16[6,2,4096]{2,1,0:T(2,128)(2,1)S(1)} %get-tuple-element.15.echo_ref, bf16[2,2048]{1,0:T(2,128)(2,1)S(1)} %get-tuple-element.16.chirp_ref), custom_call_target="tpu_custom_call" | custom-call | tf_op jit(solution)/shard_map/begin_compression/pallas_call | solution.py:329
  9.0 0.0 collective-permute-done.1.halo_ref
  9.0 0.5 %finish_compression.1 = (bf16[2,24,512]{2,1,0:T(8,128)(2,1)S(1)}, bf16[2,24,512]{2,1,0:T(8,128)(2,1)S(1)}) custom-call(s32[1]{0:T(128)S(6)} %add.15.index_ref, bf16[2,24,512]{2,1,0:T(8,128)(2,1)S(1)} %get-tuple-element.17.early_ref, f32[16,2048]{1,0:T(8,128)S(1)} %get-tuple-element.18.late_ref, bf16[6,2,2048]{2,1,0:T(2,128)(2,1)S(1)} %collective-permute-done.1.halo_ref, ...), custom_call_target="tpu_custom_call" | custom-call | tf_op jit(solution)/shard_map/finish_compression/pallas_call | solution.py:344
  9.5 0.1 collective-permute-start.2
  9.6 1.2 %collective-permute-done.2 = bf16[2,24,512]{2,1,0:T(8,128)(2,1)S(1)} collective-permute-done((bf16[2,24,512]{2,1,0:T(8,128)(2,1)S(1)}, bf16[2,24,512]{2,1,0:T(8,128)(2,1)S(1)}, u32[]{:S(2)}, u32[]{:S(2)}) %collective-permute-start.2) | collective-permute-done | bytes 49184 | tf_op jit(solution)/shard_map/ppermute | solution.py:402
  10.8 1.7 %collective-permute-start.3 = (bf16[48,512]{1,0:T(8,128)(2,1)S(1)}, bf16[48,512]{1,0:T(8,128)(2,1)S(1)}, u32[]{:S(2)}, u32[]{:S(2)}) collective-permute-start(bf16[48,512]{1,0:T(8,128)(2,1)S(1)} %get-tuple-element.25), channel_id=1, source_target_pairs={{0,20},{4,16},{8,28},{12,24},{16,4},{20,0},{24,12},{28,8},{1,21},{... | collective-permute-start | bytes 147464 | tf_op jit(solution)/shard_map/ppermute | solution.py:412
  12.5 0.5 %collective-permute-start.4 = (bf16[48,512]{1,0:T(8,128)(2,1)S(1)}, bf16[48,512]{1,0:T(8,128)(2,1)S(1)}, u32[]{:S(2)}, u32[]{:S(2)}) collective-permute-start(bf16[48,512]{1,0:T(8,128)(2,1)S(1)} %get-tuple-element.24), channel_id=1, source_target_pairs={{0,16},{4,20},{8,12},{12,8},{16,0},{20,4},{24,28},{28,24},{1,17},{... | collective-permute-start | bytes 147464 | tf_op jit(solution)/shard_map/ppermute | solution.py:412
  13.0 1.3 %collective-permute-start.5 = (bf16[48,512]{1,0:T(8,128)(2,1)S(1)}, bf16[48,512]{1,0:T(8,128)(2,1)S(1)}, u32[]{:S(2)}, u32[]{:S(2)}) collective-permute-start(bf16[48,512]{1,0:T(8,128)(2,1)S(1)} %get-tuple-element.23), channel_id=1, source_target_pairs={{0,4},{4,0},{8,24},{12,28},{16,20},{20,16},{24,8},{28,12},{1,5},{5... | collective-permute-start | bytes 147464 | tf_op jit(solution)/shard_map/ppermute | solution.py:412
  14.4 0.0 collective-permute-done.partner_ref
  14.4 1.3 %fold_operator.1.operator_ref = bf16[2,256,256]{2,1,0:T(8,128)(2,1)S(1)} custom-call(s32[1]{0:T(128)} %bitcast.index_ref, bf16[400,128]{1,0:T(8,128)(2,1)S(1)} %get-tuple-element.14.own_ref, bf16[400,128]{1,0:T(8,128)(2,1)S(1)} %collective-permute-done.partner_ref), custom_call_target="tpu_custom_call" | custom-call | tf_op jit(solution)/shard_map/fold_operator/pallas_call | solution.py:190
  15.7 0.2 %collective-permute-done.3.refs_0_ = bf16[48,512]{1,0:T(8,128)(2,1)S(1)} collective-permute-done((bf16[48,512]{1,0:T(8,128)(2,1)S(1)}, bf16[48,512]{1,0:T(8,128)(2,1)S(1)}, u32[]{:S(2)}, u32[]{:S(2)}) %collective-permute-start.3) | collective-permute-done | bytes 49184 | tf_op jit(solution)/shard_map/ppermute | solution.py:412
  15.9 1.1 %collective-permute-done.4.refs_1_ = bf16[48,512]{1,0:T(8,128)(2,1)S(1)} collective-permute-done((bf16[48,512]{1,0:T(8,128)(2,1)S(1)}, bf16[48,512]{1,0:T(8,128)(2,1)S(1)}, u32[]{:S(2)}, u32[]{:S(2)}) %collective-permute-start.4) | collective-permute-done | bytes 49184 | tf_op jit(solution)/shard_map/ppermute | solution.py:412
  17.1 0.0 collective-permute-done.5.refs_2_
  17.1 1.1 %form_image.1 = bf16[256,1024]{1,0:T(8,128)(2,1)} custom-call(s32[1]{0:T(128)} %bitcast.index_ref, bf16[2,256,256]{2,1,0:T(8,128)(2,1)S(1)} %fold_operator.1.operator_ref, bf16[2,48,512]{2,1,0:T(8,128)(2,1)S(1)} %constant_dynamic-update-slice_fusion.both_ref, bf16[48,512]{1,0:T(8,128)(2,1)S(1)} %collective-permute-done.3.refs_0_, ...), custom_call_target="tpu_custom_call" | custom-call | tf_op jit(solution)/shard_map/form_image/pallas_call | solution.py:385
  (3 shorter events, 0.0 us)
Async XLA Ops:
  1.3 7.7 %collective-permute-start.1 = (bf16[6,2,2048]{2,1,0:T(2,128)(2,1)S(1)}, bf16[6,2,2048]{2,1,0:T(2,128)(2,1)S(1)}, u32[]{:S(2)}, u32[]{:S(2)}) collective-permute-start(bf16[6,2,2048]{2,1,0:T(2,128)(2,1)S(1)} %get-tuple-element.19), channel_id=1, source_target_pairs={{0,3},{1,0},{2,1},{3,2},{4,7},{5,4},{6,5},{7,6},{8,11},{9,8},{10,9... | collective-permute-start | bytes 147464 | tf_op jit(solution)/shard_map/ppermute | solution.py:417
  6.4 8.0 %collective-permute-start = (bf16[400,128]{1,0:T(8,128)(2,1)S(1)}, bf16[400,128]{1,0:T(8,128)(2,1)S(1)}, u32[]{:S(2)}, u32[]{:S(2)}) collective-permute-start(bf16[400,128]{1,0:T(8,128)(2,1)S(1)} %get-tuple-element.14.own_ref), channel_id=1, source_target_pairs={{0,4},{4,0},{1,5},{5,1},{2,6},{6,2},{3,7},{7,3},{8,12},{12,8},{9,1... | collective-permute-start | bytes 307208 | tf_op jit(solution)/shard_map/ppermute | solution.py:402
  9.5 1.3 %collective-permute-start.2 = (bf16[2,24,512]{2,1,0:T(8,128)(2,1)S(1)}, bf16[2,24,512]{2,1,0:T(8,128)(2,1)S(1)}, u32[]{:S(2)}, u32[]{:S(2)}) collective-permute-start(bf16[2,24,512]{2,1,0:T(8,128)(2,1)S(1)} %get-tuple-element.22), channel_id=1, source_target_pairs={{0,8},{8,0},{16,24},{24,16},{1,9},{9,1},{17,25},{25,17},{2,10},{10... | collective-permute-start | bytes 147464 | tf_op jit(solution)/shard_map/ppermute | solution.py:402
  10.8 5.1 %collective-permute-start.3 = (bf16[48,512]{1,0:T(8,128)(2,1)S(1)}, bf16[48,512]{1,0:T(8,128)(2,1)S(1)}, u32[]{:S(2)}, u32[]{:S(2)}) collective-permute-start(bf16[48,512]{1,0:T(8,128)(2,1)S(1)} %get-tuple-element.25), channel_id=1, source_target_pairs={{0,20},{4,16},{8,28},{12,24},{16,4},{20,0},{24,12},{28,8},{1,21},{... | collective-permute-start | bytes 147464 | tf_op jit(solution)/shard_map/ppermute | solution.py:412
  12.5 4.6 %collective-permute-start.4 = (bf16[48,512]{1,0:T(8,128)(2,1)S(1)}, bf16[48,512]{1,0:T(8,128)(2,1)S(1)}, u32[]{:S(2)}, u32[]{:S(2)}) collective-permute-start(bf16[48,512]{1,0:T(8,128)(2,1)S(1)} %get-tuple-element.24), channel_id=1, source_target_pairs={{0,16},{4,20},{8,12},{12,8},{16,0},{20,4},{24,28},{28,24},{1,17},{... | collective-permute-start | bytes 147464 | tf_op jit(solution)/shard_map/ppermute | solution.py:412
  13.0 4.1 %collective-permute-start.5 = (bf16[48,512]{1,0:T(8,128)(2,1)S(1)}, bf16[48,512]{1,0:T(8,128)(2,1)S(1)}, u32[]{:S(2)}, u32[]{:S(2)}) collective-permute-start(bf16[48,512]{1,0:T(8,128)(2,1)S(1)} %get-tuple-element.23), channel_id=1, source_target_pairs={{0,4},{4,0},{8,24},{12,28},{16,20},{20,16},{24,8},{28,12},{1,5},{5... | collective-permute-start | bytes 147464 | tf_op jit(solution)/shard_map/ppermute | solution.py:412

commit v6 on v5

--- a/solution.py
+++ b/solution.py
@@ -18,7 +18,7 @@
 
 
 def prepare_kernel(*refs, sections, group):
-    sources, (echo_out, rim_ref, chirp_out, pack_ref), scratch = refs[:7], refs[7:11], refs[11:]
+    sources, (echo_out, chirp_out, pack_ref), scratch = refs[:7], refs[7:10], refs[10:]
     coef_ref, start_ref, width_ref, steer_ref, order_ref, starts, sems = scratch
     targets = (echo_out, coef_ref, start_ref, width_ref, steer_ref, order_ref, chirp_out)
     loads = [
@@ -29,7 +29,6 @@
         load.start()
     for load in loads:
         load.wait()
-    rim_ref[...] = echo_out[:, :, : rim_ref.shape[2]]
     levels, _, sides, parts, taps, beams = coef_ref.shape
     tap = lax.broadcasted_iota(jnp.int32, (taps, beams), 0)
     row = 0
@@ -74,7 +73,6 @@
         functools.partial(prepare_kernel, sections=sections, group=group),
         out_shape=(
             jax.ShapeDtypeStruct(echo.shape, BF16),
-            jax.ShapeDtypeStruct((*echo.shape[:2], chirp.shape[1]), BF16),
             jax.ShapeDtypeStruct(chirp.shape, BF16),
             jax.ShapeDtypeStruct((pack_rows(levels, sides, parts, taps, sections, group), beams), BF16),
         ),
@@ -285,7 +283,7 @@
 def finish_kernel(index_ref, early_ref, late_ref, halo_ref, table, keep_ref, give_ref, rows, even, odd, *, group):
     pulses = halo_ref.shape[0]
     span = late_ref.shape[1]
-    taps = halo_ref.shape[2]
+    taps = rows.shape[1] - span
     ready = early_ref.shape[0]
     chunk = 2 * early_ref.shape[2]
     sections = ready + span // chunk
@@ -294,7 +292,7 @@
     rows[:, :span] = late_ref[...]
     rows[:, span:] = jnp.zeros((2 * group, taps), F32)
     for p in range(pulses):
-        far = jnp.where(has_next, halo_ref[p].astype(F32), 0.0)
+        far = jnp.where(has_next, halo_ref[p, :, :taps].astype(F32), 0.0)
         for c in range(2):
             rows[c * group + p : c * group + p + 1, span:] = far[c : c + 1]
     done = correlate(rows, even, odd, table, span // LANE, group)
@@ -428,10 +426,10 @@
     dims = (levels, sides, parts, taps, beams)
 
     echo = jnp.transpose(echoes[:, 0], (1, 0, 2))
-    echo, rim, chirp, packed = prepare(
+    halo = from_next(echo, "rng")
+    echo, chirp, packed = prepare(
         echo, chirp, coef, band_start, band_width, weights, pulse_order, sections, group
     )
-    halo = from_next(rim, "rng")
     has_next = (lax.axis_index("rng") < lax.axis_size("rng") - 1).astype(jnp.int32)
     if subs == 2:
         packed_partner = swap(packed, "sub", 1)

time: 18.3 us -> 18.2 us (level)
  transfers between devices with their start and end apart: 6 -> 6, of which waited for: 3 -> 4; matrix products, arithmetic and copies ran while one was open for 0% -> 0% of each run, Pallas kernels for 16% -> 23%
where the time goes in v6:
time: 18.2 us; the launch traced here: 18 us
  starting transfers between devices  10.3 us (57%)
  Pallas kernels  5.2 us (29%)
  waiting for transfers between devices  2.45 us (13%)
    ppermute x1, starting transfers between devices, from_next(): lax.ppermute(value, axis, [(i, (i - 1) % count) for i in range(count)])  5.05 us
    ppermute x3, starting transfers between devices, swap_by(): return lax.ppermute(value, ('section', 'sub'), pairs)  3.55 us
    ppermute x2, starting transfers between devices, swap(): return lax.ppermute(value, axis, [(i, i ^ by) for i in range(count)])  1.66 us
    pallas_call x1, Pallas kernels, fold_operator(): pl.pallas_call(functools.partial(operator_kernel, dims=dims, sections=sec...  1.32 us
    pallas_call x1, Pallas kernels, prepare(): pl.pallas_call(functools.partial(prepare_kernel, sections=sections, group...  1.27 us
    ppermute x3, waiting for transfers between devices, swap_by(): return lax.ppermute(value, ('section', 'sub'), pairs)  1.24 us
    ppermute x2, waiting for transfers between devices, swap(): return lax.ppermute(value, axis, [(i, i ^ by) for i in range(count)])  1.21 us
    pallas_call x1, Pallas kernels, form_image(): pl.pallas_call(functools.partial(image_kernel, group=group), out_shape=ja...  1.06 us
  transfers between devices with their start and end apart: 6, of which 4 were waited for; matrix products, arithmetic and copies ran while one was open for 0% of the time, Pallas kernels for 23%

profile of v6, /device:TPU:0, one launch (start us, length us, event | category | flops | bytes accessed | tf_op | source)
XLA Modules:
  0.0 18.0 jit_solution(9340069338685786565)
XLA Ops:
  0.0 5.0 %collective-permute-start.1 = (bf16[6,2,4096]{2,1,0:T(2,128)(2,1)}, bf16[6,2,4096]{2,1,0:T(2,128)(2,1)S(1)}, u32[]{:S(2)}, u32[]{:S(2)}) collective-permute-start(bf16[6,2,4096]{2,1,0:T(2,128)(2,1)} %bitcast.16), channel_id=1, source_target_pairs={{0,3},{1,0},{2,1},{3,2},{4,7},{5,4},{6,5},{7,6},{8,11},{9,8},{10,9... | collective-permute-start | bytes 294920 | tf_op jit(solution)/shard_map/ppermute | solution.py:415
  5.0 1.3 %prepare.1 = (bf16[6,2,4096]{2,1,0:T(2,128)(2,1)S(1)}, bf16[2,2048]{1,0:T(2,128)(2,1)S(1)}, bf16[400,128]{1,0:T(8,128)(2,1)S(1)}) custom-call(bf16[6,2,4096]{2,1,0:T(2,128)(2,1)} %bitcast.17, bf16[5,1,2,2,16,128]{5,4,3,2,1,0:T(8,128)(2,1)} %bitcast.18, s32[5,1,2,128]{3,2,1,0:T(2,128)} %refs_2_.1, s32[5,1,2,128]{3,2,1,0:T(2,128)} %refs_3_.1, ...), custom_call_target="tpu_custom_call" | custom-call | tf_op jit(solution)/shard_map/prepare/pallas_call | solution.py:72
  6.3 1.6 %collective-permute-start = (bf16[400,128]{1,0:T(8,128)(2,1)S(1)}, bf16[400,128]{1,0:T(8,128)(2,1)S(1)}, u32[]{:S(2)}, u32[]{:S(2)}) collective-permute-start(bf16[400,128]{1,0:T(8,128)(2,1)S(1)} %get-tuple-element.13.own_ref), channel_id=1, source_target_pairs={{0,4},{4,0},{1,5},{5,1},{2,6},{6,2},{3,7},{7,3},{8,12},{12,8},{9,1... | collective-permute-start | bytes 307208 | tf_op jit(solution)/shard_map/ppermute | solution.py:400
  7.9 1.0 %begin_compression.1 = (bf16[2,24,512]{2,1,0:T(8,128)(2,1)S(1)}, f32[16,2048]{1,0:T(8,128)S(1)}, bf16[4352,256]{1,0:T(8,128)(2,1)S(1)}) custom-call(bf16[6,2,4096]{2,1,0:T(2,128)(2,1)S(1)} %get-tuple-element.14.echo_ref, bf16[2,2048]{1,0:T(2,128)(2,1)S(1)} %get-tuple-element.15.chirp_ref), custom_call_target="tpu_custom_call" | custom-call | tf_op jit(solution)/shard_map/begin_compression/pallas_call | solution.py:327
  9.0 0.0 collective-permute-done.1.halo_ref
  9.0 0.5 %finish_compression.1 = (bf16[2,24,512]{2,1,0:T(8,128)(2,1)S(1)}, bf16[2,24,512]{2,1,0:T(8,128)(2,1)S(1)}) custom-call(s32[1]{0:T(128)S(6)} %add.15.index_ref, bf16[2,24,512]{2,1,0:T(8,128)(2,1)S(1)} %get-tuple-element.16.early_ref, f32[16,2048]{1,0:T(8,128)S(1)} %get-tuple-element.17.late_ref, bf16[6,2,4096]{2,1,0:T(2,128)(2,1)S(1)} %collective-permute-done.1.halo_ref, ...), custom_call_target="tpu_custom_call" | custom-call | tf_op jit(solution)/shard_map/finish_compression/pallas_call | solution.py:342
  9.5 0.1 collective-permute-start.2
  9.6 1.2 %collective-permute-done.2 = bf16[2,24,512]{2,1,0:T(8,128)(2,1)S(1)} collective-permute-done((bf16[2,24,512]{2,1,0:T(8,128)(2,1)S(1)}, bf16[2,24,512]{2,1,0:T(8,128)(2,1)S(1)}, u32[]{:S(2)}, u32[]{:S(2)}) %collective-permute-start.2) | collective-permute-done | bytes 49184 | tf_op jit(solution)/shard_map/ppermute | solution.py:400
  10.8 1.5 %collective-permute-start.3 = (bf16[48,512]{1,0:T(8,128)(2,1)S(1)}, bf16[48,512]{1,0:T(8,128)(2,1)S(1)}, u32[]{:S(2)}, u32[]{:S(2)}) collective-permute-start(bf16[48,512]{1,0:T(8,128)(2,1)S(1)} %get-tuple-element.23), channel_id=1, source_target_pairs={{0,20},{4,16},{8,28},{12,24},{16,4},{20,0},{24,12},{28,8},{1,21},{... | collective-permute-start | bytes 147464 | tf_op jit(solution)/shard_map/ppermute | solution.py:410
  12.3 0.5 %collective-permute-start.4 = (bf16[48,512]{1,0:T(8,128)(2,1)S(1)}, bf16[48,512]{1,0:T(8,128)(2,1)S(1)}, u32[]{:S(2)}, u32[]{:S(2)}) collective-permute-start(bf16[48,512]{1,0:T(8,128)(2,1)S(1)} %get-tuple-element.22), channel_id=1, source_target_pairs={{0,16},{4,20},{8,12},{12,8},{16,0},{20,4},{24,28},{28,24},{1,17},{... | collective-permute-start | bytes 147464 | tf_op jit(solution)/shard_map/ppermute | solution.py:410
  12.9 1.5 %collective-permute-start.5 = (bf16[48,512]{1,0:T(8,128)(2,1)S(1)}, bf16[48,512]{1,0:T(8,128)(2,1)S(1)}, u32[]{:S(2)}, u32[]{:S(2)}) collective-permute-start(bf16[48,512]{1,0:T(8,128)(2,1)S(1)} %get-tuple-element.21), channel_id=1, source_target_pairs={{0,4},{4,0},{8,24},{12,28},{16,20},{20,16},{24,8},{28,12},{1,5},{5... | collective-permute-start | bytes 147464 | tf_op jit(solution)/shard_map/ppermute | solution.py:410
  14.4 0.0 collective-permute-done.partner_ref
  14.4 1.3 %fold_operator.1.operator_ref = bf16[2,256,256]{2,1,0:T(8,128)(2,1)S(1)} custom-call(s32[1]{0:T(128)} %bitcast.index_ref, bf16[400,128]{1,0:T(8,128)(2,1)S(1)} %get-tuple-element.13.own_ref, bf16[400,128]{1,0:T(8,128)(2,1)S(1)} %collective-permute-done.partner_ref), custom_call_target="tpu_custom_call" | custom-call | tf_op jit(solution)/shard_map/fold_operator/pallas_call | solution.py:188
  15.7 0.2 %collective-permute-done.3.refs_0_ = bf16[48,512]{1,0:T(8,128)(2,1)S(1)} collective-permute-done((bf16[48,512]{1,0:T(8,128)(2,1)S(1)}, bf16[48,512]{1,0:T(8,128)(2,1)S(1)}, u32[]{:S(2)}, u32[]{:S(2)}) %collective-permute-start.3) | collective-permute-done | bytes 49184 | tf_op jit(solution)/shard_map/ppermute | solution.py:410
  15.9 0.9 %collective-permute-done.4.refs_1_ = bf16[48,512]{1,0:T(8,128)(2,1)S(1)} collective-permute-done((bf16[48,512]{1,0:T(8,128)(2,1)S(1)}, bf16[48,512]{1,0:T(8,128)(2,1)S(1)}, u32[]{:S(2)}, u32[]{:S(2)}) %collective-permute-start.4) | collective-permute-done | bytes 49184 | tf_op jit(solution)/shard_map/ppermute | solution.py:410
  16.8 0.2 collective-permute-done.5.refs_2_
  16.9 1.1 %form_image.1 = bf16[256,1024]{1,0:T(8,128)(2,1)} custom-call(s32[1]{0:T(128)} %bitcast.index_ref, bf16[2,256,256]{2,1,0:T(8,128)(2,1)S(1)} %fold_operator.1.operator_ref, bf16[2,48,512]{2,1,0:T(8,128)(2,1)S(1)} %constant_dynamic-update-slice_fusion.both_ref, bf16[48,512]{1,0:T(8,128)(2,1)S(1)} %collective-permute-done.3.refs_0_, ...), custom_call_target="tpu_custom_call" | custom-call | tf_op jit(solution)/shard_map/form_image/pallas_call | solution.py:383
  (3 shorter events, 0.0 us)
Async XLA Ops:
  0.0 9.0 %collective-permute-start.1 = (bf16[6,2,4096]{2,1,0:T(2,128)(2,1)}, bf16[6,2,4096]{2,1,0:T(2,128)(2,1)S(1)}, u32[]{:S(2)}, u32[]{:S(2)}) collective-permute-start(bf16[6,2,4096]{2,1,0:T(2,128)(2,1)} %bitcast.16), channel_id=1, source_target_pairs={{0,3},{1,0},{2,1},{3,2},{4,7},{5,4},{6,5},{7,6},{8,11},{9,8},{10,9... | collective-permute-start | bytes 294920 | tf_op jit(solution)/shard_map/ppermute | solution.py:415
  6.3 8.0 %collective-permute-start = (bf16[400,128]{1,0:T(8,128)(2,1)S(1)}, bf16[400,128]{1,0:T(8,128)(2,1)S(1)}, u32[]{:S(2)}, u32[]{:S(2)}) collective-permute-start(bf16[400,128]{1,0:T(8,128)(2,1)S(1)} %get-tuple-element.13.own_ref), channel_id=1, source_target_pairs={{0,4},{4,0},{1,5},{5,1},{2,6},{6,2},{3,7},{7,3},{8,12},{12,8},{9,1... | collective-permute-start | bytes 307208 | tf_op jit(solution)/shard_map/ppermute | solution.py:400
  9.5 1.3 %collective-permute-start.2 = (bf16[2,24,512]{2,1,0:T(8,128)(2,1)S(1)}, bf16[2,24,512]{2,1,0:T(8,128)(2,1)S(1)}, u32[]{:S(2)}, u32[]{:S(2)}) collective-permute-start(bf16[2,24,512]{2,1,0:T(8,128)(2,1)S(1)} %get-tuple-element.20), channel_id=1, source_target_pairs={{0,8},{8,0},{16,24},{24,16},{1,9},{9,1},{17,25},{25,17},{2,10},{10... | collective-permute-start | bytes 147464 | tf_op jit(solution)/shard_map/ppermute | solution.py:400
  10.8 5.1 %collective-permute-start.3 = (bf16[48,512]{1,0:T(8,128)(2,1)S(1)}, bf16[48,512]{1,0:T(8,128)(2,1)S(1)}, u32[]{:S(2)}, u32[]{:S(2)}) collective-permute-start(bf16[48,512]{1,0:T(8,128)(2,1)S(1)} %get-tuple-element.23), channel_id=1, source_target_pairs={{0,20},{4,16},{8,28},{12,24},{16,4},{20,0},{24,12},{28,8},{1,21},{... | collective-permute-start | bytes 147464 | tf_op jit(solution)/shard_map/ppermute | solution.py:410
  12.3 4.5 %collective-permute-start.4 = (bf16[48,512]{1,0:T(8,128)(2,1)S(1)}, bf16[48,512]{1,0:T(8,128)(2,1)S(1)}, u32[]{:S(2)}, u32[]{:S(2)}) collective-permute-start(bf16[48,512]{1,0:T(8,128)(2,1)S(1)} %get-tuple-element.22), channel_id=1, source_target_pairs={{0,16},{4,20},{8,12},{12,8},{16,0},{20,4},{24,28},{28,24},{1,17},{... | collective-permute-start | bytes 147464 | tf_op jit(solution)/shard_map/ppermute | solution.py:410
  12.9 4.1 %collective-permute-start.5 = (bf16[48,512]{1,0:T(8,128)(2,1)S(1)}, bf16[48,512]{1,0:T(8,128)(2,1)S(1)}, u32[]{:S(2)}, u32[]{:S(2)}) collective-permute-start(bf16[48,512]{1,0:T(8,128)(2,1)S(1)} %get-tuple-element.21), channel_id=1, source_target_pairs={{0,4},{4,0},{8,24},{12,28},{16,20},{20,16},{24,8},{28,12},{1,5},{5... | collective-permute-start | bytes 147464 | tf_op jit(solution)/shard_map/ppermute | solution.py:410

commit v7 on v6

--- a/solution.py
+++ b/solution.py
@@ -287,12 +287,11 @@
     ready = early_ref.shape[0]
     chunk = 2 * early_ref.shape[2]
     sections = ready + span // chunk
-    section = lax.rem(index_ref[0], sections)
-    has_next = index_ref[0] >= sections
+    section = index_ref[0]
     rows[:, :span] = late_ref[...]
     rows[:, span:] = jnp.zeros((2 * group, taps), F32)
     for p in range(pulses):
-        far = jnp.where(has_next, halo_ref[p, :, :taps].astype(F32), 0.0)
+        far = halo_ref[p, :, :taps].astype(F32)
         for c in range(2):
             rows[c * group + p : c * group + p + 1, span:] = far[c : c + 1]
     done = correlate(rows, even, odd, table, span // LANE, group)
@@ -337,7 +336,7 @@
     )(echo, chirp)
 
 
-def finish_compression(place, early, late, halo, table, group):
+def finish_compression(section, early, late, halo, table, group):
     blocks = late.shape[1] // LANE + table.shape[0] // (2 * LANE) - 1
     return pl.pallas_call(
         functools.partial(finish_kernel, group=group),
@@ -346,7 +345,7 @@
         scratch_shapes=row_scratch(blocks, group),
         compiler_params=pltpu.CompilerParams(vmem_limit_bytes=24 * 1024 * 1024),
         name="finish_compression",
-    )(place, early, late, halo, table)
+    )(section, early, late, halo, table)
 
 
 def image_kernel(index_ref, operator_ref, both_ref, *refs, group):
@@ -411,8 +410,7 @@
 
 
 def from_next(value, axis):
-    count = lax.axis_size(axis)
-    return lax.ppermute(value, axis, [(i, (i - 1) % count) for i in range(count)])
+    return lax.ppermute(value, axis, [(i, i - 1) for i in range(1, lax.axis_size(axis))])
 
 
 def on_device(echoes, chirp, steer, pulse_order, band_coef, band_start, band_width):
@@ -430,12 +428,10 @@
     echo, chirp, packed = prepare(
         echo, chirp, coef, band_start, band_width, weights, pulse_order, sections, group
     )
-    has_next = (lax.axis_index("rng") < lax.axis_size("rng") - 1).astype(jnp.int32)
     if subs == 2:
         packed_partner = swap(packed, "sub", 1)
     early, late, table = begin_compression(echo, chirp, sections, group)
-    place = section + sections * has_next
-    keep, give = finish_compression(place, early, late, halo, table, group)
+    keep, give = finish_compression(section, early, late, halo, table, group)
     both = jnp.concatenate([keep, swap(give, "section", 1)], axis=1)
     far = lax.dynamic_index_in_dim(both, section[0] % 2, 0, keepdims=False)
     if subs != 2:

time: 18.2 us -> 18.4 us (1.011)
  waiting for transfers between devices: 2.45 us -> 4.96 us
  starting transfers between devices: 10.3 us -> 7.94 us
    ppermute x1, starting transfers between devices: 5.05 us -> 1.28 us  [from_next(): lax.ppermute(value, axis, [(i, i - 1) for i in range(1, lax.axis_size(axi...]
    ppermute x2, starting transfers between devices: 1.66 us -> 3.1 us  [swap(): return lax.ppermute(value, axis, [(i, i ^ by) for i in range(count)])]
    ppermute x1, waiting for transfers between devices: 0.01 us -> 1.27 us  [from_next(): lax.ppermute(value, axis, [(i, i - 1) for i in range(1, lax.axis_size(axi...]
    ppermute x3, waiting for transfers between devices: 1.24 us -> 2.49 us  [swap_by(): return lax.ppermute(value, ('section', 'sub'), pairs)]
  transfers between devices with their start and end apart: 6 -> 6, of which waited for: 4 -> 5; matrix products, arithmetic and copies ran while one was open for 0% -> 0% of each run, Pallas kernels for 23% -> 23%
where the time goes in v7:
time: 18.4 us; the launch traced here: 18.2 us
  starting transfers between devices  7.94 us (43%)
  Pallas kernels  5.22 us (28%)
  waiting for transfers between devices  4.96 us (27%)
    ppermute x3, starting transfers between devices, swap_by(): return lax.ppermute(value, ('section', 'sub'), pairs)  3.55 us
    ppermute x2, starting transfers between devices, swap(): return lax.ppermute(value, axis, [(i, i ^ by) for i in range(count)])  3.1 us
    ppermute x3, waiting for transfers between devices, swap_by(): return lax.ppermute(value, ('section', 'sub'), pairs)  2.49 us
    pallas_call x1, Pallas kernels, fold_operator(): pl.pallas_call(functools.partial(operator_kernel, dims=dims, sections=sec...  1.32 us
    ppermute x1, starting transfers between devices, from_next(): lax.ppermute(value, axis, [(i, i - 1) for i in range(1, lax.axis_size(axi...  1.28 us
    pallas_call x1, Pallas kernels, prepare(): pl.pallas_call(functools.partial(prepare_kernel, sections=sections, group...  1.27 us
    ppermute x1, waiting for transfers between devices, from_next(): lax.ppermute(value, axis, [(i, i - 1) for i in range(1, lax.axis_size(axi...  1.27 us
    ppermute x2, waiting for transfers between devices, swap(): return lax.ppermute(value, axis, [(i, i ^ by) for i in range(count)])  1.21 us
  transfers between devices with their start and end apart: 6, of which 5 were waited for; matrix products, arithmetic and copies ran while one was open for 0% of the time, Pallas kernels for 23%

profile of v7, /device:TPU:0, one launch (start us, length us, event | category | flops | bytes accessed | tf_op | source)
XLA Modules:
  0.0 18.2 jit_solution(13447042778284944094)
XLA Ops:
  0.0 1.3 %collective-permute-start.1 = (bf16[6,2,4096]{2,1,0:T(2,128)(2,1)}, bf16[6,2,4096]{2,1,0:T(2,128)(2,1)S(1)}, u32[]{:S(2)}, u32[]{:S(2)}) collective-permute-start(bf16[6,2,4096]{2,1,0:T(2,128)(2,1)} %bitcast.15), channel_id=1, source_target_pairs={{1,0},{2,1},{3,2},{5,4},{6,5},{7,6},{9,8},{10,9},{11,10},{13,12},{... | collective-permute-start | bytes 294920 | tf_op jit(solution)/shard_map/ppermute | solution.py:413
  1.3 1.3 %prepare.1 = (bf16[6,2,4096]{2,1,0:T(2,128)(2,1)S(1)}, bf16[2,2048]{1,0:T(2,128)(2,1)S(1)}, bf16[400,128]{1,0:T(8,128)(2,1)S(1)}) custom-call(bf16[6,2,4096]{2,1,0:T(2,128)(2,1)} %bitcast.16, bf16[5,1,2,2,16,128]{5,4,3,2,1,0:T(8,128)(2,1)} %bitcast.17, s32[5,1,2,128]{3,2,1,0:T(2,128)} %refs_2_.1, s32[5,1,2,128]{3,2,1,0:T(2,128)} %refs_3_.1, ...), custom_call_target="tpu_custom_call" | custom-call | tf_op jit(solution)/shard_map/prepare/pallas_call | solution.py:72
  2.6 3.0 %collective-permute-start = (bf16[400,128]{1,0:T(8,128)(2,1)S(1)}, bf16[400,128]{1,0:T(8,128)(2,1)S(1)}, u32[]{:S(2)}, u32[]{:S(2)}) collective-permute-start(bf16[400,128]{1,0:T(8,128)(2,1)S(1)} %get-tuple-element.13.own_ref), channel_id=1, source_target_pairs={{0,4},{4,0},{1,5},{5,1},{2,6},{6,2},{3,7},{7,3},{8,12},{12,8},{9,1... | collective-permute-start | bytes 307208 | tf_op jit(solution)/shard_map/ppermute | solution.py:399
  5.6 1.0 %begin_compression.1 = (bf16[2,24,512]{2,1,0:T(8,128)(2,1)S(1)}, f32[16,2048]{1,0:T(8,128)S(1)}, bf16[4352,256]{1,0:T(8,128)(2,1)S(1)}) custom-call(bf16[6,2,4096]{2,1,0:T(2,128)(2,1)S(1)} %get-tuple-element.14.echo_ref, bf16[2,2048]{1,0:T(2,128)(2,1)S(1)} %get-tuple-element.15.chirp_ref), custom_call_target="tpu_custom_call" | custom-call | tf_op jit(solution)/shard_map/begin_compression/pallas_call | solution.py:326
  6.7 1.3 %collective-permute-done.1.halo_ref = bf16[6,2,4096]{2,1,0:T(2,128)(2,1)S(1)} collective-permute-done((bf16[6,2,4096]{2,1,0:T(2,128)(2,1)}, bf16[6,2,4096]{2,1,0:T(2,128)(2,1)S(1)}, u32[]{:S(2)}, u32[]{:S(2)}) %collective-permute-start.1) | collective-permute-done | bytes 98336 | tf_op jit(solution)/shard_map/ppermute | solution.py:413
  7.9 0.5 %finish_compression.1 = (bf16[2,24,512]{2,1,0:T(8,128)(2,1)S(1)}, bf16[2,24,512]{2,1,0:T(8,128)(2,1)S(1)}) custom-call(s32[1]{0:T(128)} %bitcast.index_ref, bf16[2,24,512]{2,1,0:T(8,128)(2,1)S(1)} %get-tuple-element.16.early_ref, f32[16,2048]{1,0:T(8,128)S(1)} %get-tuple-element.17.late_ref, bf16[6,2,4096]{2,1,0:T(2,128)(2,1)S(1)} %collective-permute-done.1.halo_ref, ...), custom_call_target="tpu_custom_call" | custom-call | tf_op jit(solution)/shard_map/finish_compression/pallas_call | solution.py:341
  8.4 0.1 collective-permute-start.2
  8.5 1.2 %collective-permute-done.2 = bf16[2,24,512]{2,1,0:T(8,128)(2,1)S(1)} collective-permute-done((bf16[2,24,512]{2,1,0:T(8,128)(2,1)S(1)}, bf16[2,24,512]{2,1,0:T(8,128)(2,1)S(1)}, u32[]{:S(2)}, u32[]{:S(2)}) %collective-permute-start.2) | collective-permute-done | bytes 49184 | tf_op jit(solution)/shard_map/ppermute | solution.py:399
  9.8 2.7 %collective-permute-start.3 = (bf16[48,512]{1,0:T(8,128)(2,1)S(1)}, bf16[48,512]{1,0:T(8,128)(2,1)S(1)}, u32[]{:S(2)}, u32[]{:S(2)}) collective-permute-start(bf16[48,512]{1,0:T(8,128)(2,1)S(1)} %get-tuple-element.23), channel_id=1, source_target_pairs={{0,20},{4,16},{8,28},{12,24},{16,4},{20,0},{24,12},{28,8},{1,21},{... | collective-permute-start | bytes 147464 | tf_op jit(solution)/shard_map/ppermute | solution.py:409
  12.5 0.5 %collective-permute-start.4 = (bf16[48,512]{1,0:T(8,128)(2,1)S(1)}, bf16[48,512]{1,0:T(8,128)(2,1)S(1)}, u32[]{:S(2)}, u32[]{:S(2)}) collective-permute-start(bf16[48,512]{1,0:T(8,128)(2,1)S(1)} %get-tuple-element.22), channel_id=1, source_target_pairs={{0,16},{4,20},{8,12},{12,8},{16,0},{20,4},{24,28},{28,24},{1,17},{... | collective-permute-start | bytes 147464 | tf_op jit(solution)/shard_map/ppermute | solution.py:409
  13.1 0.3 %collective-permute-start.5 = (bf16[48,512]{1,0:T(8,128)(2,1)S(1)}, bf16[48,512]{1,0:T(8,128)(2,1)S(1)}, u32[]{:S(2)}, u32[]{:S(2)}) collective-permute-start(bf16[48,512]{1,0:T(8,128)(2,1)S(1)} %get-tuple-element.21), channel_id=1, source_target_pairs={{0,4},{4,0},{8,24},{12,28},{16,20},{20,16},{24,8},{28,12},{1,5},{5... | collective-permute-start | bytes 147464 | tf_op jit(solution)/shard_map/ppermute | solution.py:409
  13.3 0.0 collective-permute-done.partner_ref
  13.3 1.3 %fold_operator.1.operator_ref = bf16[2,256,256]{2,1,0:T(8,128)(2,1)S(1)} custom-call(s32[1]{0:T(128)} %bitcast.index_ref, bf16[400,128]{1,0:T(8,128)(2,1)S(1)} %get-tuple-element.13.own_ref, bf16[400,128]{1,0:T(8,128)(2,1)S(1)} %collective-permute-done.partner_ref), custom_call_target="tpu_custom_call" | custom-call | tf_op jit(solution)/shard_map/fold_operator/pallas_call | solution.py:188
  14.7 0.2 collective-permute-done.3.refs_0_
  14.8 1.8 %collective-permute-done.4.refs_1_ = bf16[48,512]{1,0:T(8,128)(2,1)S(1)} collective-permute-done((bf16[48,512]{1,0:T(8,128)(2,1)S(1)}, bf16[48,512]{1,0:T(8,128)(2,1)S(1)}, u32[]{:S(2)}, u32[]{:S(2)}) %collective-permute-start.4) | collective-permute-done | bytes 49184 | tf_op jit(solution)/shard_map/ppermute | solution.py:409
  16.6 0.5 %collective-permute-done.5.refs_2_ = bf16[48,512]{1,0:T(8,128)(2,1)S(1)} collective-permute-done((bf16[48,512]{1,0:T(8,128)(2,1)S(1)}, bf16[48,512]{1,0:T(8,128)(2,1)S(1)}, u32[]{:S(2)}, u32[]{:S(2)}) %collective-permute-start.5) | collective-permute-done | bytes 49184 | tf_op jit(solution)/shard_map/ppermute | solution.py:409
  17.1 1.1 %form_image.1 = bf16[256,1024]{1,0:T(8,128)(2,1)} custom-call(s32[1]{0:T(128)} %bitcast.index_ref, bf16[2,256,256]{2,1,0:T(8,128)(2,1)S(1)} %fold_operator.1.operator_ref, bf16[2,48,512]{2,1,0:T(8,128)(2,1)S(1)} %constant_dynamic-update-slice_fusion.both_ref, bf16[48,512]{1,0:T(8,128)(2,1)S(1)} %collective-permute-done.3.refs_0_, ...), custom_call_target="tpu_custom_call" | custom-call | tf_op jit(solution)/shard_map/form_image/pallas_call | solution.py:382
  (3 shorter events, 0.0 us)
Async XLA Ops:
  0.0 7.9 %collective-permute-start.1 = (bf16[6,2,4096]{2,1,0:T(2,128)(2,1)}, bf16[6,2,4096]{2,1,0:T(2,128)(2,1)S(1)}, u32[]{:S(2)}, u32[]{:S(2)}) collective-permute-start(bf16[6,2,4096]{2,1,0:T(2,128)(2,1)} %bitcast.15), channel_id=1, source_target_pairs={{1,0},{2,1},{3,2},{5,4},{6,5},{7,6},{9,8},{10,9},{11,10},{13,12},{... | collective-permute-start | bytes 294920 | tf_op jit(solution)/shard_map/ppermute | solution.py:413
  2.6 10.8 %collective-permute-start = (bf16[400,128]{1,0:T(8,128)(2,1)S(1)}, bf16[400,128]{1,0:T(8,128)(2,1)S(1)}, u32[]{:S(2)}, u32[]{:S(2)}) collective-permute-start(bf16[400,128]{1,0:T(8,128)(2,1)S(1)} %get-tuple-element.13.own_ref), channel_id=1, source_target_pairs={{0,4},{4,0},{1,5},{5,1},{2,6},{6,2},{3,7},{7,3},{8,12},{12,8},{9,1... | collective-permute-start | bytes 307208 | tf_op jit(solution)/shard_map/ppermute | solution.py:399
  8.4 1.3 %collective-permute-start.2 = (bf16[2,24,512]{2,1,0:T(8,128)(2,1)S(1)}, bf16[2,24,512]{2,1,0:T(8,128)(2,1)S(1)}, u32[]{:S(2)}, u32[]{:S(2)}) collective-permute-start(bf16[2,24,512]{2,1,0:T(8,128)(2,1)S(1)} %get-tuple-element.20), channel_id=1, source_target_pairs={{0,8},{8,0},{16,24},{24,16},{1,9},{9,1},{17,25},{25,17},{2,10},{10... | collective-permute-start | bytes 147464 | tf_op jit(solution)/shard_map/ppermute | solution.py:399
  9.8 5.1 %collective-permute-start.3 = (bf16[48,512]{1,0:T(8,128)(2,1)S(1)}, bf16[48,512]{1,0:T(8,128)(2,1)S(1)}, u32[]{:S(2)}, u32[]{:S(2)}) collective-permute-start(bf16[48,512]{1,0:T(8,128)(2,1)S(1)} %get-tuple-element.23), channel_id=1, source_target_pairs={{0,20},{4,16},{8,28},{12,24},{16,4},{20,0},{24,12},{28,8},{1,21},{... | collective-permute-start | bytes 147464 | tf_op jit(solution)/shard_map/ppermute | solution.py:409
  12.5 4.1 %collective-permute-start.4 = (bf16[48,512]{1,0:T(8,128)(2,1)S(1)}, bf16[48,512]{1,0:T(8,128)(2,1)S(1)}, u32[]{:S(2)}, u32[]{:S(2)}) collective-permute-start(bf16[48,512]{1,0:T(8,128)(2,1)S(1)} %get-tuple-element.22), channel_id=1, source_target_pairs={{0,16},{4,20},{8,12},{12,8},{16,0},{20,4},{24,28},{28,24},{1,17},{... | collective-permute-start | bytes 147464 | tf_op jit(solution)/shard_map/ppermute | solution.py:409
  13.1 4.1 %collective-permute-start.5 = (bf16[48,512]{1,0:T(8,128)(2,1)S(1)}, bf16[48,512]{1,0:T(8,128)(2,1)S(1)}, u32[]{:S(2)}, u32[]{:S(2)}) collective-permute-start(bf16[48,512]{1,0:T(8,128)(2,1)S(1)} %get-tuple-element.21), channel_id=1, source_target_pairs={{0,4},{4,0},{8,24},{12,28},{16,20},{20,16},{24,8},{28,12},{1,5},{5... | collective-permute-start | bytes 147464 | tf_op jit(solution)/shard_map/ppermute | solution.py:409

commit v8 on v6

--- a/solution.py
+++ b/solution.py
@@ -431,12 +431,12 @@
         echo, chirp, coef, band_start, band_width, weights, pulse_order, sections, group
     )
     has_next = (lax.axis_index("rng") < lax.axis_size("rng") - 1).astype(jnp.int32)
-    if subs == 2:
-        packed_partner = swap(packed, "sub", 1)
     early, late, table = begin_compression(echo, chirp, sections, group)
     place = section + sections * has_next
     keep, give = finish_compression(place, early, late, halo, table, group)
+    give, packed = lax.optimization_barrier((give, packed))
     both = jnp.concatenate([keep, swap(give, "section", 1)], axis=1)
+    packed_partner = swap(packed, "sub", 1) if subs == 2 else packed
     far = lax.dynamic_index_in_dim(both, section[0] % 2, 0, keepdims=False)
     if subs != 2:
         near = lax.dynamic_index_in_dim(both, 1 - section[0] % 2, 0, keepdims=False)

time: 18.2 us -> 18.3 us (level)
  waiting for transfers between devices: 2.45 us -> 2.65 us
    ppermute x1, waiting for transfers between devices: 0.01 us -> 0.19 us  [from_next(): lax.ppermute(value, axis, [(i, (i - 1) % count) for i in range(count)])]
  transfers between devices with their start and end apart: 6 -> 6, of which waited for: 4 -> 5; matrix products, arithmetic and copies ran while one was open for 0% -> 0% of each run, Pallas kernels for 23% -> 20%
where the time goes in v8:
time: 18.3 us; the launch traced here: 18.1 us
  starting transfers between devices  10.2 us (56%)
  Pallas kernels  5.21 us (28%)
  waiting for transfers between devices  2.65 us (14%)
    ppermute x1, starting transfers between devices, from_next(): lax.ppermute(value, axis, [(i, (i - 1) % count) for i in range(count)])  5.05 us
    ppermute x3, starting transfers between devices, swap_by(): return lax.ppermute(value, ('section', 'sub'), pairs)  3.55 us
    ppermute x2, starting transfers between devices, swap(): return lax.ppermute(value, axis, [(i, i ^ by) for i in range(count)])  1.59 us
    pallas_call x1, Pallas kernels, fold_operator(): pl.pallas_call(functools.partial(operator_kernel, dims=dims, sections=sec...  1.32 us
    pallas_call x1, Pallas kernels, prepare(): pl.pallas_call(functools.partial(prepare_kernel, sections=sections, group...  1.27 us
    ppermute x3, waiting for transfers between devices, swap_by(): return lax.ppermute(value, ('section', 'sub'), pairs)  1.23 us
    ppermute x2, waiting for transfers between devices, swap(): return lax.ppermute(value, axis, [(i, i ^ by) for i in range(count)])  1.23 us
    pallas_call x1, Pallas kernels, form_image(): pl.pallas_call(functools.partial(image_kernel, group=group), out_shape=ja...  1.06 us
  transfers between devices with their start and end apart: 6, of which 5 were waited for; matrix products, arithmetic and copies ran while one was open for 0% of the time, Pallas kernels for 20%

profile of v8, /device:TPU:0, one launch (start us, length us, event | category | flops | bytes accessed | tf_op | source)
XLA Modules:
  0.0 18.1 jit_solution(495031467451584425)
XLA Ops:
  0.0 5.0 %collective-permute-start = (bf16[6,2,4096]{2,1,0:T(2,128)(2,1)}, bf16[6,2,4096]{2,1,0:T(2,128)(2,1)S(1)}, u32[]{:S(2)}, u32[]{:S(2)}) collective-permute-start(bf16[6,2,4096]{2,1,0:T(2,128)(2,1)} %bitcast.16), channel_id=1, source_target_pairs={{0,3},{1,0},{2,1},{3,2},{4,7},{5,4},{6,5},{7,6},{8,11},{9,8},{10,9... | collective-permute-start | bytes 294920 | tf_op jit(solution)/shard_map/ppermute | solution.py:415
  5.0 1.3 %prepare.1 = (bf16[6,2,4096]{2,1,0:T(2,128)(2,1)S(1)}, bf16[2,2048]{1,0:T(2,128)(2,1)S(1)}, bf16[400,128]{1,0:T(8,128)(2,1)S(1)}) custom-call(bf16[6,2,4096]{2,1,0:T(2,128)(2,1)} %bitcast.17, bf16[5,1,2,2,16,128]{5,4,3,2,1,0:T(8,128)(2,1)} %bitcast.18, s32[5,1,2,128]{3,2,1,0:T(2,128)} %refs_2_.1, s32[5,1,2,128]{3,2,1,0:T(2,128)} %refs_3_.1, ...), custom_call_target="tpu_custom_call" | custom-call | tf_op jit(solution)/shard_map/prepare/pallas_call | solution.py:72
  6.3 1.0 %begin_compression.1 = (bf16[2,24,512]{2,1,0:T(8,128)(2,1)S(1)}, f32[16,2048]{1,0:T(8,128)S(1)}, bf16[4352,256]{1,0:T(8,128)(2,1)S(1)}) custom-call(bf16[6,2,4096]{2,1,0:T(2,128)(2,1)S(1)} %get-tuple-element.15.echo_ref, bf16[2,2048]{1,0:T(2,128)(2,1)S(1)} %get-tuple-element.16.chirp_ref), custom_call_target="tpu_custom_call" | custom-call | tf_op jit(solution)/shard_map/begin_compression/pallas_call | solution.py:327
  7.4 0.2 %collective-permute-done.halo_ref = bf16[6,2,4096]{2,1,0:T(2,128)(2,1)S(1)} collective-permute-done((bf16[6,2,4096]{2,1,0:T(2,128)(2,1)}, bf16[6,2,4096]{2,1,0:T(2,128)(2,1)S(1)}, u32[]{:S(2)}, u32[]{:S(2)}) %collective-permute-start) | collective-permute-done | bytes 98336 | tf_op jit(solution)/shard_map/ppermute | solution.py:415
  7.6 0.5 %finish_compression.1 = (bf16[2,24,512]{2,1,0:T(8,128)(2,1)S(1)}, bf16[2,24,512]{2,1,0:T(8,128)(2,1)S(1)}) custom-call(s32[1]{0:T(128)S(6)} %add.15.index_ref, bf16[2,24,512]{2,1,0:T(8,128)(2,1)S(1)} %get-tuple-element.17.early_ref, f32[16,2048]{1,0:T(8,128)S(1)} %get-tuple-element.18.late_ref, bf16[6,2,4096]{2,1,0:T(2,128)(2,1)S(1)} %collective-permute-done.halo_ref, ...), custom_call_target="tpu_custom_call" | custom-call | tf_op jit(solution)/shard_map/finish_compression/pallas_call | solution.py:342
  8.1 1.6 %collective-permute-start.1 = (bf16[400,128]{1,0:T(8,128)(2,1)S(1)}, bf16[400,128]{1,0:T(8,128)(2,1)S(1)}, u32[]{:S(2)}, u32[]{:S(2)}) collective-permute-start(bf16[400,128]{1,0:T(8,128)(2,1)S(1)} %get-tuple-element.22.own_ref), channel_id=1, source_target_pairs={{0,4},{4,0},{1,5},{5,1},{2,6},{6,2},{3,7},{7,3},{8,12},{12,8},{9,1... | collective-permute-start | bytes 307208 | tf_op jit(solution)/shard_map/ppermute | solution.py:400
  9.7 0.0 collective-permute-start.2
  9.7 1.2 %collective-permute-done.2 = bf16[2,24,512]{2,1,0:T(8,128)(2,1)S(1)} collective-permute-done((bf16[2,24,512]{2,1,0:T(8,128)(2,1)S(1)}, bf16[2,24,512]{2,1,0:T(8,128)(2,1)S(1)}, u32[]{:S(2)}, u32[]{:S(2)}) %collective-permute-start.2) | collective-permute-done | bytes 49184 | tf_op jit(solution)/shard_map/ppermute | solution.py:400
  10.9 1.5 %collective-permute-start.3 = (bf16[48,512]{1,0:T(8,128)(2,1)S(1)}, bf16[48,512]{1,0:T(8,128)(2,1)S(1)}, u32[]{:S(2)}, u32[]{:S(2)}) collective-permute-start(bf16[48,512]{1,0:T(8,128)(2,1)S(1)} %get-tuple-element.27), channel_id=1, source_target_pairs={{0,20},{4,16},{8,28},{12,24},{16,4},{20,0},{24,12},{28,8},{1,21},{... | collective-permute-start | bytes 147464 | tf_op jit(solution)/shard_map/ppermute | solution.py:410
  12.4 0.5 %collective-permute-start.4 = (bf16[48,512]{1,0:T(8,128)(2,1)S(1)}, bf16[48,512]{1,0:T(8,128)(2,1)S(1)}, u32[]{:S(2)}, u32[]{:S(2)}) collective-permute-start(bf16[48,512]{1,0:T(8,128)(2,1)S(1)} %get-tuple-element.26), channel_id=1, source_target_pairs={{0,16},{4,20},{8,12},{12,8},{16,0},{20,4},{24,28},{28,24},{1,17},{... | collective-permute-start | bytes 147464 | tf_op jit(solution)/shard_map/ppermute | solution.py:410
  13.0 1.5 %collective-permute-start.5 = (bf16[48,512]{1,0:T(8,128)(2,1)S(1)}, bf16[48,512]{1,0:T(8,128)(2,1)S(1)}, u32[]{:S(2)}, u32[]{:S(2)}) collective-permute-start(bf16[48,512]{1,0:T(8,128)(2,1)S(1)} %get-tuple-element.25), channel_id=1, source_target_pairs={{0,4},{4,0},{8,24},{12,28},{16,20},{20,16},{24,8},{28,12},{1,5},{5... | collective-permute-start | bytes 147464 | tf_op jit(solution)/shard_map/ppermute | solution.py:410
  14.5 0.0 collective-permute-done.1.partner_ref
  14.5 1.3 %fold_operator.1.operator_ref = bf16[2,256,256]{2,1,0:T(8,128)(2,1)S(1)} custom-call(s32[1]{0:T(128)} %bitcast.index_ref, bf16[400,128]{1,0:T(8,128)(2,1)S(1)} %get-tuple-element.22.own_ref, bf16[400,128]{1,0:T(8,128)(2,1)S(1)} %collective-permute-done.1.partner_ref), custom_call_target="tpu_custom_call" | custom-call | tf_op jit(solution)/shard_map/fold_operator/pallas_call | solution.py:188
  15.8 0.2 %collective-permute-done.3.refs_0_ = bf16[48,512]{1,0:T(8,128)(2,1)S(1)} collective-permute-done((bf16[48,512]{1,0:T(8,128)(2,1)S(1)}, bf16[48,512]{1,0:T(8,128)(2,1)S(1)}, u32[]{:S(2)}, u32[]{:S(2)}) %collective-permute-start.3) | collective-permute-done | bytes 49184 | tf_op jit(solution)/shard_map/ppermute | solution.py:410
  16.0 0.9 %collective-permute-done.4.refs_1_ = bf16[48,512]{1,0:T(8,128)(2,1)S(1)} collective-permute-done((bf16[48,512]{1,0:T(8,128)(2,1)S(1)}, bf16[48,512]{1,0:T(8,128)(2,1)S(1)}, u32[]{:S(2)}, u32[]{:S(2)}) %collective-permute-start.4) | collective-permute-done | bytes 49184 | tf_op jit(solution)/shard_map/ppermute | solution.py:410
  16.9 0.2 collective-permute-done.5.refs_2_
  17.1 1.1 %form_image.1 = bf16[256,1024]{1,0:T(8,128)(2,1)} custom-call(s32[1]{0:T(128)} %bitcast.index_ref, bf16[2,256,256]{2,1,0:T(8,128)(2,1)S(1)} %fold_operator.1.operator_ref, bf16[2,48,512]{2,1,0:T(8,128)(2,1)S(1)} %constant_dynamic-update-slice_fusion.both_ref, bf16[48,512]{1,0:T(8,128)(2,1)S(1)} %collective-permute-done.3.refs_0_, ...), custom_call_target="tpu_custom_call" | custom-call | tf_op jit(solution)/shard_map/form_image/pallas_call | solution.py:383
  (3 shorter events, 0.0 us)
Async XLA Ops:
  0.0 7.6 %collective-permute-start = (bf16[6,2,4096]{2,1,0:T(2,128)(2,1)}, bf16[6,2,4096]{2,1,0:T(2,128)(2,1)S(1)}, u32[]{:S(2)}, u32[]{:S(2)}) collective-permute-start(bf16[6,2,4096]{2,1,0:T(2,128)(2,1)} %bitcast.16), channel_id=1, source_target_pairs={{0,3},{1,0},{2,1},{3,2},{4,7},{5,4},{6,5},{7,6},{8,11},{9,8},{10,9... | collective-permute-start | bytes 294920 | tf_op jit(solution)/shard_map/ppermute | solution.py:415
  8.1 6.4 %collective-permute-start.1 = (bf16[400,128]{1,0:T(8,128)(2,1)S(1)}, bf16[400,128]{1,0:T(8,128)(2,1)S(1)}, u32[]{:S(2)}, u32[]{:S(2)}) collective-permute-start(bf16[400,128]{1,0:T(8,128)(2,1)S(1)} %get-tuple-element.22.own_ref), channel_id=1, source_target_pairs={{0,4},{4,0},{1,5},{5,1},{2,6},{6,2},{3,7},{7,3},{8,12},{12,8},{9,1... | collective-permute-start | bytes 307208 | tf_op jit(solution)/shard_map/ppermute | solution.py:400
  9.7 1.2 %collective-permute-start.2 = (bf16[2,24,512]{2,1,0:T(8,128)(2,1)S(1)}, bf16[2,24,512]{2,1,0:T(8,128)(2,1)S(1)}, u32[]{:S(2)}, u32[]{:S(2)}) collective-permute-start(bf16[2,24,512]{2,1,0:T(8,128)(2,1)S(1)} %get-tuple-element.24), channel_id=1, source_target_pairs={{0,8},{8,0},{16,24},{24,16},{1,9},{9,1},{17,25},{25,17},{2,10},{10... | collective-permute-start | bytes 147464 | tf_op jit(solution)/shard_map/ppermute | solution.py:400
  10.9 5.1 %collective-permute-start.3 = (bf16[48,512]{1,0:T(8,128)(2,1)S(1)}, bf16[48,512]{1,0:T(8,128)(2,1)S(1)}, u32[]{:S(2)}, u32[]{:S(2)}) collective-permute-start(bf16[48,512]{1,0:T(8,128)(2,1)S(1)} %get-tuple-element.27), channel_id=1, source_target_pairs={{0,20},{4,16},{8,28},{12,24},{16,4},{20,0},{24,12},{28,8},{1,21},{... | collective-permute-start | bytes 147464 | tf_op jit(solution)/shard_map/ppermute | solution.py:410
  12.4 4.5 %collective-permute-start.4 = (bf16[48,512]{1,0:T(8,128)(2,1)S(1)}, bf16[48,512]{1,0:T(8,128)(2,1)S(1)}, u32[]{:S(2)}, u32[]{:S(2)}) collective-permute-start(bf16[48,512]{1,0:T(8,128)(2,1)S(1)} %get-tuple-element.26), channel_id=1, source_target_pairs={{0,16},{4,20},{8,12},{12,8},{16,0},{20,4},{24,28},{28,24},{1,17},{... | collective-permute-start | bytes 147464 | tf_op jit(solution)/shard_map/ppermute | solution.py:410
  13.0 4.1 %collective-permute-start.5 = (bf16[48,512]{1,0:T(8,128)(2,1)S(1)}, bf16[48,512]{1,0:T(8,128)(2,1)S(1)}, u32[]{:S(2)}, u32[]{:S(2)}) collective-permute-start(bf16[48,512]{1,0:T(8,128)(2,1)S(1)} %get-tuple-element.25), channel_id=1, source_target_pairs={{0,4},{4,0},{8,24},{12,28},{16,20},{20,16},{24,8},{28,12},{1,5},{5... | collective-permute-start | bytes 147464 | tf_op jit(solution)/shard_map/ppermute | solution.py:410

commit v9 on v6

--- a/solution.py
+++ b/solution.py
@@ -174,8 +174,8 @@
         quarters = [jnp.concatenate(sources[q * pairs : (q + 1) * pairs], axis=0) for q in range(4)]
         quarters = [
             quarters[0],
-            quarters[3],
-            jnp.where(first_core, quarters[1], quarters[2]),
+            jnp.where(first_core, quarters[3], quarters[2]),
+            jnp.where(first_core, quarters[1], quarters[3]),
             jnp.where(first_core, quarters[2], quarters[1]),
         ]
         high, low = split_two(jnp.concatenate(quarters, axis=0).T)
@@ -443,8 +443,8 @@
         chunks = [near, swap(far, "section", 2)]
         return merge_images(section, chunks, packed, dims, sections, group, pulses_each)
     chunks = [
-        swap_by(far, lambda s, a: (s ^ 2, a ^ 1)),
-        swap_by(both[0], lambda s, a: (s, a ^ 1) if s % 2 else (s ^ 2, a)),
+        swap_by(both[0], lambda s, a: (s, a ^ 1) if s % 2 else (s ^ 2, a ^ 1)),
+        swap_by(far, lambda s, a: (s ^ 2, a ^ 1) if s % 2 else (s ^ 2, a)),
         swap_by(both[1], lambda s, a: (s ^ 2, a) if s % 2 else (s, a ^ 1)),
     ]
     operator = fold_operator(section, packed, packed_partner, dims, sections, group, pulses_each)

time: 18.2 us -> 18.2 us (level)
  no operation moved by 1% of the time
where the time goes in v9:
time: 18.2 us; the launch traced here: 18 us
  starting transfers between devices  10.3 us (57%)
  Pallas kernels  5.2 us (29%)
  waiting for transfers between devices  2.42 us (13%)
    ppermute x1, starting transfers between devices, from_next(): lax.ppermute(value, axis, [(i, (i - 1) % count) for i in range(count)])  5.05 us
    ppermute x3, starting transfers between devices, swap_by(): return lax.ppermute(value, ('section', 'sub'), pairs)  3.59 us
    ppermute x2, starting transfers between devices, swap(): return lax.ppermute(value, axis, [(i, i ^ by) for i in range(count)])  1.66 us
    pallas_call x1, Pallas kernels, fold_operator(): pl.pallas_call(functools.partial(operator_kernel, dims=dims, sections=sec...  1.32 us
    pallas_call x1, Pallas kernels, prepare(): pl.pallas_call(functools.partial(prepare_kernel, sections=sections, group...  1.27 us
    ppermute x3, waiting for transfers between devices, swap_by(): return lax.ppermute(value, ('section', 'sub'), pairs)  1.21 us
    ppermute x2, waiting for transfers between devices, swap(): return lax.ppermute(value, axis, [(i, i ^ by) for i in range(count)])  1.21 us
    pallas_call x1, Pallas kernels, form_image(): pl.pallas_call(functools.partial(image_kernel, group=group), out_shape=ja...  1.06 us
  transfers between devices with their start and end apart: 6, of which 4 were waited for; matrix products, arithmetic and copies ran while one was open for 0% of the time, Pallas kernels for 23%

profile of v9, /device:TPU:0, one launch (start us, length us, event | category | flops | bytes accessed | tf_op | source)
XLA Modules:
  0.0 18.0 jit_solution(12215027497553326667)
XLA Ops:
  0.0 5.0 %collective-permute-start.1 = (bf16[6,2,4096]{2,1,0:T(2,128)(2,1)}, bf16[6,2,4096]{2,1,0:T(2,128)(2,1)S(1)}, u32[]{:S(2)}, u32[]{:S(2)}) collective-permute-start(bf16[6,2,4096]{2,1,0:T(2,128)(2,1)} %bitcast.16), channel_id=1, source_target_pairs={{0,3},{1,0},{2,1},{3,2},{4,7},{5,4},{6,5},{7,6},{8,11},{9,8},{10,9... | collective-permute-start | bytes 294920 | tf_op jit(solution)/shard_map/ppermute | solution.py:415
  5.0 1.3 %prepare.1 = (bf16[6,2,4096]{2,1,0:T(2,128)(2,1)S(1)}, bf16[2,2048]{1,0:T(2,128)(2,1)S(1)}, bf16[400,128]{1,0:T(8,128)(2,1)S(1)}) custom-call(bf16[6,2,4096]{2,1,0:T(2,128)(2,1)} %bitcast.17, bf16[5,1,2,2,16,128]{5,4,3,2,1,0:T(8,128)(2,1)} %bitcast.18, s32[5,1,2,128]{3,2,1,0:T(2,128)} %refs_2_.1, s32[5,1,2,128]{3,2,1,0:T(2,128)} %refs_3_.1, ...), custom_call_target="tpu_custom_call" | custom-call | tf_op jit(solution)/shard_map/prepare/pallas_call | solution.py:72
  6.3 1.6 %collective-permute-start = (bf16[400,128]{1,0:T(8,128)(2,1)S(1)}, bf16[400,128]{1,0:T(8,128)(2,1)S(1)}, u32[]{:S(2)}, u32[]{:S(2)}) collective-permute-start(bf16[400,128]{1,0:T(8,128)(2,1)S(1)} %get-tuple-element.13.own_ref), channel_id=1, source_target_pairs={{0,4},{4,0},{1,5},{5,1},{2,6},{6,2},{3,7},{7,3},{8,12},{12,8},{9,1... | collective-permute-start | bytes 307208 | tf_op jit(solution)/shard_map/ppermute | solution.py:400
  7.9 1.0 %begin_compression.1 = (bf16[2,24,512]{2,1,0:T(8,128)(2,1)S(1)}, f32[16,2048]{1,0:T(8,128)S(1)}, bf16[4352,256]{1,0:T(8,128)(2,1)S(1)}) custom-call(bf16[6,2,4096]{2,1,0:T(2,128)(2,1)S(1)} %get-tuple-element.14.echo_ref, bf16[2,2048]{1,0:T(2,128)(2,1)S(1)} %get-tuple-element.15.chirp_ref), custom_call_target="tpu_custom_call" | custom-call | tf_op jit(solution)/shard_map/begin_compression/pallas_call | solution.py:327
  9.0 0.0 collective-permute-done.1.halo_ref
  9.0 0.5 %finish_compression.1 = (bf16[2,24,512]{2,1,0:T(8,128)(2,1)S(1)}, bf16[2,24,512]{2,1,0:T(8,128)(2,1)S(1)}) custom-call(s32[1]{0:T(128)S(6)} %add.15.index_ref, bf16[2,24,512]{2,1,0:T(8,128)(2,1)S(1)} %get-tuple-element.16.early_ref, f32[16,2048]{1,0:T(8,128)S(1)} %get-tuple-element.17.late_ref, bf16[6,2,4096]{2,1,0:T(2,128)(2,1)S(1)} %collective-permute-done.1.halo_ref, ...), custom_call_target="tpu_custom_call" | custom-call | tf_op jit(solution)/shard_map/finish_compression/pallas_call | solution.py:342
  9.5 0.1 collective-permute-start.2
  9.6 1.2 %collective-permute-done.2 = bf16[2,24,512]{2,1,0:T(8,128)(2,1)S(1)} collective-permute-done((bf16[2,24,512]{2,1,0:T(8,128)(2,1)S(1)}, bf16[2,24,512]{2,1,0:T(8,128)(2,1)S(1)}, u32[]{:S(2)}, u32[]{:S(2)}) %collective-permute-start.2) | collective-permute-done | bytes 49184 | tf_op jit(solution)/shard_map/ppermute | solution.py:400
  10.8 1.5 %collective-permute-start.3 = (bf16[48,512]{1,0:T(8,128)(2,1)S(1)}, bf16[48,512]{1,0:T(8,128)(2,1)S(1)}, u32[]{:S(2)}, u32[]{:S(2)}) collective-permute-start(bf16[48,512]{1,0:T(8,128)(2,1)S(1)} %get-tuple-element.23), channel_id=1, source_target_pairs={{0,20},{4,16},{8,12},{12,8},{16,4},{20,0},{24,28},{28,24},{1,21},{... | collective-permute-start | bytes 147464 | tf_op jit(solution)/shard_map/ppermute | solution.py:410
  12.3 0.5 %collective-permute-start.4 = (bf16[48,512]{1,0:T(8,128)(2,1)S(1)}, bf16[48,512]{1,0:T(8,128)(2,1)S(1)}, u32[]{:S(2)}, u32[]{:S(2)}) collective-permute-start(bf16[48,512]{1,0:T(8,128)(2,1)S(1)} %get-tuple-element.22), channel_id=1, source_target_pairs={{0,16},{4,20},{8,28},{12,24},{16,0},{20,4},{24,12},{28,8},{1,17},{... | collective-permute-start | bytes 147464 | tf_op jit(solution)/shard_map/ppermute | solution.py:410
  12.9 1.5 %collective-permute-start.5 = (bf16[48,512]{1,0:T(8,128)(2,1)S(1)}, bf16[48,512]{1,0:T(8,128)(2,1)S(1)}, u32[]{:S(2)}, u32[]{:S(2)}) collective-permute-start(bf16[48,512]{1,0:T(8,128)(2,1)S(1)} %get-tuple-element.21), channel_id=1, source_target_pairs={{0,4},{4,0},{8,24},{12,28},{16,20},{20,16},{24,8},{28,12},{1,5},{5... | collective-permute-start | bytes 147464 | tf_op jit(solution)/shard_map/ppermute | solution.py:410
  14.4 0.0 collective-permute-done.partner_ref
  14.4 1.3 %fold_operator.1.operator_ref = bf16[2,256,256]{2,1,0:T(8,128)(2,1)S(1)} custom-call(s32[1]{0:T(128)} %bitcast.index_ref, bf16[400,128]{1,0:T(8,128)(2,1)S(1)} %get-tuple-element.13.own_ref, bf16[400,128]{1,0:T(8,128)(2,1)S(1)} %collective-permute-done.partner_ref), custom_call_target="tpu_custom_call" | custom-call | tf_op jit(solution)/shard_map/fold_operator/pallas_call | solution.py:188
  15.7 0.2 collective-permute-done.3.refs_0_
  15.9 0.9 %collective-permute-done.4.refs_1_ = bf16[48,512]{1,0:T(8,128)(2,1)S(1)} collective-permute-done((bf16[48,512]{1,0:T(8,128)(2,1)S(1)}, bf16[48,512]{1,0:T(8,128)(2,1)S(1)}, u32[]{:S(2)}, u32[]{:S(2)}) %collective-permute-start.4) | collective-permute-done | bytes 49184 | tf_op jit(solution)/shard_map/ppermute | solution.py:410
  16.8 0.2 collective-permute-done.5.refs_2_
  16.9 1.1 %form_image.1 = bf16[256,1024]{1,0:T(8,128)(2,1)} custom-call(s32[1]{0:T(128)} %bitcast.index_ref, bf16[2,256,256]{2,1,0:T(8,128)(2,1)S(1)} %fold_operator.1.operator_ref, bf16[2,48,512]{2,1,0:T(8,128)(2,1)S(1)} %constant_dynamic-update-slice_fusion.both_ref, bf16[48,512]{1,0:T(8,128)(2,1)S(1)} %collective-permute-done.3.refs_0_, ...), custom_call_target="tpu_custom_call" | custom-call | tf_op jit(solution)/shard_map/form_image/pallas_call | solution.py:383
  (3 shorter events, 0.0 us)
Async XLA Ops:
  0.0 9.0 %collective-permute-start.1 = (bf16[6,2,4096]{2,1,0:T(2,128)(2,1)}, bf16[6,2,4096]{2,1,0:T(2,128)(2,1)S(1)}, u32[]{:S(2)}, u32[]{:S(2)}) collective-permute-start(bf16[6,2,4096]{2,1,0:T(2,128)(2,1)} %bitcast.16), channel_id=1, source_target_pairs={{0,3},{1,0},{2,1},{3,2},{4,7},{5,4},{6,5},{7,6},{8,11},{9,8},{10,9... | collective-permute-start | bytes 294920 | tf_op jit(solution)/shard_map/ppermute | solution.py:415
  6.3 8.1 %collective-permute-start = (bf16[400,128]{1,0:T(8,128)(2,1)S(1)}, bf16[400,128]{1,0:T(8,128)(2,1)S(1)}, u32[]{:S(2)}, u32[]{:S(2)}) collective-permute-start(bf16[400,128]{1,0:T(8,128)(2,1)S(1)} %get-tuple-element.13.own_ref), channel_id=1, source_target_pairs={{0,4},{4,0},{1,5},{5,1},{2,6},{6,2},{3,7},{7,3},{8,12},{12,8},{9,1... | collective-permute-start | bytes 307208 | tf_op jit(solution)/shard_map/ppermute | solution.py:400
  9.5 1.3 %collective-permute-start.2 = (bf16[2,24,512]{2,1,0:T(8,128)(2,1)S(1)}, bf16[2,24,512]{2,1,0:T(8,128)(2,1)S(1)}, u32[]{:S(2)}, u32[]{:S(2)}) collective-permute-start(bf16[2,24,512]{2,1,0:T(8,128)(2,1)S(1)} %get-tuple-element.20), channel_id=1, source_target_pairs={{0,8},{8,0},{16,24},{24,16},{1,9},{9,1},{17,25},{25,17},{2,10},{10... | collective-permute-start | bytes 147464 | tf_op jit(solution)/shard_map/ppermute | solution.py:400
  10.8 5.1 %collective-permute-start.3 = (bf16[48,512]{1,0:T(8,128)(2,1)S(1)}, bf16[48,512]{1,0:T(8,128)(2,1)S(1)}, u32[]{:S(2)}, u32[]{:S(2)}) collective-permute-start(bf16[48,512]{1,0:T(8,128)(2,1)S(1)} %get-tuple-element.23), channel_id=1, source_target_pairs={{0,20},{4,16},{8,12},{12,8},{16,4},{20,0},{24,28},{28,24},{1,21},{... | collective-permute-start | bytes 147464 | tf_op jit(solution)/shard_map/ppermute | solution.py:410
  12.3 4.5 %collective-permute-start.4 = (bf16[48,512]{1,0:T(8,128)(2,1)S(1)}, bf16[48,512]{1,0:T(8,128)(2,1)S(1)}, u32[]{:S(2)}, u32[]{:S(2)}) collective-permute-start(bf16[48,512]{1,0:T(8,128)(2,1)S(1)} %get-tuple-element.22), channel_id=1, source_target_pairs={{0,16},{4,20},{8,28},{12,24},{16,0},{20,4},{24,12},{28,8},{1,17},{... | collective-permute-start | bytes 147464 | tf_op jit(solution)/shard_map/ppermute | solution.py:410
  12.9 4.1 %collective-permute-start.5 = (bf16[48,512]{1,0:T(8,128)(2,1)S(1)}, bf16[48,512]{1,0:T(8,128)(2,1)S(1)}, u32[]{:S(2)}, u32[]{:S(2)}) collective-permute-start(bf16[48,512]{1,0:T(8,128)(2,1)S(1)} %get-tuple-element.21), channel_id=1, source_target_pairs={{0,4},{4,0},{8,24},{12,28},{16,20},{20,16},{24,8},{28,12},{1,5},{5... | collective-permute-start | bytes 147464 | tf_op jit(solution)/shard_map/ppermute | solution.py:410

commit v10 on v8

--- a/solution.py
+++ b/solution.py
@@ -199,32 +199,37 @@
     )(section, own, partner)
 
 
-def correlate(rows, even, odd, table, blocks, group):
-    extra = table.shape[0] // (2 * LANE) - 1
-    total = blocks + extra
-    held = [
-        jnp.concatenate(
-            [rows[:group, b * LANE : (b + 1) * LANE], rows[group:, b * LANE : (b + 1) * LANE]], axis=1
-        )
-        for b in range(total)
-    ]
-    for b in range(0, total, 2):
-        even[b * group : (b + 2) * group] = jnp.concatenate(held[b : b + 2], axis=0).astype(BF16)
-    for b in range(1, total - 1, 2):
-        odd[(b - 1) * group : (b + 1) * group] = jnp.concatenate(held[b : b + 2], axis=0).astype(BF16)
-    window = blocks * group
+def lay_out(rows, refs, held, first, blocks, group, keep):
+    span = blocks * LANE
+    rows[...] = jnp.zeros_like(rows)
+    for m, ref in enumerate(refs):
+        for p in range(ref.shape[0]):
+            samples = ref[p, :, :span].astype(F32)
+            samples = samples if keep is None else jnp.where(keep, samples, 0.0)
+            for c in range(2):
+                rows[c, m * group + p : m * group + p + 1, :] = samples[c : c + 1]
+    stack = rows.shape[1]
+    for b in range(blocks):
+        for c in range(2):
+            held[(first + b) * stack : (first + b + 1) * stack, c * LANE : (c + 1) * LANE] = rows[
+                c, :, b * LANE : (b + 1) * LANE
+            ].astype(BF16)
+
+
+def correlate(held, table, first, blocks, stack):
+    lags = table.shape[0] // (2 * LANE)
     pieces = []
-    for lag in range(extra + 1):
-        source, at = (even, lag) if lag % 2 == 0 else (odd, lag - 1)
-        pieces.append(source[at * group : at * group + window])
+    for lag in range(lags):
+        at = pl.multiple_of((first + lag) * stack, stack)
+        pieces.append(held[pl.ds(at, blocks * stack)])
     return jnp.dot(jnp.concatenate(pieces, axis=1), table[...], preferred_element_type=F32)
 
 
-def as_chunk(done, s, chunk, group, each):
+def as_chunk(done, source, chunk, stack, group, each):
     real, imag = [
         jnp.concatenate(
             [
-                done[(s * chunk + b) * group : (s * chunk + b + 1) * group, c * LANE : (c + 1) * LANE]
+                done[b * stack + source * group : b * stack + (source + 1) * group, c * LANE : (c + 1) * LANE]
                 for b in range(chunk)
             ],
             axis=1,
@@ -242,7 +247,7 @@
     return jnp.concatenate([lead[:, :middle], lead[:, middle:], rest], axis=0).astype(BF16)
 
 
-def begin_kernel(echo_ref, chirp_ref, early_ref, late_ref, table, rows, even, odd, *, group):
+def begin_kernel(index_ref, echo_ref, other_ref, chirp_ref, early_ref, late_ref, table, rows, held, *, group):
     pulses, _, length = echo_ref.shape
     extra = chirp_ref.shape[1] // LANE
     reverse = LANE - 1 - lax.broadcasted_iota(jnp.int32, (2, LANE), 1)
@@ -269,93 +274,89 @@
         table[at : at + LANE, LANE:] = (-imag).astype(BF16)
         table[at + LANE : at + 2 * LANE, :LANE] = imag.astype(BF16)
         table[at + LANE : at + 2 * LANE, LANE:] = real.astype(BF16)
-    rows[...] = jnp.zeros_like(rows)
-    for p in range(pulses):
-        near = echo_ref[p].astype(F32)
-        for c in range(2):
-            rows[c * group + p : c * group + p + 1, :] = near[c : c + 1]
-    late_ref[...] = rows[:, length - late_ref.shape[1] :]
-    done = correlate(rows, even, odd, table, length // LANE - extra, group)
-    for s in range(early_ref.shape[0]):
-        early_ref[s] = as_chunk(done, s, 2 * early_ref.shape[2] // LANE, group, pulses)
-
-
-def finish_kernel(index_ref, early_ref, late_ref, halo_ref, table, keep_ref, give_ref, rows, even, odd, *, group):
+    blocks, stack = length // LANE, rows.shape[1]
+    lay_out(rows, (echo_ref, other_ref), held, 0, blocks, group, None)
+    kept = late_ref.shape[0]
+    late_ref[...] = held[blocks * stack - kept :]
+    chunk = 2 * early_ref.shape[1] // LANE
+    done = correlate(held, table, index_ref[0] % 2 * chunk, chunk, stack)
+    early_ref[...] = jnp.concatenate(
+        [as_chunk(done, m, chunk, stack, group, pulses) for m in range(2)], axis=0
+    )
+
+
+def finish_kernel(
+    index_ref, early_ref, late_ref, halo_ref, other_ref, table,
+    near_ref, far_ref, first_ref, second_ref, rows, held, *, group, sections
+):
     pulses = halo_ref.shape[0]
-    span = late_ref.shape[1]
-    taps = rows.shape[1] - span
-    ready = early_ref.shape[0]
-    chunk = 2 * early_ref.shape[2]
-    sections = ready + span // chunk
     section = lax.rem(index_ref[0], sections)
-    has_next = index_ref[0] >= sections
-    rows[:, :span] = late_ref[...]
-    rows[:, span:] = jnp.zeros((2 * group, taps), F32)
-    for p in range(pulses):
-        far = jnp.where(has_next, halo_ref[p, :, :taps].astype(F32), 0.0)
-        for c in range(2):
-            rows[c * group + p : c * group + p + 1, span:] = far[c : c + 1]
-    done = correlate(rows, even, odd, table, span // LANE, group)
-    for s in range(sections):
-        stacked = early_ref[s] if s < ready else as_chunk(done, s - ready, chunk // LANE, group, pulses)
-        slot = section ^ s
-        far_chunk, other_core = slot // 2, slot % 2
-        place = far_chunk ^ 1 ^ (section % 2) ^ other_core
-
-        @pl.when(other_core == 0)
+    side, core = section // 2, section % 2
+    stack = rows.shape[1]
+    kept, taps = late_ref.shape[0], rows.shape[2]
+    held[:kept] = late_ref[...]
+    lay_out(rows, (halo_ref, other_ref), held, kept // stack, taps // LANE, group, index_ref[0] >= sections)
+    chunk = 2 * early_ref.shape[1] // LANE
+    done = correlate(held, table, core * chunk, chunk, stack)
+    early = early_ref[...]
+    late = jnp.concatenate([as_chunk(done, m, chunk, stack, group, pulses) for m in range(2)], axis=0)
+
+    def put(ref, is_late):
+        @pl.when(is_late)
         def _():
-            keep_ref[place] = stacked
-
-        @pl.when(other_core == 1)
+            ref[...] = late
+
+        @pl.when(jnp.logical_not(is_late))
         def _():
-            give_ref[place] = stacked
-
-
-def row_scratch(blocks, group):
-    return [
-        pltpu.VMEM((2 * group, blocks * LANE), F32),
-        pltpu.VMEM((blocks * group, 2 * LANE), BF16),
-        pltpu.VMEM((blocks * group, 2 * LANE), BF16),
-    ]
-
-
-def begin_compression(echo, chirp, sections, group):
+            ref[...] = early
+
+    put(near_ref, side == 1)
+    put(far_ref, side == 0)
+    put(first_ref, side == core)
+    put(second_ref, side != core)
+
+
+def begin_compression(section, echo, other, chirp, sections, group):
     _, _, length = echo.shape
     taps = chirp.shape[1]
-    chunk = length // sections
-    early = (length - taps) // chunk
+    chunk, stack = length // sections, 2 * group
     return pl.pallas_call(
         functools.partial(begin_kernel, group=group),
         out_shape=(
-            jax.ShapeDtypeStruct((early, 3 * group, chunk // 2), BF16),
-            jax.ShapeDtypeStruct((2 * group, length - early * chunk), F32),
+            jax.ShapeDtypeStruct((6 * group, chunk // 2), BF16),
+            jax.ShapeDtypeStruct((length // 2 // LANE * stack, 2 * LANE), BF16),
             jax.ShapeDtypeStruct(((taps // LANE + 1) * 2 * LANE, 2 * LANE), BF16),
         ),
-        scratch_shapes=row_scratch(length // LANE, group),
+        in_specs=[pl.BlockSpec(memory_space=pltpu.SMEM)] + [pl.BlockSpec(memory_space=pltpu.VMEM)] * 3,
+        scratch_shapes=[
+            pltpu.VMEM((2, stack, length), F32),
+            pltpu.VMEM((length // LANE * stack, 2 * LANE), BF16),
+        ],
         compiler_params=pltpu.CompilerParams(vmem_limit_bytes=24 * 1024 * 1024),
         name="begin_compression",
-    )(echo, chirp)
-
-
-def finish_compression(place, early, late, halo, table, group):
-    blocks = late.shape[1] // LANE + table.shape[0] // (2 * LANE) - 1
+    )(section, echo, other, chirp)
+
+
+def finish_compression(place, early, late, halo, other, table, sections, group):
+    stack, taps = 2 * group, table.shape[0] // 2 - LANE
     return pl.pallas_call(
-        functools.partial(finish_kernel, group=group),
-        out_shape=[jax.ShapeDtypeStruct((2, *early.shape[1:]), BF16)] * 2,
-        in_specs=[pl.BlockSpec(memory_space=pltpu.SMEM)] + [pl.BlockSpec(memory_space=pltpu.VMEM)] * 4,
-        scratch_shapes=row_scratch(blocks, group),
+        functools.partial(finish_kernel, group=group, sections=sections),
+        out_shape=[jax.ShapeDtypeStruct(early.shape, BF16)] * 4,
+        in_specs=[pl.BlockSpec(memory_space=pltpu.SMEM)] + [pl.BlockSpec(memory_space=pltpu.VMEM)] * 5,
+        scratch_shapes=[
+            pltpu.VMEM((2, stack, taps), F32),
+            pltpu.VMEM((late.shape[0] + taps // LANE * stack, 2 * LANE), BF16),
+        ],
         compiler_params=pltpu.CompilerParams(vmem_limit_bytes=24 * 1024 * 1024),
         name="finish_compression",
-    )(place, early, late, halo, table)
-
-
-def image_kernel(index_ref, operator_ref, both_ref, *refs, group):
+    )(place, early, late, halo, other, table)
+
+
+def image_kernel(operator_ref, *refs, group):
     chunks, (out_ref, parts, sems) = refs[:-3], refs[-3:]
     count, _, tile = parts.shape
-    width = both_ref.shape[2]
-    near = 1 - index_ref[0] % 2
-    held = [both_ref[near]] + [chunk[...] for chunk in chunks]
-    held = [value.astype(F32) for value in held]
+    width = chunks[0].shape[1]
+    held = [chunk[...].astype(F32) for chunk in chunks]
     copies = []
     for i in range(count):
         half, at = divmod(i * tile, width)
@@ -376,15 +377,14 @@
         copy.wait()
 
 
-def form_image(section, operator, both, chunks, group):
-    height, half = operator.shape[1], both.shape[2]
+def form_image(operator, chunks, group):
+    height, half = operator.shape[1], chunks[0].shape[1]
     tile = 256 if half % 256 == 0 else half
     count = 2 * half // tile
     return pl.pallas_call(
         functools.partial(image_kernel, group=group),
         out_shape=jax.ShapeDtypeStruct((height, 2 * half), BF16),
-        in_specs=[pl.BlockSpec(memory_space=pltpu.SMEM)]
-        + [pl.BlockSpec(memory_space=pltpu.VMEM)] * (2 + len(chunks)),
+        in_specs=[pl.BlockSpec(memory_space=pltpu.VMEM)] * (1 + len(chunks)),
         out_specs=pl.BlockSpec(memory_space=pl.ANY),
         scratch_shapes=[
             pltpu.VMEM((count, height, tile), BF16),
@@ -392,7 +392,7 @@
         ],
         compiler_params=pltpu.CompilerParams(vmem_limit_bytes=16 * 1024 * 1024),
         name="form_image",
-    )(section, operator, both, *chunks)
+    )(operator, *chunks)
 
 
 def swap(value, axis, by):
@@ -427,28 +427,29 @@
 
     echo = jnp.transpose(echoes[:, 0], (1, 0, 2))
     halo = from_next(echo, "rng")
+    other = swap(echo, "section", 1)
+    has_next = (lax.axis_index("rng") < lax.axis_size("rng") - 1).astype(jnp.int32)
     echo, chirp, packed = prepare(
         echo, chirp, coef, band_start, band_width, weights, pulse_order, sections, group
     )
-    has_next = (lax.axis_index("rng") < lax.axis_size("rng") - 1).astype(jnp.int32)
-    early, late, table = begin_compression(echo, chirp, sections, group)
+    packed_partner = swap(packed, "sub", 1) if subs == 2 else packed
+    halo, chirp = lax.optimization_barrier((halo, chirp))
+    early, late, table = begin_compression(section, echo, other, chirp, sections, group)
     place = section + sections * has_next
-    keep, give = finish_compression(place, early, late, halo, table, group)
-    give, packed = lax.optimization_barrier((give, packed))
-    both = jnp.concatenate([keep, swap(give, "section", 1)], axis=1)
-    packed_partner = swap(packed, "sub", 1) if subs == 2 else packed
-    far = lax.dynamic_index_in_dim(both, section[0] % 2, 0, keepdims=False)
+    near, far, first, second = finish_compression(
+        place, early, late, halo, swap(halo, "section", 1), table, sections, group
+    )
     if subs != 2:
-        near = lax.dynamic_index_in_dim(both, 1 - section[0] % 2, 0, keepdims=False)
         chunks = [near, swap(far, "section", 2)]
         return merge_images(section, chunks, packed, dims, sections, group, pulses_each)
     chunks = [
+        near,
         swap_by(far, lambda s, a: (s ^ 2, a ^ 1)),
-        swap_by(both[0], lambda s, a: (s, a ^ 1) if s % 2 else (s ^ 2, a)),
-        swap_by(both[1], lambda s, a: (s ^ 2, a) if s % 2 else (s, a ^ 1)),
+        swap_by(first, lambda s, a: (s, a ^ 1) if s % 2 else (s ^ 2, a)),
+        swap_by(second, lambda s, a: (s ^ 2, a) if s % 2 else (s, a ^ 1)),
     ]
     operator = fold_operator(section, packed, packed_partner, dims, sections, group, pulses_each)
-    image = form_image(section, operator, both, chunks, group)
+    image = form_image(operator, chunks, group)
     return image.reshape(2, beams, 1, image.shape[1])
 
 

time: 18.3 us -> 18.2 us (level)
  Pallas kernels: 5.21 us -> 5.43 us
    ppermute x2 -> x3, waiting for transfers between devices: 1.23 us -> 0.01 us  [swap(): return lax.ppermute(value, axis, [(i, i ^ by) for i in range(count)])]
    ppermute x1, waiting for transfers between devices: 0.19 us -> 1.25 us  [from_next(): lax.ppermute(value, axis, [(i, (i - 1) % count) for i in range(count)])]
    ppermute x2 -> x3, starting transfers between devices: 1.59 us -> 1.52 us  [swap(): return lax.ppermute(value, axis, [(i, i ^ by) for i in range(count)])]
  transfers between devices with their start and end apart: 6 -> 7, of which waited for: 5 -> 4; matrix products, arithmetic and copies ran while one was open for 0% -> 0% of each run, Pallas kernels for 20% -> 24%
where the time goes in v10:
time: 18.2 us; the launch traced here: 18.1 us
  starting transfers between devices  10.1 us (55%)
  Pallas kernels  5.43 us (30%)
  waiting for transfers between devices  2.49 us (14%)
    ppermute x1, starting transfers between devices, from_next(): lax.ppermute(value, axis, [(i, (i - 1) % count) for i in range(count)])  5.05 us
    ppermute x3, starting transfers between devices, swap_by(): return lax.ppermute(value, ('section', 'sub'), pairs)  3.55 us
    ppermute x3, starting transfers between devices, swap(): return lax.ppermute(value, axis, [(i, i ^ by) for i in range(count)])  1.52 us
    pallas_call x1, Pallas kernels, fold_operator(): pl.pallas_call(functools.partial(operator_kernel, dims=dims, sections=sec...  1.32 us
    pallas_call x1, Pallas kernels, prepare(): pl.pallas_call(functools.partial(prepare_kernel, sections=sections, group...  1.27 us
    ppermute x1, waiting for transfers between devices, from_next(): lax.ppermute(value, axis, [(i, (i - 1) % count) for i in range(count)])  1.25 us
    ppermute x3, waiting for transfers between devices, swap_by(): return lax.ppermute(value, ('section', 'sub'), pairs)  1.24 us
    pallas_call x1, Pallas kernels, begin_compression(): pl.pallas_call(functools.partial(begin_kernel, group=group), out_shape=(j...  1.19 us
  transfers between devices with their start and end apart: 7, of which 4 were waited for; matrix products, arithmetic and copies ran while one was open for 0% of the time, Pallas kernels for 24%

profile of v10, /device:TPU:0, one launch (start us, length us, event | category | flops | bytes accessed | tf_op | source)
XLA Modules:
  0.0 18.1 jit_solution(8228476714872460421)
XLA Ops:
  0.0 5.0 %collective-permute-start.2 = (bf16[6,2,4096]{2,1,0:T(2,128)(2,1)}, bf16[6,2,4096]{2,1,0:T(2,128)(2,1)S(1)}, u32[]{:S(2)}, u32[]{:S(2)}) collective-permute-start(bf16[6,2,4096]{2,1,0:T(2,128)(2,1)} %bitcast.10), channel_id=1, source_target_pairs={{0,3},{1,0},{2,1},{3,2},{4,7},{5,4},{6,5},{7,6},{8,11},{9,8},{10,9... | collective-permute-start | bytes 294920 | tf_op jit(solution)/shard_map/ppermute | solution.py:415
  5.0 0.0 collective-permute-start.1
  5.1 1.3 %prepare.1 = (bf16[6,2,4096]{2,1,0:T(2,128)(2,1)S(1)}, bf16[2,2048]{1,0:T(2,128)(2,1)S(1)}, bf16[400,128]{1,0:T(8,128)(2,1)S(1)}) custom-call(bf16[6,2,4096]{2,1,0:T(2,128)(2,1)} %bitcast.12, bf16[5,1,2,2,16,128]{5,4,3,2,1,0:T(8,128)(2,1)} %bitcast.13, s32[5,1,2,128]{3,2,1,0:T(2,128)} %refs_2_.1, s32[5,1,2,128]{3,2,1,0:T(2,128)} %refs_3_.1, ...), custom_call_target="tpu_custom_call" | custom-call | tf_op jit(solution)/shard_map/prepare/pallas_call | solution.py:72
  6.3 1.2 %collective-permute-done.2.halo_ref = bf16[6,2,4096]{2,1,0:T(2,128)(2,1)S(1)} collective-permute-done((bf16[6,2,4096]{2,1,0:T(2,128)(2,1)}, bf16[6,2,4096]{2,1,0:T(2,128)(2,1)S(1)}, u32[]{:S(2)}, u32[]{:S(2)}) %collective-permute-start.2) | collective-permute-done | bytes 98336 | tf_op jit(solution)/shard_map/ppermute | solution.py:415
  7.6 0.0 collective-permute-start.3
  7.6 1.5 %collective-permute-start = (bf16[400,128]{1,0:T(8,128)(2,1)S(1)}, bf16[400,128]{1,0:T(8,128)(2,1)S(1)}, u32[]{:S(2)}, u32[]{:S(2)}) collective-permute-start(bf16[400,128]{1,0:T(8,128)(2,1)S(1)} %get-tuple-element.17.own_ref), channel_id=1, source_target_pairs={{0,4},{4,0},{1,5},{5,1},{2,6},{6,2},{3,7},{7,3},{8,12},{12,8},{9,1... | collective-permute-start | bytes 307208 | tf_op jit(solution)/shard_map/ppermute | solution.py:400
  9.1 0.0 collective-permute-done.1.other_ref
  9.1 1.2 %begin_compression.1 = (bf16[48,512]{1,0:T(8,128)(2,1)S(1)}, bf16[256,256]{1,0:T(8,128)(2,1)S(1)}, bf16[4352,256]{1,0:T(8,128)(2,1)S(1)}) custom-call(s32[1]{0:T(128)} %bitcast.index_ref, bf16[6,2,4096]{2,1,0:T(2,128)(2,1)S(1)} %get-tuple-element.18.echo_ref, bf16[6,2,4096]{2,1,0:T(2,128)(2,1)S(1)} %collective-permute-done.1.other_ref, ...), custom_call_target="tpu_custom_call" | custom-call | tf_op jit(solution)/shard_map/begin_compression/pallas_call | solution.py:323
  10.3 0.0 collective-permute-done.3.other_ref
  10.3 0.6 %finish_compression.1 = (bf16[48,512]{1,0:T(8,128)(2,1)S(1)}, bf16[48,512]{1,0:T(8,128)(2,1)S(1)}, bf16[48,512]{1,0:T(8,128)(2,1)S(1)}, bf16[48,512]{1,0:T(8,128)(2,1)S(1)}) custom-call(s32[1]{0:T(128)S(6)} %add.7.index_ref, bf16[48,512]{1,0:T(8,128)(2,1)S(1)} %get-tuple-element.21.early_ref, bf16[256,256]{1,0:T(8,128)(2,1)S(1)} %get-tuple-element.22.late_ref, ...), custom_call_target="tpu_custom_call" | custom-call | tf_op jit(solution)/shard_map/finish_compression/pallas_call | solution.py:342
  10.9 1.5 %collective-permute-start.4 = (bf16[48,512]{1,0:T(8,128)(2,1)S(1)}, bf16[48,512]{1,0:T(8,128)(2,1)S(1)}, u32[]{:S(2)}, u32[]{:S(2)}) collective-permute-start(bf16[48,512]{1,0:T(8,128)(2,1)S(1)} %get-tuple-element.26), channel_id=1, source_target_pairs={{0,20},{4,16},{8,28},{12,24},{16,4},{20,0},{24,12},{28,8},{1,21},{... | collective-permute-start | bytes 147464 | tf_op jit(solution)/shard_map/ppermute | solution.py:410
  12.4 0.5 %collective-permute-start.5 = (bf16[48,512]{1,0:T(8,128)(2,1)S(1)}, bf16[48,512]{1,0:T(8,128)(2,1)S(1)}, u32[]{:S(2)}, u32[]{:S(2)}) collective-permute-start(bf16[48,512]{1,0:T(8,128)(2,1)S(1)} %get-tuple-element.27), channel_id=1, source_target_pairs={{0,16},{4,20},{8,12},{12,8},{16,0},{20,4},{24,28},{28,24},{1,17},{... | collective-permute-start | bytes 147464 | tf_op jit(solution)/shard_map/ppermute | solution.py:410
  12.9 1.5 %collective-permute-start.6 = (bf16[48,512]{1,0:T(8,128)(2,1)S(1)}, bf16[48,512]{1,0:T(8,128)(2,1)S(1)}, u32[]{:S(2)}, u32[]{:S(2)}) collective-permute-start(bf16[48,512]{1,0:T(8,128)(2,1)S(1)} %get-tuple-element.28), channel_id=1, source_target_pairs={{0,4},{4,0},{8,24},{12,28},{16,20},{20,16},{24,8},{28,12},{1,5},{5... | collective-permute-start | bytes 147464 | tf_op jit(solution)/shard_map/ppermute | solution.py:410
  14.5 0.0 collective-permute-done.partner_ref
  14.5 1.3 %fold_operator.1.operator_ref = bf16[2,256,256]{2,1,0:T(8,128)(2,1)S(1)} custom-call(s32[1]{0:T(128)} %bitcast.index_ref, bf16[400,128]{1,0:T(8,128)(2,1)S(1)} %get-tuple-element.17.own_ref, bf16[400,128]{1,0:T(8,128)(2,1)S(1)} %collective-permute-done.partner_ref), custom_call_target="tpu_custom_call" | custom-call | tf_op jit(solution)/shard_map/fold_operator/pallas_call | solution.py:188
  15.8 0.2 %collective-permute-done.4.refs_1_ = bf16[48,512]{1,0:T(8,128)(2,1)S(1)} collective-permute-done((bf16[48,512]{1,0:T(8,128)(2,1)S(1)}, bf16[48,512]{1,0:T(8,128)(2,1)S(1)}, u32[]{:S(2)}, u32[]{:S(2)}) %collective-permute-start.4) | collective-permute-done | bytes 49184 | tf_op jit(solution)/shard_map/ppermute | solution.py:410
  16.0 0.8 %collective-permute-done.5.refs_2_ = bf16[48,512]{1,0:T(8,128)(2,1)S(1)} collective-permute-done((bf16[48,512]{1,0:T(8,128)(2,1)S(1)}, bf16[48,512]{1,0:T(8,128)(2,1)S(1)}, u32[]{:S(2)}, u32[]{:S(2)}) %collective-permute-start.5) | collective-permute-done | bytes 49184 | tf_op jit(solution)/shard_map/ppermute | solution.py:410
  16.8 0.2 %collective-permute-done.6.refs_3_ = bf16[48,512]{1,0:T(8,128)(2,1)S(1)} collective-permute-done((bf16[48,512]{1,0:T(8,128)(2,1)S(1)}, bf16[48,512]{1,0:T(8,128)(2,1)S(1)}, u32[]{:S(2)}, u32[]{:S(2)}) %collective-permute-start.6) | collective-permute-done | bytes 49184 | tf_op jit(solution)/shard_map/ppermute | solution.py:410
  17.0 1.1 %form_image.1 = bf16[256,1024]{1,0:T(8,128)(2,1)} custom-call(bf16[2,256,256]{2,1,0:T(8,128)(2,1)S(1)} %fold_operator.1.operator_ref, bf16[48,512]{1,0:T(8,128)(2,1)S(1)} %get-tuple-element.25.refs_0_, bf16[48,512]{1,0:T(8,128)(2,1)S(1)} %collective-permute-done.4.refs_1_, bf16[48,512]{1,0:T(8,128)(2,1)S(1)} %collective-permute-done.5.refs_2_, ...), custom_call_target="tpu_custom_call" | custom-call | tf_op jit(solution)/shard_map/form_image/pallas_call | solution.py:384
Async XLA Ops:
  0.0 7.6 %collective-permute-start.2 = (bf16[6,2,4096]{2,1,0:T(2,128)(2,1)}, bf16[6,2,4096]{2,1,0:T(2,128)(2,1)S(1)}, u32[]{:S(2)}, u32[]{:S(2)}) collective-permute-start(bf16[6,2,4096]{2,1,0:T(2,128)(2,1)} %bitcast.10), channel_id=1, source_target_pairs={{0,3},{1,0},{2,1},{3,2},{4,7},{5,4},{6,5},{7,6},{8,11},{9,8},{10,9... | collective-permute-start | bytes 294920 | tf_op jit(solution)/shard_map/ppermute | solution.py:415
  5.0 4.1 %collective-permute-start.1 = (bf16[6,2,4096]{2,1,0:T(2,128)(2,1)}, bf16[6,2,4096]{2,1,0:T(2,128)(2,1)S(1)}, u32[]{:S(2)}, u32[]{:S(2)}) collective-permute-start(bf16[6,2,4096]{2,1,0:T(2,128)(2,1)} %bitcast.11), channel_id=1, source_target_pairs={{0,8},{8,0},{16,24},{24,16},{1,9},{9,1},{17,25},{25,17},{2,10},{10... | collective-permute-start | bytes 294920 | tf_op jit(solution)/shard_map/ppermute | solution.py:400
  7.6 2.7 %collective-permute-start.3 = (bf16[6,2,4096]{2,1,0:T(2,128)(2,1)S(1)}, bf16[6,2,4096]{2,1,0:T(2,128)(2,1)S(1)}, u32[]{:S(2)}, u32[]{:S(2)}) collective-permute-start(bf16[6,2,4096]{2,1,0:T(2,128)(2,1)S(1)} %collective-permute-done.2.halo_ref), channel_id=1, source_target_pairs={{0,8},{8,0},{16,24},{24,16},{1,9},{9,1},{17,25},{25,17},{2,10},{10... | collective-permute-start | bytes 294920 | tf_op jit(solution)/shard_map/ppermute | solution.py:400
  7.6 6.9 %collective-permute-start = (bf16[400,128]{1,0:T(8,128)(2,1)S(1)}, bf16[400,128]{1,0:T(8,128)(2,1)S(1)}, u32[]{:S(2)}, u32[]{:S(2)}) collective-permute-start(bf16[400,128]{1,0:T(8,128)(2,1)S(1)} %get-tuple-element.17.own_ref), channel_id=1, source_target_pairs={{0,4},{4,0},{1,5},{5,1},{2,6},{6,2},{3,7},{7,3},{8,12},{12,8},{9,1... | collective-permute-start | bytes 307208 | tf_op jit(solution)/shard_map/ppermute | solution.py:400
  10.9 5.1 %collective-permute-start.4 = (bf16[48,512]{1,0:T(8,128)(2,1)S(1)}, bf16[48,512]{1,0:T(8,128)(2,1)S(1)}, u32[]{:S(2)}, u32[]{:S(2)}) collective-permute-start(bf16[48,512]{1,0:T(8,128)(2,1)S(1)} %get-tuple-element.26), channel_id=1, source_target_pairs={{0,20},{4,16},{8,28},{12,24},{16,4},{20,0},{24,12},{28,8},{1,21},{... | collective-permute-start | bytes 147464 | tf_op jit(solution)/shard_map/ppermute | solution.py:410
  12.4 4.4 %collective-permute-start.5 = (bf16[48,512]{1,0:T(8,128)(2,1)S(1)}, bf16[48,512]{1,0:T(8,128)(2,1)S(1)}, u32[]{:S(2)}, u32[]{:S(2)}) collective-permute-start(bf16[48,512]{1,0:T(8,128)(2,1)S(1)} %get-tuple-element.27), channel_id=1, source_target_pairs={{0,16},{4,20},{8,12},{12,8},{16,0},{20,4},{24,28},{28,24},{1,17},{... | collective-permute-start | bytes 147464 | tf_op jit(solution)/shard_map/ppermute | solution.py:410
  12.9 4.1 %collective-permute-start.6 = (bf16[48,512]{1,0:T(8,128)(2,1)S(1)}, bf16[48,512]{1,0:T(8,128)(2,1)S(1)}, u32[]{:S(2)}, u32[]{:S(2)}) collective-permute-start(bf16[48,512]{1,0:T(8,128)(2,1)S(1)} %get-tuple-element.28), channel_id=1, source_target_pairs={{0,4},{4,0},{8,24},{12,28},{16,20},{20,16},{24,8},{28,12},{1,5},{5... | collective-permute-start | bytes 147464 | tf_op jit(solution)/shard_map/ppermute | solution.py:410

commit v11 on v7

--- a/solution.py
+++ b/solution.py
@@ -280,18 +280,22 @@
         early_ref[s] = as_chunk(done, s, 2 * early_ref.shape[2] // LANE, group, pulses)
 
 
-def finish_kernel(index_ref, early_ref, late_ref, halo_ref, table, keep_ref, give_ref, rows, even, odd, *, group):
+def finish_kernel(
+    index_ref, early_ref, late_ref, odd_halo_ref, halo_ref, table, keep_ref, give_ref, rows, even, odd, *, group
+):
     pulses = halo_ref.shape[0]
     span = late_ref.shape[1]
     taps = rows.shape[1] - span
     ready = early_ref.shape[0]
     chunk = 2 * early_ref.shape[2]
     sections = ready + span // chunk
-    section = index_ref[0]
+    section = lax.rem(index_ref[0], sections)
+    kind = index_ref[0] // sections
     rows[:, :span] = late_ref[...]
     rows[:, span:] = jnp.zeros((2 * group, taps), F32)
     for p in range(pulses):
-        far = halo_ref[p, :, :taps].astype(F32)
+        far = jnp.where(kind == 1, halo_ref[p, :, :taps].astype(F32), 0.0)
+        far = jnp.where(kind == 2, odd_halo_ref[p, :, :taps].astype(F32), far)
         for c in range(2):
             rows[c * group + p : c * group + p + 1, span:] = far[c : c + 1]
     done = correlate(rows, even, odd, table, span // LANE, group)
@@ -336,16 +340,16 @@
     )(echo, chirp)
 
 
-def finish_compression(section, early, late, halo, table, group):
+def finish_compression(place, early, late, halos, table, group):
     blocks = late.shape[1] // LANE + table.shape[0] // (2 * LANE) - 1
     return pl.pallas_call(
         functools.partial(finish_kernel, group=group),
         out_shape=[jax.ShapeDtypeStruct((2, *early.shape[1:]), BF16)] * 2,
-        in_specs=[pl.BlockSpec(memory_space=pltpu.SMEM)] + [pl.BlockSpec(memory_space=pltpu.VMEM)] * 4,
+        in_specs=[pl.BlockSpec(memory_space=pltpu.SMEM)] + [pl.BlockSpec(memory_space=pltpu.VMEM)] * 5,
         scratch_shapes=row_scratch(blocks, group),
         compiler_params=pltpu.CompilerParams(vmem_limit_bytes=24 * 1024 * 1024),
         name="finish_compression",
-    )(section, early, late, halo, table)
+    )(place, early, late, *halos, table)
 
 
 def image_kernel(index_ref, operator_ref, both_ref, *refs, group):
@@ -410,7 +414,12 @@
 
 
 def from_next(value, axis):
-    return lax.ppermute(value, axis, [(i, i - 1) for i in range(1, lax.axis_size(axis))])
+    count = lax.axis_size(axis)
+    results = []
+    for parity in (0, 1):
+        peers = [min(max(((i + parity) ^ 1) - parity, 0), count - 1) for i in range(count)]
+        results.append(lax.ppermute(value, axis, list(enumerate(peers))))
+    return results[::-1]
 
 
 def on_device(echoes, chirp, steer, pulse_order, band_coef, band_start, band_width):
@@ -424,14 +433,17 @@
     dims = (levels, sides, parts, taps, beams)
 
     echo = jnp.transpose(echoes[:, 0], (1, 0, 2))
-    halo = from_next(echo, "rng")
+    halos = from_next(echo, "rng")
     echo, chirp, packed = prepare(
         echo, chirp, coef, band_start, band_width, weights, pulse_order, sections, group
     )
+    rng, last = lax.axis_index("rng").astype(jnp.int32), lax.axis_size("rng") - 1
+    kind = jnp.where(rng < last, 1 + rng % 2, 0)
     if subs == 2:
         packed_partner = swap(packed, "sub", 1)
     early, late, table = begin_compression(echo, chirp, sections, group)
-    keep, give = finish_compression(section, early, late, halo, table, group)
+    place = section + sections * kind
+    keep, give = finish_compression(place, early, late, halos, table, group)
     both = jnp.concatenate([keep, swap(give, "section", 1)], axis=1)
     far = lax.dynamic_index_in_dim(both, section[0] % 2, 0, keepdims=False)
     if subs != 2:

time: 18.4 us -> 19.7 us (1.071)
  starting transfers between devices: 7.94 us -> 11.8 us
  waiting for transfers between devices: 4.96 us -> 2.45 us
    ppermute x1 -> x2, starting transfers between devices: 1.28 us -> 6.57 us  [from_next(): results.append(lax.ppermute(value, axis, list(enumerate(peers))))]
    ppermute x2, starting transfers between devices: 3.1 us -> 1.66 us  [swap(): return lax.ppermute(value, axis, [(i, i ^ by) for i in range(count)])]
    ppermute x1 -> x2, waiting for transfers between devices: 1.27 us -> 0.01 us  [from_next(): results.append(lax.ppermute(value, axis, list(enumerate(peers))))]
    ppermute x3, waiting for transfers between devices: 2.49 us -> 1.24 us  [swap_by(): return lax.ppermute(value, ('section', 'sub'), pairs)]
  transfers between devices with their start and end apart: 6 -> 7, of which waited for: 5 -> 4; matrix products, arithmetic and copies ran while one was open for 0% -> 0% of each run, Pallas kernels for 23% -> 21%
where the time goes in v11:
time: 19.7 us; the launch traced here: 19.5 us
  starting transfers between devices  11.8 us (60%)
  Pallas kernels  5.21 us (26%)
  waiting for transfers between devices  2.45 us (12%)
    ppermute x2, starting transfers between devices, from_next(): results.append(lax.ppermute(value, axis, list(enumerate(peers))))  6.57 us
    ppermute x3, starting transfers between devices, swap_by(): return lax.ppermute(value, ('section', 'sub'), pairs)  3.55 us
    ppermute x2, starting transfers between devices, swap(): return lax.ppermute(value, axis, [(i, i ^ by) for i in range(count)])  1.66 us
    pallas_call x1, Pallas kernels, fold_operator(): pl.pallas_call(functools.partial(operator_kernel, dims=dims, sections=sec...  1.32 us
    pallas_call x1, Pallas kernels, prepare(): pl.pallas_call(functools.partial(prepare_kernel, sections=sections, group...  1.27 us
    ppermute x3, waiting for transfers between devices, swap_by(): return lax.ppermute(value, ('section', 'sub'), pairs)  1.24 us
    ppermute x2, waiting for transfers between devices, swap(): return lax.ppermute(value, axis, [(i, i ^ by) for i in range(count)])  1.21 us
    pallas_call x1, Pallas kernels, form_image(): pl.pallas_call(functools.partial(image_kernel, group=group), out_shape=ja...  1.06 us
  transfers between devices with their start and end apart: 7, of which 4 were waited for; matrix products, arithmetic and copies ran while one was open for 0% of the time, Pallas kernels for 21%

profile of v11, /device:TPU:0, one launch (start us, length us, event | category | flops | bytes accessed | tf_op | source)
XLA Modules:
  0.0 19.5 jit_solution(14395095097119941252)
XLA Ops:
  0.0 1.5 %collective-permute-start.1 = (bf16[6,2,4096]{2,1,0:T(2,128)(2,1)}, bf16[6,2,4096]{2,1,0:T(2,128)(2,1)S(1)}, u32[]{:S(2)}, u32[]{:S(2)}) collective-permute-start(bf16[6,2,4096]{2,1,0:T(2,128)(2,1)} %bitcast.16), channel_id=1, source_target_pairs={{0,0},{1,2},{2,1},{3,3},{4,4},{5,6},{6,5},{7,7},{8,8},{9,10},{10,9... | collective-permute-start | bytes 294920 | tf_op jit(solution)/shard_map/ppermute | solution.py:421
  1.5 5.0 %collective-permute-start.2 = (bf16[6,2,4096]{2,1,0:T(2,128)(2,1)}, bf16[6,2,4096]{2,1,0:T(2,128)(2,1)S(1)}, u32[]{:S(2)}, u32[]{:S(2)}) collective-permute-start(bf16[6,2,4096]{2,1,0:T(2,128)(2,1)} %bitcast.17), channel_id=1, source_target_pairs={{0,1},{1,0},{2,3},{3,2},{4,5},{5,4},{6,7},{7,6},{8,9},{9,8},{10,11... | collective-permute-start | bytes 294920 | tf_op jit(solution)/shard_map/ppermute | solution.py:421
  6.6 1.3 %prepare.1 = (bf16[6,2,4096]{2,1,0:T(2,128)(2,1)S(1)}, bf16[2,2048]{1,0:T(2,128)(2,1)S(1)}, bf16[400,128]{1,0:T(8,128)(2,1)S(1)}) custom-call(bf16[6,2,4096]{2,1,0:T(2,128)(2,1)} %bitcast.18, bf16[5,1,2,2,16,128]{5,4,3,2,1,0:T(8,128)(2,1)} %bitcast.19, s32[5,1,2,128]{3,2,1,0:T(2,128)} %refs_2_.1, s32[5,1,2,128]{3,2,1,0:T(2,128)} %refs_3_.1, ...), custom_call_target="tpu_custom_call" | custom-call | tf_op jit(solution)/shard_map/prepare/pallas_call | solution.py:72
  7.8 1.6 %collective-permute-start = (bf16[400,128]{1,0:T(8,128)(2,1)S(1)}, bf16[400,128]{1,0:T(8,128)(2,1)S(1)}, u32[]{:S(2)}, u32[]{:S(2)}) collective-permute-start(bf16[400,128]{1,0:T(8,128)(2,1)S(1)} %get-tuple-element.13.own_ref), channel_id=1, source_target_pairs={{0,4},{4,0},{1,5},{5,1},{2,6},{6,2},{3,7},{7,3},{8,12},{12,8},{9,1... | collective-permute-start | bytes 307208 | tf_op jit(solution)/shard_map/ppermute | solution.py:403
  9.4 1.0 %begin_compression.1 = (bf16[2,24,512]{2,1,0:T(8,128)(2,1)S(1)}, f32[16,2048]{1,0:T(8,128)S(1)}, bf16[4352,256]{1,0:T(8,128)(2,1)S(1)}) custom-call(bf16[6,2,4096]{2,1,0:T(2,128)(2,1)S(1)} %get-tuple-element.14.echo_ref, bf16[2,2048]{1,0:T(2,128)(2,1)S(1)} %get-tuple-element.15.chirp_ref), custom_call_target="tpu_custom_call" | custom-call | tf_op jit(solution)/shard_map/begin_compression/pallas_call | solution.py:330
  10.5 0.0 collective-permute-done.1.odd_halo_ref
  10.5 0.0 collective-permute-done.2.halo_ref
  10.5 0.5 %finish_compression.1 = (bf16[2,24,512]{2,1,0:T(8,128)(2,1)S(1)}, bf16[2,24,512]{2,1,0:T(8,128)(2,1)S(1)}) custom-call(s32[1]{0:T(128)S(6)} %add.19.index_ref, bf16[2,24,512]{2,1,0:T(8,128)(2,1)S(1)} %get-tuple-element.16.early_ref, f32[16,2048]{1,0:T(8,128)S(1)} %get-tuple-element.17.late_ref, bf16[6,2,4096]{2,1,0:T(2,128)(2,1)S(1)} %collective-permute-done.1.odd_halo_ref, ...), custom_call_target="tpu_custom_call" | custom-call | tf_op jit(solution)/shard_map/finish_compression/pallas_call | solution.py:345
  11.0 0.1 collective-permute-start.3
  11.1 1.2 %collective-permute-done.3 = bf16[2,24,512]{2,1,0:T(8,128)(2,1)S(1)} collective-permute-done((bf16[2,24,512]{2,1,0:T(8,128)(2,1)S(1)}, bf16[2,24,512]{2,1,0:T(8,128)(2,1)S(1)}, u32[]{:S(2)}, u32[]{:S(2)}) %collective-permute-start.3) | collective-permute-done | bytes 49184 | tf_op jit(solution)/shard_map/ppermute | solution.py:403
  12.3 1.5 %collective-permute-start.4 = (bf16[48,512]{1,0:T(8,128)(2,1)S(1)}, bf16[48,512]{1,0:T(8,128)(2,1)S(1)}, u32[]{:S(2)}, u32[]{:S(2)}) collective-permute-start(bf16[48,512]{1,0:T(8,128)(2,1)S(1)} %get-tuple-element.23), channel_id=1, source_target_pairs={{0,20},{4,16},{8,28},{12,24},{16,4},{20,0},{24,12},{28,8},{1,21},{... | collective-permute-start | bytes 147464 | tf_op jit(solution)/shard_map/ppermute | solution.py:413
  13.8 0.5 %collective-permute-start.5 = (bf16[48,512]{1,0:T(8,128)(2,1)S(1)}, bf16[48,512]{1,0:T(8,128)(2,1)S(1)}, u32[]{:S(2)}, u32[]{:S(2)}) collective-permute-start(bf16[48,512]{1,0:T(8,128)(2,1)S(1)} %get-tuple-element.22), channel_id=1, source_target_pairs={{0,16},{4,20},{8,12},{12,8},{16,0},{20,4},{24,28},{28,24},{1,17},{... | collective-permute-start | bytes 147464 | tf_op jit(solution)/shard_map/ppermute | solution.py:413
  14.4 1.5 %collective-permute-start.6 = (bf16[48,512]{1,0:T(8,128)(2,1)S(1)}, bf16[48,512]{1,0:T(8,128)(2,1)S(1)}, u32[]{:S(2)}, u32[]{:S(2)}) collective-permute-start(bf16[48,512]{1,0:T(8,128)(2,1)S(1)} %get-tuple-element.21), channel_id=1, source_target_pairs={{0,4},{4,0},{8,24},{12,28},{16,20},{20,16},{24,8},{28,12},{1,5},{5... | collective-permute-start | bytes 147464 | tf_op jit(solution)/shard_map/ppermute | solution.py:413
  15.9 0.0 collective-permute-done.partner_ref
  15.9 1.3 %fold_operator.1.operator_ref = bf16[2,256,256]{2,1,0:T(8,128)(2,1)S(1)} custom-call(s32[1]{0:T(128)} %bitcast.index_ref, bf16[400,128]{1,0:T(8,128)(2,1)S(1)} %get-tuple-element.13.own_ref, bf16[400,128]{1,0:T(8,128)(2,1)S(1)} %collective-permute-done.partner_ref), custom_call_target="tpu_custom_call" | custom-call | tf_op jit(solution)/shard_map/fold_operator/pallas_call | solution.py:188
  17.2 0.2 %collective-permute-done.4.refs_0_ = bf16[48,512]{1,0:T(8,128)(2,1)S(1)} collective-permute-done((bf16[48,512]{1,0:T(8,128)(2,1)S(1)}, bf16[48,512]{1,0:T(8,128)(2,1)S(1)}, u32[]{:S(2)}, u32[]{:S(2)}) %collective-permute-start.4) | collective-permute-done | bytes 49184 | tf_op jit(solution)/shard_map/ppermute | solution.py:413
  17.5 0.9 %collective-permute-done.5.refs_1_ = bf16[48,512]{1,0:T(8,128)(2,1)S(1)} collective-permute-done((bf16[48,512]{1,0:T(8,128)(2,1)S(1)}, bf16[48,512]{1,0:T(8,128)(2,1)S(1)}, u32[]{:S(2)}, u32[]{:S(2)}) %collective-permute-start.5) | collective-permute-done | bytes 49184 | tf_op jit(solution)/shard_map/ppermute | solution.py:413
  18.3 0.2 collective-permute-done.6.refs_2_
  18.5 1.1 %form_image.1 = bf16[256,1024]{1,0:T(8,128)(2,1)} custom-call(s32[1]{0:T(128)} %bitcast.index_ref, bf16[2,256,256]{2,1,0:T(8,128)(2,1)S(1)} %fold_operator.1.operator_ref, bf16[2,48,512]{2,1,0:T(8,128)(2,1)S(1)} %constant_dynamic-update-slice_fusion.both_ref, bf16[48,512]{1,0:T(8,128)(2,1)S(1)} %collective-permute-done.4.refs_0_, ...), custom_call_target="tpu_custom_call" | custom-call | tf_op jit(solution)/shard_map/form_image/pallas_call | solution.py:386
  (3 shorter events, 0.0 us)
Async XLA Ops:
  0.0 10.5 %collective-permute-start.1 = (bf16[6,2,4096]{2,1,0:T(2,128)(2,1)}, bf16[6,2,4096]{2,1,0:T(2,128)(2,1)S(1)}, u32[]{:S(2)}, u32[]{:S(2)}) collective-permute-start(bf16[6,2,4096]{2,1,0:T(2,128)(2,1)} %bitcast.16), channel_id=1, source_target_pairs={{0,0},{1,2},{2,1},{3,3},{4,4},{5,6},{6,5},{7,7},{8,8},{9,10},{10,9... | collective-permute-start | bytes 294920 | tf_op jit(solution)/shard_map/ppermute | solution.py:421
  1.5 9.0 %collective-permute-start.2 = (bf16[6,2,4096]{2,1,0:T(2,128)(2,1)}, bf16[6,2,4096]{2,1,0:T(2,128)(2,1)S(1)}, u32[]{:S(2)}, u32[]{:S(2)}) collective-permute-start(bf16[6,2,4096]{2,1,0:T(2,128)(2,1)} %bitcast.17), channel_id=1, source_target_pairs={{0,1},{1,0},{2,3},{3,2},{4,5},{5,4},{6,7},{7,6},{8,9},{9,8},{10,11... | collective-permute-start | bytes 294920 | tf_op jit(solution)/shard_map/ppermute | solution.py:421
  7.8 8.1 %collective-permute-start = (bf16[400,128]{1,0:T(8,128)(2,1)S(1)}, bf16[400,128]{1,0:T(8,128)(2,1)S(1)}, u32[]{:S(2)}, u32[]{:S(2)}) collective-permute-start(bf16[400,128]{1,0:T(8,128)(2,1)S(1)} %get-tuple-element.13.own_ref), channel_id=1, source_target_pairs={{0,4},{4,0},{1,5},{5,1},{2,6},{6,2},{3,7},{7,3},{8,12},{12,8},{9,1... | collective-permute-start | bytes 307208 | tf_op jit(solution)/shard_map/ppermute | solution.py:403
  11.0 1.3 %collective-permute-start.3 = (bf16[2,24,512]{2,1,0:T(8,128)(2,1)S(1)}, bf16[2,24,512]{2,1,0:T(8,128)(2,1)S(1)}, u32[]{:S(2)}, u32[]{:S(2)}) collective-permute-start(bf16[2,24,512]{2,1,0:T(8,128)(2,1)S(1)} %get-tuple-element.20), channel_id=1, source_target_pairs={{0,8},{8,0},{16,24},{24,16},{1,9},{9,1},{17,25},{25,17},{2,10},{10... | collective-permute-start | bytes 147464 | tf_op jit(solution)/shard_map/ppermute | solution.py:403
  12.3 5.1 %collective-permute-start.4 = (bf16[48,512]{1,0:T(8,128)(2,1)S(1)}, bf16[48,512]{1,0:T(8,128)(2,1)S(1)}, u32[]{:S(2)}, u32[]{:S(2)}) collective-permute-start(bf16[48,512]{1,0:T(8,128)(2,1)S(1)} %get-tuple-element.23), channel_id=1, source_target_pairs={{0,20},{4,16},{8,28},{12,24},{16,4},{20,0},{24,12},{28,8},{1,21},{... | collective-permute-start | bytes 147464 | tf_op jit(solution)/shard_map/ppermute | solution.py:413
  13.8 4.5 %collective-permute-start.5 = (bf16[48,512]{1,0:T(8,128)(2,1)S(1)}, bf16[48,512]{1,0:T(8,128)(2,1)S(1)}, u32[]{:S(2)}, u32[]{:S(2)}) collective-permute-start(bf16[48,512]{1,0:T(8,128)(2,1)S(1)} %get-tuple-element.22), channel_id=1, source_target_pairs={{0,16},{4,20},{8,12},{12,8},{16,0},{20,4},{24,28},{28,24},{1,17},{... | collective-permute-start | bytes 147464 | tf_op jit(solution)/shard_map/ppermute | solution.py:413
  14.4 4.1 %collective-permute-start.6 = (bf16[48,512]{1,0:T(8,128)(2,1)S(1)}, bf16[48,512]{1,0:T(8,128)(2,1)S(1)}, u32[]{:S(2)}, u32[]{:S(2)}) collective-permute-start(bf16[48,512]{1,0:T(8,128)(2,1)S(1)} %get-tuple-element.21), channel_id=1, source_target_pairs={{0,4},{4,0},{8,24},{12,28},{16,20},{20,16},{24,8},{28,12},{1,5},{5... | collective-permute-start | bytes 147464 | tf_op jit(solution)/shard_map/ppermute | solution.py:413

commit v12 on v10

--- a/solution.py
+++ b/solution.py
@@ -247,8 +247,7 @@
     return jnp.concatenate([lead[:, :middle], lead[:, middle:], rest], axis=0).astype(BF16)
 
 
-def begin_kernel(index_ref, echo_ref, other_ref, chirp_ref, early_ref, late_ref, table, rows, held, *, group):
-    pulses, _, length = echo_ref.shape
+def table_kernel(chirp_ref, table):
     extra = chirp_ref.shape[1] // LANE
     reverse = LANE - 1 - lax.broadcasted_iota(jnp.int32, (2, LANE), 1)
     below = lax.broadcasted_iota(jnp.int32, (LANE, LANE), 1) <= lax.broadcasted_iota(
@@ -274,6 +273,10 @@
         table[at : at + LANE, LANE:] = (-imag).astype(BF16)
         table[at + LANE : at + 2 * LANE, :LANE] = imag.astype(BF16)
         table[at + LANE : at + 2 * LANE, LANE:] = real.astype(BF16)
+
+
+def begin_kernel(index_ref, echo_ref, other_ref, table, early_ref, late_ref, rows, held, *, group):
+    pulses, _, length = echo_ref.shape
     blocks, stack = length // LANE, rows.shape[1]
     lay_out(rows, (echo_ref, other_ref), held, 0, blocks, group, None)
     kept = late_ref.shape[0]
@@ -316,16 +319,24 @@
     put(second_ref, side != core)
 
 
-def begin_compression(section, echo, other, chirp, sections, group):
+def lag_tables(chirp):
+    lags = chirp.shape[1] // LANE + 1
+    return pl.pallas_call(
+        table_kernel,
+        out_shape=jax.ShapeDtypeStruct((lags * 2 * LANE, 2 * LANE), BF16),
+        compiler_params=pltpu.CompilerParams(vmem_limit_bytes=16 * 1024 * 1024),
+        name="lag_tables",
+    )(chirp)
+
+
+def begin_compression(section, echo, other, table, sections, group):
     _, _, length = echo.shape
-    taps = chirp.shape[1]
     chunk, stack = length // sections, 2 * group
     return pl.pallas_call(
         functools.partial(begin_kernel, group=group),
         out_shape=(
             jax.ShapeDtypeStruct((6 * group, chunk // 2), BF16),
             jax.ShapeDtypeStruct((length // 2 // LANE * stack, 2 * LANE), BF16),
-            jax.ShapeDtypeStruct(((taps // LANE + 1) * 2 * LANE, 2 * LANE), BF16),
         ),
         in_specs=[pl.BlockSpec(memory_space=pltpu.SMEM)] + [pl.BlockSpec(memory_space=pltpu.VMEM)] * 3,
         scratch_shapes=[
@@ -334,7 +345,7 @@
         ],
         compiler_params=pltpu.CompilerParams(vmem_limit_bytes=24 * 1024 * 1024),
         name="begin_compression",
-    )(section, echo, other, chirp)
+    )(section, echo, other, table)
 
 
 def finish_compression(place, early, late, halo, other, table, sections, group):
@@ -433,8 +444,8 @@
         echo, chirp, coef, band_start, band_width, weights, pulse_order, sections, group
     )
     packed_partner = swap(packed, "sub", 1) if subs == 2 else packed
-    halo, chirp = lax.optimization_barrier((halo, chirp))
-    early, late, table = begin_compression(section, echo, other, chirp, sections, group)
+    halo, table = lax.optimization_barrier((halo, lag_tables(chirp)))
+    early, late = begin_compression(section, echo, other, table, sections, group)
     place = section + sections * has_next
     near, far, first, second = finish_compression(
         place, early, late, halo, swap(halo, "section", 1), table, sections, group

time: 18.2 us -> 18 us (0.989)
  waiting for transfers between devices: 2.49 us -> 1.51 us
  Pallas kernels: 5.43 us -> 5.83 us
  starting transfers between devices: 10.1 us -> 10.4 us
    ppermute x1, waiting for transfers between devices: 1.25 us -> 0.26 us  [from_next(): lax.ppermute(value, axis, [(i, (i - 1) % count) for i in range(count)])]
    pallas_call x0 -> x1, Pallas kernels: none -> 0.98 us  [lag_tables(): pl.pallas_call(table_kernel, out_shape=jax.ShapeDtypeStruct((lags * 2 * L...]
    pallas_call x1, Pallas kernels: 1.19 us -> 0.63 us  [begin_compression(): pl.pallas_call(functools.partial(begin_kernel, group=group), out_shape=(j...]
    ppermute x3, starting transfers between devices: 1.52 us -> 1.84 us  [swap(): return lax.ppermute(value, axis, [(i, i ^ by) for i in range(count)])]
  transfers between devices with their start and end apart: 7 -> 7, of which waited for: 4 -> 4; matrix products, arithmetic and copies ran while one was open for 0% -> 0% of each run, Pallas kernels for 24% -> 27%
where the time goes in v12:
time: 18 us; the launch traced here: 17.8 us
  starting transfers between devices  10.4 us (58%)
  Pallas kernels  5.83 us (32%)
  waiting for transfers between devices  1.51 us (8%)
    ppermute x1, starting transfers between devices, from_next(): lax.ppermute(value, axis, [(i, (i - 1) % count) for i in range(count)])  5.05 us
    ppermute x3, starting transfers between devices, swap_by(): return lax.ppermute(value, ('section', 'sub'), pairs)  3.55 us
    ppermute x3, starting transfers between devices, swap(): return lax.ppermute(value, axis, [(i, i ^ by) for i in range(count)])  1.84 us
    pallas_call x1, Pallas kernels, fold_operator(): pl.pallas_call(functools.partial(operator_kernel, dims=dims, sections=sec...  1.32 us
    pallas_call x1, Pallas kernels, prepare(): pl.pallas_call(functools.partial(prepare_kernel, sections=sections, group...  1.27 us
    ppermute x3, waiting for transfers between devices, swap_by(): return lax.ppermute(value, ('section', 'sub'), pairs)  1.24 us
    pallas_call x1, Pallas kernels, form_image(): pl.pallas_call(functools.partial(image_kernel, group=group), out_shape=ja...  1.06 us
    pallas_call x1, Pallas kernels, lag_tables(): pl.pallas_call(table_kernel, out_shape=jax.ShapeDtypeStruct((lags * 2 * L...  0.98 us
  transfers between devices with their start and end apart: 7, of which 4 were waited for; matrix products, arithmetic and copies ran while one was open for 0% of the time, Pallas kernels for 27%

profile of v12, /device:TPU:0, one launch (start us, length us, event | category | flops | bytes accessed | tf_op | source)
XLA Modules:
  0.0 17.8 jit_solution(9062940719257591926)
XLA Ops:
  0.0 5.0 %collective-permute-start.2 = (bf16[6,2,4096]{2,1,0:T(2,128)(2,1)}, bf16[6,2,4096]{2,1,0:T(2,128)(2,1)S(1)}, u32[]{:S(2)}, u32[]{:S(2)}) collective-permute-start(bf16[6,2,4096]{2,1,0:T(2,128)(2,1)} %bitcast.10), channel_id=1, source_target_pairs={{0,3},{1,0},{2,1},{3,2},{4,7},{5,4},{6,5},{7,6},{8,11},{9,8},{10,9... | collective-permute-start | bytes 294920 | tf_op jit(solution)/shard_map/ppermute | solution.py:426
  5.0 0.0 collective-permute-start.1
  5.1 1.3 %prepare.1 = (bf16[6,2,4096]{2,1,0:T(2,128)(2,1)S(1)}, bf16[2,2048]{1,0:T(2,128)(2,1)S(1)}, bf16[400,128]{1,0:T(8,128)(2,1)S(1)}) custom-call(bf16[6,2,4096]{2,1,0:T(2,128)(2,1)} %bitcast.12, bf16[5,1,2,2,16,128]{5,4,3,2,1,0:T(8,128)(2,1)} %bitcast.13, s32[5,1,2,128]{3,2,1,0:T(2,128)} %refs_2_.1, s32[5,1,2,128]{3,2,1,0:T(2,128)} %refs_3_.1, ...), custom_call_target="tpu_custom_call" | custom-call | tf_op jit(solution)/shard_map/prepare/pallas_call | solution.py:72
  6.3 1.0 %lag_tables.1.table = bf16[4352,256]{1,0:T(8,128)(2,1)S(1)} custom-call(bf16[2,2048]{1,0:T(2,128)(2,1)S(1)} %get-tuple-element.18.chirp_ref), custom_call_target="tpu_custom_call" | custom-call | tf_op jit(solution)/shard_map/lag_tables/pallas_call | solution.py:324
  7.3 0.3 %collective-permute-done.2.halo_ref = bf16[6,2,4096]{2,1,0:T(2,128)(2,1)S(1)} collective-permute-done((bf16[6,2,4096]{2,1,0:T(2,128)(2,1)}, bf16[6,2,4096]{2,1,0:T(2,128)(2,1)S(1)}, u32[]{:S(2)}, u32[]{:S(2)}) %collective-permute-start.2) | collective-permute-done | bytes 98336 | tf_op jit(solution)/shard_map/ppermute | solution.py:426
  7.6 0.3 %collective-permute-start.3 = (bf16[6,2,4096]{2,1,0:T(2,128)(2,1)S(1)}, bf16[6,2,4096]{2,1,0:T(2,128)(2,1)S(1)}, u32[]{:S(2)}, u32[]{:S(2)}) collective-permute-start(bf16[6,2,4096]{2,1,0:T(2,128)(2,1)S(1)} %collective-permute-done.2.halo_ref), channel_id=1, source_target_pairs={{0,8},{8,0},{16,24},{24,16},{1,9},{9,1},{17,25},{25,17},{2,10},{10... | collective-permute-start | bytes 294920 | tf_op jit(solution)/shard_map/ppermute | solution.py:411
  7.9 1.5 %collective-permute-start = (bf16[400,128]{1,0:T(8,128)(2,1)S(1)}, bf16[400,128]{1,0:T(8,128)(2,1)S(1)}, u32[]{:S(2)}, u32[]{:S(2)}) collective-permute-start(bf16[400,128]{1,0:T(8,128)(2,1)S(1)} %get-tuple-element.16.own_ref), channel_id=1, source_target_pairs={{0,4},{4,0},{1,5},{5,1},{2,6},{6,2},{3,7},{7,3},{8,12},{12,8},{9,1... | collective-permute-start | bytes 307208 | tf_op jit(solution)/shard_map/ppermute | solution.py:411
  9.4 0.0 collective-permute-done.1.other_ref
  9.4 0.6 %begin_compression.1 = (bf16[48,512]{1,0:T(8,128)(2,1)S(1)}, bf16[256,256]{1,0:T(8,128)(2,1)S(1)}) custom-call(s32[1]{0:T(128)} %bitcast.index_ref, bf16[6,2,4096]{2,1,0:T(2,128)(2,1)S(1)} %get-tuple-element.17.echo_ref, bf16[6,2,4096]{2,1,0:T(2,128)(2,1)S(1)} %collective-permute-done.1.other_ref, bf16[4352,256]{1,0:T(8,128)(2,1)S(1)} %lag_tables.1.table), custom_call_target="tpu_custom_call" | custom-call | tf_op jit(solution)/shard_map/begin_compression/pallas_call | solution.py:335
  10.1 0.0 collective-permute-done.3.other_ref
  10.1 0.6 %finish_compression.1 = (bf16[48,512]{1,0:T(8,128)(2,1)S(1)}, bf16[48,512]{1,0:T(8,128)(2,1)S(1)}, bf16[48,512]{1,0:T(8,128)(2,1)S(1)}, bf16[48,512]{1,0:T(8,128)(2,1)S(1)}) custom-call(s32[1]{0:T(128)S(6)} %add.7.index_ref, bf16[48,512]{1,0:T(8,128)(2,1)S(1)} %get-tuple-element.20.early_ref, bf16[256,256]{1,0:T(8,128)(2,1)S(1)} %get-tuple-element.21.late_ref, ...), custom_call_target="tpu_custom_call" | custom-call | tf_op jit(solution)/shard_map/finish_compression/pallas_call | solution.py:353
  10.7 1.5 %collective-permute-start.4 = (bf16[48,512]{1,0:T(8,128)(2,1)S(1)}, bf16[48,512]{1,0:T(8,128)(2,1)S(1)}, u32[]{:S(2)}, u32[]{:S(2)}) collective-permute-start(bf16[48,512]{1,0:T(8,128)(2,1)S(1)} %get-tuple-element.24), channel_id=1, source_target_pairs={{0,20},{4,16},{8,28},{12,24},{16,4},{20,0},{24,12},{28,8},{1,21},{... | collective-permute-start | bytes 147464 | tf_op jit(solution)/shard_map/ppermute | solution.py:421
  12.2 0.5 %collective-permute-start.5 = (bf16[48,512]{1,0:T(8,128)(2,1)S(1)}, bf16[48,512]{1,0:T(8,128)(2,1)S(1)}, u32[]{:S(2)}, u32[]{:S(2)}) collective-permute-start(bf16[48,512]{1,0:T(8,128)(2,1)S(1)} %get-tuple-element.25), channel_id=1, source_target_pairs={{0,16},{4,20},{8,12},{12,8},{16,0},{20,4},{24,28},{28,24},{1,17},{... | collective-permute-start | bytes 147464 | tf_op jit(solution)/shard_map/ppermute | solution.py:421
  12.7 1.5 %collective-permute-start.6 = (bf16[48,512]{1,0:T(8,128)(2,1)S(1)}, bf16[48,512]{1,0:T(8,128)(2,1)S(1)}, u32[]{:S(2)}, u32[]{:S(2)}) collective-permute-start(bf16[48,512]{1,0:T(8,128)(2,1)S(1)} %get-tuple-element.26), channel_id=1, source_target_pairs={{0,4},{4,0},{8,24},{12,28},{16,20},{20,16},{24,8},{28,12},{1,5},{5... | collective-permute-start | bytes 147464 | tf_op jit(solution)/shard_map/ppermute | solution.py:421
  14.2 0.0 collective-permute-done.partner_ref
  14.2 1.3 %fold_operator.1.operator_ref = bf16[2,256,256]{2,1,0:T(8,128)(2,1)S(1)} custom-call(s32[1]{0:T(128)} %bitcast.index_ref, bf16[400,128]{1,0:T(8,128)(2,1)S(1)} %get-tuple-element.16.own_ref, bf16[400,128]{1,0:T(8,128)(2,1)S(1)} %collective-permute-done.partner_ref), custom_call_target="tpu_custom_call" | custom-call | tf_op jit(solution)/shard_map/fold_operator/pallas_call | solution.py:188
  15.5 0.2 collective-permute-done.4.refs_1_
  15.7 1.0 %collective-permute-done.5.refs_2_ = bf16[48,512]{1,0:T(8,128)(2,1)S(1)} collective-permute-done((bf16[48,512]{1,0:T(8,128)(2,1)S(1)}, bf16[48,512]{1,0:T(8,128)(2,1)S(1)}, u32[]{:S(2)}, u32[]{:S(2)}) %collective-permute-start.5) | collective-permute-done | bytes 49184 | tf_op jit(solution)/shard_map/ppermute | solution.py:421
  16.7 0.1 collective-permute-done.6.refs_3_
  16.8 1.1 %form_image.1 = bf16[256,1024]{1,0:T(8,128)(2,1)} custom-call(bf16[2,256,256]{2,1,0:T(8,128)(2,1)S(1)} %fold_operator.1.operator_ref, bf16[48,512]{1,0:T(8,128)(2,1)S(1)} %get-tuple-element.23.refs_0_, bf16[48,512]{1,0:T(8,128)(2,1)S(1)} %collective-permute-done.4.refs_1_, bf16[48,512]{1,0:T(8,128)(2,1)S(1)} %collective-permute-done.5.refs_2_, ...), custom_call_target="tpu_custom_call" | custom-call | tf_op jit(solution)/shard_map/form_image/pallas_call | solution.py:395
Async XLA Ops:
  0.0 7.6 %collective-permute-start.2 = (bf16[6,2,4096]{2,1,0:T(2,128)(2,1)}, bf16[6,2,4096]{2,1,0:T(2,128)(2,1)S(1)}, u32[]{:S(2)}, u32[]{:S(2)}) collective-permute-start(bf16[6,2,4096]{2,1,0:T(2,128)(2,1)} %bitcast.10), channel_id=1, source_target_pairs={{0,3},{1,0},{2,1},{3,2},{4,7},{5,4},{6,5},{7,6},{8,11},{9,8},{10,9... | collective-permute-start | bytes 294920 | tf_op jit(solution)/shard_map/ppermute | solution.py:426
  5.0 4.4 %collective-permute-start.1 = (bf16[6,2,4096]{2,1,0:T(2,128)(2,1)}, bf16[6,2,4096]{2,1,0:T(2,128)(2,1)S(1)}, u32[]{:S(2)}, u32[]{:S(2)}) collective-permute-start(bf16[6,2,4096]{2,1,0:T(2,128)(2,1)} %bitcast.11), channel_id=1, source_target_pairs={{0,8},{8,0},{16,24},{24,16},{1,9},{9,1},{17,25},{25,17},{2,10},{10... | collective-permute-start | bytes 294920 | tf_op jit(solution)/shard_map/ppermute | solution.py:411
  7.6 2.5 %collective-permute-start.3 = (bf16[6,2,4096]{2,1,0:T(2,128)(2,1)S(1)}, bf16[6,2,4096]{2,1,0:T(2,128)(2,1)S(1)}, u32[]{:S(2)}, u32[]{:S(2)}) collective-permute-start(bf16[6,2,4096]{2,1,0:T(2,128)(2,1)S(1)} %collective-permute-done.2.halo_ref), channel_id=1, source_target_pairs={{0,8},{8,0},{16,24},{24,16},{1,9},{9,1},{17,25},{25,17},{2,10},{10... | collective-permute-start | bytes 294920 | tf_op jit(solution)/shard_map/ppermute | solution.py:411
  7.9 6.3 %collective-permute-start = (bf16[400,128]{1,0:T(8,128)(2,1)S(1)}, bf16[400,128]{1,0:T(8,128)(2,1)S(1)}, u32[]{:S(2)}, u32[]{:S(2)}) collective-permute-start(bf16[400,128]{1,0:T(8,128)(2,1)S(1)} %get-tuple-element.16.own_ref), channel_id=1, source_target_pairs={{0,4},{4,0},{1,5},{5,1},{2,6},{6,2},{3,7},{7,3},{8,12},{12,8},{9,1... | collective-permute-start | bytes 307208 | tf_op jit(solution)/shard_map/ppermute | solution.py:411
  10.7 5.1 %collective-permute-start.4 = (bf16[48,512]{1,0:T(8,128)(2,1)S(1)}, bf16[48,512]{1,0:T(8,128)(2,1)S(1)}, u32[]{:S(2)}, u32[]{:S(2)}) collective-permute-start(bf16[48,512]{1,0:T(8,128)(2,1)S(1)} %get-tuple-element.24), channel_id=1, source_target_pairs={{0,20},{4,16},{8,28},{12,24},{16,4},{20,0},{24,12},{28,8},{1,21},{... | collective-permute-start | bytes 147464 | tf_op jit(solution)/shard_map/ppermute | solution.py:421
  12.2 4.5 %collective-permute-start.5 = (bf16[48,512]{1,0:T(8,128)(2,1)S(1)}, bf16[48,512]{1,0:T(8,128)(2,1)S(1)}, u32[]{:S(2)}, u32[]{:S(2)}) collective-permute-start(bf16[48,512]{1,0:T(8,128)(2,1)S(1)} %get-tuple-element.25), channel_id=1, source_target_pairs={{0,16},{4,20},{8,12},{12,8},{16,0},{20,4},{24,28},{28,24},{1,17},{... | collective-permute-start | bytes 147464 | tf_op jit(solution)/shard_map/ppermute | solution.py:421
  12.7 4.1 %collective-permute-start.6 = (bf16[48,512]{1,0:T(8,128)(2,1)S(1)}, bf16[48,512]{1,0:T(8,128)(2,1)S(1)}, u32[]{:S(2)}, u32[]{:S(2)}) collective-permute-start(bf16[48,512]{1,0:T(8,128)(2,1)S(1)} %get-tuple-element.26), channel_id=1, source_target_pairs={{0,4},{4,0},{8,24},{12,28},{16,20},{20,16},{24,8},{28,12},{1,5},{5... | collective-permute-start | bytes 147464 | tf_op jit(solution)/shard_map/ppermute | solution.py:421

commit v13 on v6

--- a/solution.py
+++ b/solution.py
@@ -254,12 +254,12 @@
         if lag < extra:
             piece = chirp_ref[:, lag * LANE : (lag + 1) * LANE].astype(F32)
             piece = jnp.take_along_axis(piece, reverse, axis=1, mode="promise_in_bounds")
-            turned = [
-                pltpu.roll(
-                    jnp.broadcast_to(piece[c : c + 1], (LANE, LANE)), 1, 1, stride=1, stride_axis=0
-                )
-                for c in range(2)
-            ]
+            turned = []
+            for c in range(2):
+                few = jnp.broadcast_to(piece[c : c + 1], (SUBL, LANE))
+                few = pltpu.roll(few, 1, 1, stride=1, stride_axis=0)
+                groups = [few] + [pltpu.roll(few, first, 1) for first in range(SUBL, LANE, SUBL)]
+                turned.append(jnp.concatenate(groups, axis=0))
         else:
             turned = [jnp.zeros((LANE, LANE), F32)] * 2
         real, imag = [jnp.where(below, turned[c], before[c]) for c in range(2)]

time: 18.2 us -> 18.4 us (1.011)
  Pallas kernels: 5.2 us -> 5.45 us
    pallas_call x1, Pallas kernels: 1.04 us -> 1.28 us  [begin_compression(): pl.pallas_call(functools.partial(begin_kernel, group=group), out_shape=(j...]
  transfers between devices with their start and end apart: 6 -> 6, of which waited for: 4 -> 4; matrix products, arithmetic and copies ran while one was open for 0% -> 0% of each run, Pallas kernels for 23% -> 24%
where the time goes in v13:
time: 18.4 us; the launch traced here: 18.2 us
  starting transfers between devices  10.3 us (56%)
  Pallas kernels  5.45 us (30%)
  waiting for transfers between devices  2.45 us (13%)
    ppermute x1, starting transfers between devices, from_next(): lax.ppermute(value, axis, [(i, (i - 1) % count) for i in range(count)])  5.05 us
    ppermute x3, starting transfers between devices, swap_by(): return lax.ppermute(value, ('section', 'sub'), pairs)  3.55 us
    ppermute x2, starting transfers between devices, swap(): return lax.ppermute(value, axis, [(i, i ^ by) for i in range(count)])  1.66 us
    pallas_call x1, Pallas kernels, fold_operator(): pl.pallas_call(functools.partial(operator_kernel, dims=dims, sections=sec...  1.32 us
    pallas_call x1, Pallas kernels, begin_compression(): pl.pallas_call(functools.partial(begin_kernel, group=group), out_shape=(j...  1.28 us
    pallas_call x1, Pallas kernels, prepare(): pl.pallas_call(functools.partial(prepare_kernel, sections=sections, group...  1.27 us
    ppermute x3, waiting for transfers between devices, swap_by(): return lax.ppermute(value, ('section', 'sub'), pairs)  1.24 us
    ppermute x2, waiting for transfers between devices, swap(): return lax.ppermute(value, axis, [(i, i ^ by) for i in range(count)])  1.21 us
  transfers between devices with their start and end apart: 6, of which 4 were waited for; matrix products, arithmetic and copies ran while one was open for 0% of the time, Pallas kernels for 24%

profile of v13, /device:TPU:0, one launch (start us, length us, event | category | flops | bytes accessed | tf_op | source)
XLA Modules:
  0.0 18.2 jit_solution(12425390841617217398)
XLA Ops:
  0.0 5.0 %collective-permute-start.1 = (bf16[6,2,4096]{2,1,0:T(2,128)(2,1)}, bf16[6,2,4096]{2,1,0:T(2,128)(2,1)S(1)}, u32[]{:S(2)}, u32[]{:S(2)}) collective-permute-start(bf16[6,2,4096]{2,1,0:T(2,128)(2,1)} %bitcast.16), channel_id=1, source_target_pairs={{0,3},{1,0},{2,1},{3,2},{4,7},{5,4},{6,5},{7,6},{8,11},{9,8},{10,9... | collective-permute-start | bytes 294920 | tf_op jit(solution)/shard_map/ppermute | solution.py:415
  5.0 1.3 %prepare.1 = (bf16[6,2,4096]{2,1,0:T(2,128)(2,1)S(1)}, bf16[2,2048]{1,0:T(2,128)(2,1)S(1)}, bf16[400,128]{1,0:T(8,128)(2,1)S(1)}) custom-call(bf16[6,2,4096]{2,1,0:T(2,128)(2,1)} %bitcast.17, bf16[5,1,2,2,16,128]{5,4,3,2,1,0:T(8,128)(2,1)} %bitcast.18, s32[5,1,2,128]{3,2,1,0:T(2,128)} %refs_2_.1, s32[5,1,2,128]{3,2,1,0:T(2,128)} %refs_3_.1, ...), custom_call_target="tpu_custom_call" | custom-call | tf_op jit(solution)/shard_map/prepare/pallas_call | solution.py:72
  6.3 1.6 %collective-permute-start = (bf16[400,128]{1,0:T(8,128)(2,1)S(1)}, bf16[400,128]{1,0:T(8,128)(2,1)S(1)}, u32[]{:S(2)}, u32[]{:S(2)}) collective-permute-start(bf16[400,128]{1,0:T(8,128)(2,1)S(1)} %get-tuple-element.13.own_ref), channel_id=1, source_target_pairs={{0,4},{4,0},{1,5},{5,1},{2,6},{6,2},{3,7},{7,3},{8,12},{12,8},{9,1... | collective-permute-start | bytes 307208 | tf_op jit(solution)/shard_map/ppermute | solution.py:400
  7.9 1.3 %begin_compression.1 = (bf16[2,24,512]{2,1,0:T(8,128)(2,1)S(1)}, f32[16,2048]{1,0:T(8,128)S(1)}, bf16[4352,256]{1,0:T(8,128)(2,1)S(1)}) custom-call(bf16[6,2,4096]{2,1,0:T(2,128)(2,1)S(1)} %get-tuple-element.14.echo_ref, bf16[2,2048]{1,0:T(2,128)(2,1)S(1)} %get-tuple-element.15.chirp_ref), custom_call_target="tpu_custom_call" | custom-call | tf_op jit(solution)/shard_map/begin_compression/pallas_call | solution.py:327
  9.2 0.0 collective-permute-done.1.halo_ref
  9.2 0.5 %finish_compression.1 = (bf16[2,24,512]{2,1,0:T(8,128)(2,1)S(1)}, bf16[2,24,512]{2,1,0:T(8,128)(2,1)S(1)}) custom-call(s32[1]{0:T(128)S(6)} %add.15.index_ref, bf16[2,24,512]{2,1,0:T(8,128)(2,1)S(1)} %get-tuple-element.16.early_ref, f32[16,2048]{1,0:T(8,128)S(1)} %get-tuple-element.17.late_ref, bf16[6,2,4096]{2,1,0:T(2,128)(2,1)S(1)} %collective-permute-done.1.halo_ref, ...), custom_call_target="tpu_custom_call" | custom-call | tf_op jit(solution)/shard_map/finish_compression/pallas_call | solution.py:342
  9.7 0.1 collective-permute-start.2
  9.8 1.2 %collective-permute-done.2 = bf16[2,24,512]{2,1,0:T(8,128)(2,1)S(1)} collective-permute-done((bf16[2,24,512]{2,1,0:T(8,128)(2,1)S(1)}, bf16[2,24,512]{2,1,0:T(8,128)(2,1)S(1)}, u32[]{:S(2)}, u32[]{:S(2)}) %collective-permute-start.2) | collective-permute-done | bytes 49184 | tf_op jit(solution)/shard_map/ppermute | solution.py:400
  11.1 1.5 %collective-permute-start.3 = (bf16[48,512]{1,0:T(8,128)(2,1)S(1)}, bf16[48,512]{1,0:T(8,128)(2,1)S(1)}, u32[]{:S(2)}, u32[]{:S(2)}) collective-permute-start(bf16[48,512]{1,0:T(8,128)(2,1)S(1)} %get-tuple-element.23), channel_id=1, source_target_pairs={{0,20},{4,16},{8,28},{12,24},{16,4},{20,0},{24,12},{28,8},{1,21},{... | collective-permute-start | bytes 147464 | tf_op jit(solution)/shard_map/ppermute | solution.py:410
  12.6 0.5 %collective-permute-start.4 = (bf16[48,512]{1,0:T(8,128)(2,1)S(1)}, bf16[48,512]{1,0:T(8,128)(2,1)S(1)}, u32[]{:S(2)}, u32[]{:S(2)}) collective-permute-start(bf16[48,512]{1,0:T(8,128)(2,1)S(1)} %get-tuple-element.22), channel_id=1, source_target_pairs={{0,16},{4,20},{8,12},{12,8},{16,0},{20,4},{24,28},{28,24},{1,17},{... | collective-permute-start | bytes 147464 | tf_op jit(solution)/shard_map/ppermute | solution.py:410
  13.1 1.5 %collective-permute-start.5 = (bf16[48,512]{1,0:T(8,128)(2,1)S(1)}, bf16[48,512]{1,0:T(8,128)(2,1)S(1)}, u32[]{:S(2)}, u32[]{:S(2)}) collective-permute-start(bf16[48,512]{1,0:T(8,128)(2,1)S(1)} %get-tuple-element.21), channel_id=1, source_target_pairs={{0,4},{4,0},{8,24},{12,28},{16,20},{20,16},{24,8},{28,12},{1,5},{5... | collective-permute-start | bytes 147464 | tf_op jit(solution)/shard_map/ppermute | solution.py:410
  14.6 0.0 collective-permute-done.partner_ref
  14.6 1.3 %fold_operator.1.operator_ref = bf16[2,256,256]{2,1,0:T(8,128)(2,1)S(1)} custom-call(s32[1]{0:T(128)} %bitcast.index_ref, bf16[400,128]{1,0:T(8,128)(2,1)S(1)} %get-tuple-element.13.own_ref, bf16[400,128]{1,0:T(8,128)(2,1)S(1)} %collective-permute-done.partner_ref), custom_call_target="tpu_custom_call" | custom-call | tf_op jit(solution)/shard_map/fold_operator/pallas_call | solution.py:188
  15.9 0.2 %collective-permute-done.3.refs_0_ = bf16[48,512]{1,0:T(8,128)(2,1)S(1)} collective-permute-done((bf16[48,512]{1,0:T(8,128)(2,1)S(1)}, bf16[48,512]{1,0:T(8,128)(2,1)S(1)}, u32[]{:S(2)}, u32[]{:S(2)}) %collective-permute-start.3) | collective-permute-done | bytes 49184 | tf_op jit(solution)/shard_map/ppermute | solution.py:410
  16.2 0.8 %collective-permute-done.4.refs_1_ = bf16[48,512]{1,0:T(8,128)(2,1)S(1)} collective-permute-done((bf16[48,512]{1,0:T(8,128)(2,1)S(1)}, bf16[48,512]{1,0:T(8,128)(2,1)S(1)}, u32[]{:S(2)}, u32[]{:S(2)}) %collective-permute-start.4) | collective-permute-done | bytes 49184 | tf_op jit(solution)/shard_map/ppermute | solution.py:410
  17.0 0.2 collective-permute-done.5.refs_2_
  17.2 1.1 %form_image.1 = bf16[256,1024]{1,0:T(8,128)(2,1)} custom-call(s32[1]{0:T(128)} %bitcast.index_ref, bf16[2,256,256]{2,1,0:T(8,128)(2,1)S(1)} %fold_operator.1.operator_ref, bf16[2,48,512]{2,1,0:T(8,128)(2,1)S(1)} %constant_dynamic-update-slice_fusion.both_ref, bf16[48,512]{1,0:T(8,128)(2,1)S(1)} %collective-permute-done.3.refs_0_, ...), custom_call_target="tpu_custom_call" | custom-call | tf_op jit(solution)/shard_map/form_image/pallas_call | solution.py:383
  (3 shorter events, 0.0 us)
Async XLA Ops:
  0.0 9.2 %collective-permute-start.1 = (bf16[6,2,4096]{2,1,0:T(2,128)(2,1)}, bf16[6,2,4096]{2,1,0:T(2,128)(2,1)S(1)}, u32[]{:S(2)}, u32[]{:S(2)}) collective-permute-start(bf16[6,2,4096]{2,1,0:T(2,128)(2,1)} %bitcast.16), channel_id=1, source_target_pairs={{0,3},{1,0},{2,1},{3,2},{4,7},{5,4},{6,5},{7,6},{8,11},{9,8},{10,9... | collective-permute-start | bytes 294920 | tf_op jit(solution)/shard_map/ppermute | solution.py:415
  6.3 8.3 %collective-permute-start = (bf16[400,128]{1,0:T(8,128)(2,1)S(1)}, bf16[400,128]{1,0:T(8,128)(2,1)S(1)}, u32[]{:S(2)}, u32[]{:S(2)}) collective-permute-start(bf16[400,128]{1,0:T(8,128)(2,1)S(1)} %get-tuple-element.13.own_ref), channel_id=1, source_target_pairs={{0,4},{4,0},{1,5},{5,1},{2,6},{6,2},{3,7},{7,3},{8,12},{12,8},{9,1... | collective-permute-start | bytes 307208 | tf_op jit(solution)/shard_map/ppermute | solution.py:400
  9.7 1.3 %collective-permute-start.2 = (bf16[2,24,512]{2,1,0:T(8,128)(2,1)S(1)}, bf16[2,24,512]{2,1,0:T(8,128)(2,1)S(1)}, u32[]{:S(2)}, u32[]{:S(2)}) collective-permute-start(bf16[2,24,512]{2,1,0:T(8,128)(2,1)S(1)} %get-tuple-element.20), channel_id=1, source_target_pairs={{0,8},{8,0},{16,24},{24,16},{1,9},{9,1},{17,25},{25,17},{2,10},{10... | collective-permute-start | bytes 147464 | tf_op jit(solution)/shard_map/ppermute | solution.py:400
  11.1 5.1 %collective-permute-start.3 = (bf16[48,512]{1,0:T(8,128)(2,1)S(1)}, bf16[48,512]{1,0:T(8,128)(2,1)S(1)}, u32[]{:S(2)}, u32[]{:S(2)}) collective-permute-start(bf16[48,512]{1,0:T(8,128)(2,1)S(1)} %get-tuple-element.23), channel_id=1, source_target_pairs={{0,20},{4,16},{8,28},{12,24},{16,4},{20,0},{24,12},{28,8},{1,21},{... | collective-permute-start | bytes 147464 | tf_op jit(solution)/shard_map/ppermute | solution.py:410
  12.6 4.5 %collective-permute-start.4 = (bf16[48,512]{1,0:T(8,128)(2,1)S(1)}, bf16[48,512]{1,0:T(8,128)(2,1)S(1)}, u32[]{:S(2)}, u32[]{:S(2)}) collective-permute-start(bf16[48,512]{1,0:T(8,128)(2,1)S(1)} %get-tuple-element.22), channel_id=1, source_target_pairs={{0,16},{4,20},{8,12},{12,8},{16,0},{20,4},{24,28},{28,24},{1,17},{... | collective-permute-start | bytes 147464 | tf_op jit(solution)/shard_map/ppermute | solution.py:410
  13.1 4.1 %collective-permute-start.5 = (bf16[48,512]{1,0:T(8,128)(2,1)S(1)}, bf16[48,512]{1,0:T(8,128)(2,1)S(1)}, u32[]{:S(2)}, u32[]{:S(2)}) collective-permute-start(bf16[48,512]{1,0:T(8,128)(2,1)S(1)} %get-tuple-element.21), channel_id=1, source_target_pairs={{0,4},{4,0},{8,24},{12,28},{16,20},{20,16},{24,8},{28,12},{1,5},{5... | collective-permute-start | bytes 147464 | tf_op jit(solution)/shard_map/ppermute | solution.py:410

commit v14 on v13

--- a/solution.py
+++ b/solution.py
@@ -249,26 +249,26 @@
     below = lax.broadcasted_iota(jnp.int32, (LANE, LANE), 1) <= lax.broadcasted_iota(
         jnp.int32, (LANE, LANE), 0
     )
-    before = [jnp.zeros((LANE, LANE), F32)] * 2
+    before = [jnp.zeros((LANE, LANE), BF16)] * 2
     for lag in range(extra + 1):
         if lag < extra:
             piece = chirp_ref[:, lag * LANE : (lag + 1) * LANE].astype(F32)
             piece = jnp.take_along_axis(piece, reverse, axis=1, mode="promise_in_bounds")
             turned = []
             for c in range(2):
-                few = jnp.broadcast_to(piece[c : c + 1], (SUBL, LANE))
-                few = pltpu.roll(few, 1, 1, stride=1, stride_axis=0)
-                groups = [few] + [pltpu.roll(few, first, 1) for first in range(SUBL, LANE, SUBL)]
+                few = jnp.broadcast_to(piece[c : c + 1], (2 * SUBL, LANE))
+                few = pltpu.roll(few, 1, 1, stride=1, stride_axis=0).astype(BF16)
+                groups = [few] + [pltpu.roll(few, at, 1) for at in range(2 * SUBL, LANE, 2 * SUBL)]
                 turned.append(jnp.concatenate(groups, axis=0))
         else:
-            turned = [jnp.zeros((LANE, LANE), F32)] * 2
+            turned = [jnp.zeros((LANE, LANE), BF16)] * 2
         real, imag = [jnp.where(below, turned[c], before[c]) for c in range(2)]
         before = turned
         at = lag * 2 * LANE
-        table[at : at + LANE, :LANE] = real.astype(BF16)
-        table[at : at + LANE, LANE:] = (-imag).astype(BF16)
-        table[at + LANE : at + 2 * LANE, :LANE] = imag.astype(BF16)
-        table[at + LANE : at + 2 * LANE, LANE:] = real.astype(BF16)
+        table[at : at + LANE, :LANE] = real
+        table[at : at + LANE, LANE:] = -imag
+        table[at + LANE : at + 2 * LANE, :LANE] = imag
+        table[at + LANE : at + 2 * LANE, LANE:] = real
     rows[...] = jnp.zeros_like(rows)
     for p in range(pulses):
         near = echo_ref[p].astype(F32)

time: 18.4 us -> 18.1 us (0.984)
  Pallas kernels: 5.45 us -> 5.15 us
    pallas_call x1, Pallas kernels: 1.28 us -> 0.99 us  [begin_compression(): pl.pallas_call(functools.partial(begin_kernel, group=group), out_shape=(j...]
  transfers between devices with their start and end apart: 6 -> 6, of which waited for: 4 -> 4; matrix products, arithmetic and copies ran while one was open for 0% -> 0% of each run, Pallas kernels for 24% -> 23%
where the time goes in v14:
time: 18.1 us; the launch traced here: 18 us
  starting transfers between devices  10.3 us (57%)
  Pallas kernels  5.15 us (28%)
  waiting for transfers between devices  2.45 us (14%)
    ppermute x1, starting transfers between devices, from_next(): lax.ppermute(value, axis, [(i, (i - 1) % count) for i in range(count)])  5.05 us
    ppermute x3, starting transfers between devices, swap_by(): return lax.ppermute(value, ('section', 'sub'), pairs)  3.55 us
    ppermute x2, starting transfers between devices, swap(): return lax.ppermute(value, axis, [(i, i ^ by) for i in range(count)])  1.66 us
    pallas_call x1, Pallas kernels, fold_operator(): pl.pallas_call(functools.partial(operator_kernel, dims=dims, sections=sec...  1.32 us
    pallas_call x1, Pallas kernels, prepare(): pl.pallas_call(functools.partial(prepare_kernel, sections=sections, group...  1.27 us
    ppermute x3, waiting for transfers between devices, swap_by(): return lax.ppermute(value, ('section', 'sub'), pairs)  1.24 us
    ppermute x2, waiting for transfers between devices, swap(): return lax.ppermute(value, axis, [(i, i ^ by) for i in range(count)])  1.21 us
    pallas_call x1, Pallas kernels, form_image(): pl.pallas_call(functools.partial(image_kernel, group=group), out_shape=ja...  1.06 us
  transfers between devices with their start and end apart: 6, of which 4 were waited for; matrix products, arithmetic and copies ran while one was open for 0% of the time, Pallas kernels for 23%

profile of v14, /device:TPU:0, one launch (start us, length us, event | category | flops | bytes accessed | tf_op | source)
XLA Modules:
  0.0 18.0 jit_solution(14967126590185913492)
XLA Ops:
  0.0 5.0 %collective-permute-start.1 = (bf16[6,2,4096]{2,1,0:T(2,128)(2,1)}, bf16[6,2,4096]{2,1,0:T(2,128)(2,1)S(1)}, u32[]{:S(2)}, u32[]{:S(2)}) collective-permute-start(bf16[6,2,4096]{2,1,0:T(2,128)(2,1)} %bitcast.16), channel_id=1, source_target_pairs={{0,3},{1,0},{2,1},{3,2},{4,7},{5,4},{6,5},{7,6},{8,11},{9,8},{10,9... | collective-permute-start | bytes 294920 | tf_op jit(solution)/shard_map/ppermute | solution.py:415
  5.0 1.3 %prepare.1 = (bf16[6,2,4096]{2,1,0:T(2,128)(2,1)S(1)}, bf16[2,2048]{1,0:T(2,128)(2,1)S(1)}, bf16[400,128]{1,0:T(8,128)(2,1)S(1)}) custom-call(bf16[6,2,4096]{2,1,0:T(2,128)(2,1)} %bitcast.17, bf16[5,1,2,2,16,128]{5,4,3,2,1,0:T(8,128)(2,1)} %bitcast.18, s32[5,1,2,128]{3,2,1,0:T(2,128)} %refs_2_.1, s32[5,1,2,128]{3,2,1,0:T(2,128)} %refs_3_.1, ...), custom_call_target="tpu_custom_call" | custom-call | tf_op jit(solution)/shard_map/prepare/pallas_call | solution.py:72
  6.3 1.6 %collective-permute-start = (bf16[400,128]{1,0:T(8,128)(2,1)S(1)}, bf16[400,128]{1,0:T(8,128)(2,1)S(1)}, u32[]{:S(2)}, u32[]{:S(2)}) collective-permute-start(bf16[400,128]{1,0:T(8,128)(2,1)S(1)} %get-tuple-element.13.own_ref), channel_id=1, source_target_pairs={{0,4},{4,0},{1,5},{5,1},{2,6},{6,2},{3,7},{7,3},{8,12},{12,8},{9,1... | collective-permute-start | bytes 307208 | tf_op jit(solution)/shard_map/ppermute | solution.py:400
  7.9 1.0 %begin_compression.1 = (bf16[2,24,512]{2,1,0:T(8,128)(2,1)S(1)}, f32[16,2048]{1,0:T(8,128)S(1)}, bf16[4352,256]{1,0:T(8,128)(2,1)S(1)}) custom-call(bf16[6,2,4096]{2,1,0:T(2,128)(2,1)S(1)} %get-tuple-element.14.echo_ref, bf16[2,2048]{1,0:T(2,128)(2,1)S(1)} %get-tuple-element.15.chirp_ref), custom_call_target="tpu_custom_call" | custom-call | tf_op jit(solution)/shard_map/begin_compression/pallas_call | solution.py:327
  8.9 0.0 collective-permute-done.1.halo_ref
  8.9 0.5 %finish_compression.1 = (bf16[2,24,512]{2,1,0:T(8,128)(2,1)S(1)}, bf16[2,24,512]{2,1,0:T(8,128)(2,1)S(1)}) custom-call(s32[1]{0:T(128)S(6)} %add.15.index_ref, bf16[2,24,512]{2,1,0:T(8,128)(2,1)S(1)} %get-tuple-element.16.early_ref, f32[16,2048]{1,0:T(8,128)S(1)} %get-tuple-element.17.late_ref, bf16[6,2,4096]{2,1,0:T(2,128)(2,1)S(1)} %collective-permute-done.1.halo_ref, ...), custom_call_target="tpu_custom_call" | custom-call | tf_op jit(solution)/shard_map/finish_compression/pallas_call | solution.py:342
  9.4 0.1 collective-permute-start.2
  9.5 1.2 %collective-permute-done.2 = bf16[2,24,512]{2,1,0:T(8,128)(2,1)S(1)} collective-permute-done((bf16[2,24,512]{2,1,0:T(8,128)(2,1)S(1)}, bf16[2,24,512]{2,1,0:T(8,128)(2,1)S(1)}, u32[]{:S(2)}, u32[]{:S(2)}) %collective-permute-start.2) | collective-permute-done | bytes 49184 | tf_op jit(solution)/shard_map/ppermute | solution.py:400
  10.8 1.5 %collective-permute-start.3 = (bf16[48,512]{1,0:T(8,128)(2,1)S(1)}, bf16[48,512]{1,0:T(8,128)(2,1)S(1)}, u32[]{:S(2)}, u32[]{:S(2)}) collective-permute-start(bf16[48,512]{1,0:T(8,128)(2,1)S(1)} %get-tuple-element.23), channel_id=1, source_target_pairs={{0,20},{4,16},{8,28},{12,24},{16,4},{20,0},{24,12},{28,8},{1,21},{... | collective-permute-start | bytes 147464 | tf_op jit(solution)/shard_map/ppermute | solution.py:410
  12.3 0.5 %collective-permute-start.4 = (bf16[48,512]{1,0:T(8,128)(2,1)S(1)}, bf16[48,512]{1,0:T(8,128)(2,1)S(1)}, u32[]{:S(2)}, u32[]{:S(2)}) collective-permute-start(bf16[48,512]{1,0:T(8,128)(2,1)S(1)} %get-tuple-element.22), channel_id=1, source_target_pairs={{0,16},{4,20},{8,12},{12,8},{16,0},{20,4},{24,28},{28,24},{1,17},{... | collective-permute-start | bytes 147464 | tf_op jit(solution)/shard_map/ppermute | solution.py:410
  12.8 1.5 %collective-permute-start.5 = (bf16[48,512]{1,0:T(8,128)(2,1)S(1)}, bf16[48,512]{1,0:T(8,128)(2,1)S(1)}, u32[]{:S(2)}, u32[]{:S(2)}) collective-permute-start(bf16[48,512]{1,0:T(8,128)(2,1)S(1)} %get-tuple-element.21), channel_id=1, source_target_pairs={{0,4},{4,0},{8,24},{12,28},{16,20},{20,16},{24,8},{28,12},{1,5},{5... | collective-permute-start | bytes 147464 | tf_op jit(solution)/shard_map/ppermute | solution.py:410
  14.3 0.0 collective-permute-done.partner_ref
  14.3 1.3 %fold_operator.1.operator_ref = bf16[2,256,256]{2,1,0:T(8,128)(2,1)S(1)} custom-call(s32[1]{0:T(128)} %bitcast.index_ref, bf16[400,128]{1,0:T(8,128)(2,1)S(1)} %get-tuple-element.13.own_ref, bf16[400,128]{1,0:T(8,128)(2,1)S(1)} %collective-permute-done.partner_ref), custom_call_target="tpu_custom_call" | custom-call | tf_op jit(solution)/shard_map/fold_operator/pallas_call | solution.py:188
  15.7 0.2 %collective-permute-done.3.refs_0_ = bf16[48,512]{1,0:T(8,128)(2,1)S(1)} collective-permute-done((bf16[48,512]{1,0:T(8,128)(2,1)S(1)}, bf16[48,512]{1,0:T(8,128)(2,1)S(1)}, u32[]{:S(2)}, u32[]{:S(2)}) %collective-permute-start.3) | collective-permute-done | bytes 49184 | tf_op jit(solution)/shard_map/ppermute | solution.py:410
  15.9 0.9 %collective-permute-done.4.refs_1_ = bf16[48,512]{1,0:T(8,128)(2,1)S(1)} collective-permute-done((bf16[48,512]{1,0:T(8,128)(2,1)S(1)}, bf16[48,512]{1,0:T(8,128)(2,1)S(1)}, u32[]{:S(2)}, u32[]{:S(2)}) %collective-permute-start.4) | collective-permute-done | bytes 49184 | tf_op jit(solution)/shard_map/ppermute | solution.py:410
  16.7 0.2 collective-permute-done.5.refs_2_
  16.9 1.1 %form_image.1 = bf16[256,1024]{1,0:T(8,128)(2,1)} custom-call(s32[1]{0:T(128)} %bitcast.index_ref, bf16[2,256,256]{2,1,0:T(8,128)(2,1)S(1)} %fold_operator.1.operator_ref, bf16[2,48,512]{2,1,0:T(8,128)(2,1)S(1)} %constant_dynamic-update-slice_fusion.both_ref, bf16[48,512]{1,0:T(8,128)(2,1)S(1)} %collective-permute-done.3.refs_0_, ...), custom_call_target="tpu_custom_call" | custom-call | tf_op jit(solution)/shard_map/form_image/pallas_call | solution.py:383
  (3 shorter events, 0.0 us)
Async XLA Ops:
  0.0 8.9 %collective-permute-start.1 = (bf16[6,2,4096]{2,1,0:T(2,128)(2,1)}, bf16[6,2,4096]{2,1,0:T(2,128)(2,1)S(1)}, u32[]{:S(2)}, u32[]{:S(2)}) collective-permute-start(bf16[6,2,4096]{2,1,0:T(2,128)(2,1)} %bitcast.16), channel_id=1, source_target_pairs={{0,3},{1,0},{2,1},{3,2},{4,7},{5,4},{6,5},{7,6},{8,11},{9,8},{10,9... | collective-permute-start | bytes 294920 | tf_op jit(solution)/shard_map/ppermute | solution.py:415
  6.3 8.0 %collective-permute-start = (bf16[400,128]{1,0:T(8,128)(2,1)S(1)}, bf16[400,128]{1,0:T(8,128)(2,1)S(1)}, u32[]{:S(2)}, u32[]{:S(2)}) collective-permute-start(bf16[400,128]{1,0:T(8,128)(2,1)S(1)} %get-tuple-element.13.own_ref), channel_id=1, source_target_pairs={{0,4},{4,0},{1,5},{5,1},{2,6},{6,2},{3,7},{7,3},{8,12},{12,8},{9,1... | collective-permute-start | bytes 307208 | tf_op jit(solution)/shard_map/ppermute | solution.py:400
  9.4 1.3 %collective-permute-start.2 = (bf16[2,24,512]{2,1,0:T(8,128)(2,1)S(1)}, bf16[2,24,512]{2,1,0:T(8,128)(2,1)S(1)}, u32[]{:S(2)}, u32[]{:S(2)}) collective-permute-start(bf16[2,24,512]{2,1,0:T(8,128)(2,1)S(1)} %get-tuple-element.20), channel_id=1, source_target_pairs={{0,8},{8,0},{16,24},{24,16},{1,9},{9,1},{17,25},{25,17},{2,10},{10... | collective-permute-start | bytes 147464 | tf_op jit(solution)/shard_map/ppermute | solution.py:400
  10.8 5.1 %collective-permute-start.3 = (bf16[48,512]{1,0:T(8,128)(2,1)S(1)}, bf16[48,512]{1,0:T(8,128)(2,1)S(1)}, u32[]{:S(2)}, u32[]{:S(2)}) collective-permute-start(bf16[48,512]{1,0:T(8,128)(2,1)S(1)} %get-tuple-element.23), channel_id=1, source_target_pairs={{0,20},{4,16},{8,28},{12,24},{16,4},{20,0},{24,12},{28,8},{1,21},{... | collective-permute-start | bytes 147464 | tf_op jit(solution)/shard_map/ppermute | solution.py:410
  12.3 4.5 %collective-permute-start.4 = (bf16[48,512]{1,0:T(8,128)(2,1)S(1)}, bf16[48,512]{1,0:T(8,128)(2,1)S(1)}, u32[]{:S(2)}, u32[]{:S(2)}) collective-permute-start(bf16[48,512]{1,0:T(8,128)(2,1)S(1)} %get-tuple-element.22), channel_id=1, source_target_pairs={{0,16},{4,20},{8,12},{12,8},{16,0},{20,4},{24,28},{28,24},{1,17},{... | collective-permute-start | bytes 147464 | tf_op jit(solution)/shard_map/ppermute | solution.py:410
  12.8 4.1 %collective-permute-start.5 = (bf16[48,512]{1,0:T(8,128)(2,1)S(1)}, bf16[48,512]{1,0:T(8,128)(2,1)S(1)}, u32[]{:S(2)}, u32[]{:S(2)}) collective-permute-start(bf16[48,512]{1,0:T(8,128)(2,1)S(1)} %get-tuple-element.21), channel_id=1, source_target_pairs={{0,4},{4,0},{8,24},{12,28},{16,20},{20,16},{24,8},{28,12},{1,5},{5... | collective-permute-start | bytes 147464 | tf_op jit(solution)/shard_map/ppermute | solution.py:410

commit v15 on v14

--- a/solution.py
+++ b/solution.py
@@ -199,38 +199,22 @@
     )(section, own, partner)
 
 
-def correlate(rows, even, odd, table, blocks, group):
-    extra = table.shape[0] // (2 * LANE) - 1
-    total = blocks + extra
-    held = [
-        jnp.concatenate(
-            [rows[:group, b * LANE : (b + 1) * LANE], rows[group:, b * LANE : (b + 1) * LANE]], axis=1
-        )
-        for b in range(total)
-    ]
-    for b in range(0, total, 2):
-        even[b * group : (b + 2) * group] = jnp.concatenate(held[b : b + 2], axis=0).astype(BF16)
-    for b in range(1, total - 1, 2):
-        odd[(b - 1) * group : (b + 1) * group] = jnp.concatenate(held[b : b + 2], axis=0).astype(BF16)
-    window = blocks * group
-    pieces = []
-    for lag in range(extra + 1):
-        source, at = (even, lag) if lag % 2 == 0 else (odd, lag - 1)
-        pieces.append(source[at * group : at * group + window])
+def correlate(rows, held, table, blocks, group):
+    lags, stack = table.shape[0] // LANE, 2 * group
+    for b in range(blocks + lags - 1):
+        held[b * stack : (b + 1) * stack] = rows[:, b * LANE : (b + 1) * LANE].astype(BF16)
+    pieces = [held[lag * stack : (lag + blocks) * stack] for lag in range(lags)]
     return jnp.dot(jnp.concatenate(pieces, axis=1), table[...], preferred_element_type=F32)
 
 
 def as_chunk(done, s, chunk, group, each):
-    real, imag = [
-        jnp.concatenate(
-            [
-                done[(s * chunk + b) * group : (s * chunk + b + 1) * group, c * LANE : (c + 1) * LANE]
-                for b in range(chunk)
-            ],
-            axis=1,
-        )
-        for c in range(2)
-    ]
+    real, imag = [], []
+    for b in range(s * chunk, (s + 1) * chunk):
+        at = 2 * b * group
+        first, second = done[at : at + group], done[at + group : at + 2 * group]
+        real.append(first[:, :LANE] + second[:, LANE:])
+        imag.append(second[:, :LANE] - first[:, LANE:])
+    real, imag = jnp.concatenate(real, axis=1), jnp.concatenate(imag, axis=1)
     middle = chunk * LANE // 2
     lead, moved = pack_rows_of(real, imag, each)
     row = lax.broadcasted_iota(jnp.int32, (group, middle), 0)
@@ -242,7 +226,7 @@
     return jnp.concatenate([lead[:, :middle], lead[:, middle:], rest], axis=0).astype(BF16)
 
 
-def begin_kernel(echo_ref, chirp_ref, early_ref, late_ref, table, rows, even, odd, *, group):
+def begin_kernel(echo_ref, chirp_ref, early_ref, late_ref, table, rows, held, *, group):
     pulses, _, length = echo_ref.shape
     extra = chirp_ref.shape[1] // LANE
     reverse = LANE - 1 - lax.broadcasted_iota(jnp.int32, (2, LANE), 1)
@@ -264,23 +248,20 @@
             turned = [jnp.zeros((LANE, LANE), BF16)] * 2
         real, imag = [jnp.where(below, turned[c], before[c]) for c in range(2)]
         before = turned
-        at = lag * 2 * LANE
-        table[at : at + LANE, :LANE] = real
-        table[at : at + LANE, LANE:] = -imag
-        table[at + LANE : at + 2 * LANE, :LANE] = imag
-        table[at + LANE : at + 2 * LANE, LANE:] = real
+        table[lag * LANE : (lag + 1) * LANE, :LANE] = real
+        table[lag * LANE : (lag + 1) * LANE, LANE:] = imag
     rows[...] = jnp.zeros_like(rows)
     for p in range(pulses):
         near = echo_ref[p].astype(F32)
         for c in range(2):
             rows[c * group + p : c * group + p + 1, :] = near[c : c + 1]
     late_ref[...] = rows[:, length - late_ref.shape[1] :]
-    done = correlate(rows, even, odd, table, length // LANE - extra, group)
+    done = correlate(rows, held, table, length // LANE - extra, group)
     for s in range(early_ref.shape[0]):
         early_ref[s] = as_chunk(done, s, 2 * early_ref.shape[2] // LANE, group, pulses)
 
 
-def finish_kernel(index_ref, early_ref, late_ref, halo_ref, table, keep_ref, give_ref, rows, even, odd, *, group):
+def finish_kernel(index_ref, early_ref, late_ref, halo_ref, table, keep_ref, give_ref, rows, held, *, group):
     pulses = halo_ref.shape[0]
     span = late_ref.shape[1]
     taps = rows.shape[1] - span
@@ -295,7 +276,7 @@
         far = jnp.where(has_next, halo_ref[p, :, :taps].astype(F32), 0.0)
         for c in range(2):
             rows[c * group + p : c * group + p + 1, span:] = far[c : c + 1]
-    done = correlate(rows, even, odd, table, span // LANE, group)
+    done = correlate(rows, held, table, span // LANE, group)
     for s in range(sections):
         stacked = early_ref[s] if s < ready else as_chunk(done, s - ready, chunk // LANE, group, pulses)
         slot = section ^ s
@@ -314,8 +295,7 @@
 def row_scratch(blocks, group):
     return [
         pltpu.VMEM((2 * group, blocks * LANE), F32),
-        pltpu.VMEM((blocks * group, 2 * LANE), BF16),
-        pltpu.VMEM((blocks * group, 2 * LANE), BF16),
+        pltpu.VMEM((2 * blocks * group, LANE), BF16),
     ]
 
 
@@ -329,7 +309,7 @@
         out_shape=(
             jax.ShapeDtypeStruct((early, 3 * group, chunk // 2), BF16),
             jax.ShapeDtypeStruct((2 * group, length - early * chunk), F32),
-            jax.ShapeDtypeStruct(((taps // LANE + 1) * 2 * LANE, 2 * LANE), BF16),
+            jax.ShapeDtypeStruct((taps + LANE, 2 * LANE), BF16),
         ),
         scratch_shapes=row_scratch(length // LANE, group),
         compiler_params=pltpu.CompilerParams(vmem_limit_bytes=24 * 1024 * 1024),
@@ -338,7 +318,7 @@
 
 
 def finish_compression(place, early, late, halo, table, group):
-    blocks = late.shape[1] // LANE + table.shape[0] // (2 * LANE) - 1
+    blocks = late.shape[1] // LANE + table.shape[0] // LANE - 1
     return pl.pallas_call(
         functools.partial(finish_kernel, group=group),
         out_shape=[jax.ShapeDtypeStruct((2, *early.shape[1:]), BF16)] * 2,

time: 18.1 us -> 18.1 us (level)
  no operation moved by 1% of the time
where the time goes in v15:
time: 18.1 us; the launch traced here: 17.9 us
  starting transfers between devices  10.3 us (57%)
  Pallas kernels  5.15 us (28%)
  waiting for transfers between devices  2.42 us (13%)
    ppermute x1, starting transfers between devices, from_next(): lax.ppermute(value, axis, [(i, (i - 1) % count) for i in range(count)])  5.05 us
    ppermute x3, starting transfers between devices, swap_by(): return lax.ppermute(value, ('section', 'sub'), pairs)  3.55 us
    ppermute x2, starting transfers between devices, swap(): return lax.ppermute(value, axis, [(i, i ^ by) for i in range(count)])  1.66 us
    pallas_call x1, Pallas kernels, fold_operator(): pl.pallas_call(functools.partial(operator_kernel, dims=dims, sections=sec...  1.32 us
    pallas_call x1, Pallas kernels, prepare(): pl.pallas_call(functools.partial(prepare_kernel, sections=sections, group...  1.27 us
    ppermute x3, waiting for transfers between devices, swap_by(): return lax.ppermute(value, ('section', 'sub'), pairs)  1.22 us
    ppermute x2, waiting for transfers between devices, swap(): return lax.ppermute(value, axis, [(i, i ^ by) for i in range(count)])  1.21 us
    pallas_call x1, Pallas kernels, form_image(): pl.pallas_call(functools.partial(image_kernel, group=group), out_shape=ja...  1.06 us
  transfers between devices with their start and end apart: 6, of which 4 were waited for; matrix products, arithmetic and copies ran while one was open for 0% of the time, Pallas kernels for 23%

profile of v15, /device:TPU:0, one launch (start us, length us, event | category | flops | bytes accessed | tf_op | source)
XLA Modules:
  0.0 17.9 jit_solution(14063600925490318520)
XLA Ops:
  0.0 5.0 %collective-permute-start.1 = (bf16[6,2,4096]{2,1,0:T(2,128)(2,1)}, bf16[6,2,4096]{2,1,0:T(2,128)(2,1)S(1)}, u32[]{:S(2)}, u32[]{:S(2)}) collective-permute-start(bf16[6,2,4096]{2,1,0:T(2,128)(2,1)} %bitcast.16), channel_id=1, source_target_pairs={{0,3},{1,0},{2,1},{3,2},{4,7},{5,4},{6,5},{7,6},{8,11},{9,8},{10,9... | collective-permute-start | bytes 294920 | tf_op jit(solution)/shard_map/ppermute | solution.py:395
  5.0 1.3 %prepare.1 = (bf16[6,2,4096]{2,1,0:T(2,128)(2,1)S(1)}, bf16[2,2048]{1,0:T(2,128)(2,1)S(1)}, bf16[400,128]{1,0:T(8,128)(2,1)S(1)}) custom-call(bf16[6,2,4096]{2,1,0:T(2,128)(2,1)} %bitcast.17, bf16[5,1,2,2,16,128]{5,4,3,2,1,0:T(8,128)(2,1)} %bitcast.18, s32[5,1,2,128]{3,2,1,0:T(2,128)} %refs_2_.1, s32[5,1,2,128]{3,2,1,0:T(2,128)} %refs_3_.1, ...), custom_call_target="tpu_custom_call" | custom-call | tf_op jit(solution)/shard_map/prepare/pallas_call | solution.py:72
  6.3 1.6 %collective-permute-start = (bf16[400,128]{1,0:T(8,128)(2,1)S(1)}, bf16[400,128]{1,0:T(8,128)(2,1)S(1)}, u32[]{:S(2)}, u32[]{:S(2)}) collective-permute-start(bf16[400,128]{1,0:T(8,128)(2,1)S(1)} %get-tuple-element.13.own_ref), channel_id=1, source_target_pairs={{0,4},{4,0},{1,5},{5,1},{2,6},{6,2},{3,7},{7,3},{8,12},{12,8},{9,1... | collective-permute-start | bytes 307208 | tf_op jit(solution)/shard_map/ppermute | solution.py:380
  7.9 0.9 %begin_compression.1 = (bf16[2,24,512]{2,1,0:T(8,128)(2,1)S(1)}, f32[16,2048]{1,0:T(8,128)S(1)}, bf16[2176,256]{1,0:T(8,128)(2,1)S(1)}) custom-call(bf16[6,2,4096]{2,1,0:T(2,128)(2,1)S(1)} %get-tuple-element.14.echo_ref, bf16[2,2048]{1,0:T(2,128)(2,1)S(1)} %get-tuple-element.15.chirp_ref), custom_call_target="tpu_custom_call" | custom-call | tf_op jit(solution)/shard_map/begin_compression/pallas_call | solution.py:307
  8.9 0.0 collective-permute-done.1.halo_ref
  8.9 0.6 %finish_compression.1 = (bf16[2,24,512]{2,1,0:T(8,128)(2,1)S(1)}, bf16[2,24,512]{2,1,0:T(8,128)(2,1)S(1)}) custom-call(s32[1]{0:T(128)S(6)} %add.15.index_ref, bf16[2,24,512]{2,1,0:T(8,128)(2,1)S(1)} %get-tuple-element.16.early_ref, f32[16,2048]{1,0:T(8,128)S(1)} %get-tuple-element.17.late_ref, bf16[6,2,4096]{2,1,0:T(2,128)(2,1)S(1)} %collective-permute-done.1.halo_ref, ...), custom_call_target="tpu_custom_call" | custom-call | tf_op jit(solution)/shard_map/finish_compression/pallas_call | solution.py:322
  9.4 0.1 collective-permute-start.2
  9.5 1.2 %collective-permute-done.2 = bf16[2,24,512]{2,1,0:T(8,128)(2,1)S(1)} collective-permute-done((bf16[2,24,512]{2,1,0:T(8,128)(2,1)S(1)}, bf16[2,24,512]{2,1,0:T(8,128)(2,1)S(1)}, u32[]{:S(2)}, u32[]{:S(2)}) %collective-permute-start.2) | collective-permute-done | bytes 49184 | tf_op jit(solution)/shard_map/ppermute | solution.py:380
  10.8 1.5 %collective-permute-start.3 = (bf16[48,512]{1,0:T(8,128)(2,1)S(1)}, bf16[48,512]{1,0:T(8,128)(2,1)S(1)}, u32[]{:S(2)}, u32[]{:S(2)}) collective-permute-start(bf16[48,512]{1,0:T(8,128)(2,1)S(1)} %get-tuple-element.23), channel_id=1, source_target_pairs={{0,20},{4,16},{8,28},{12,24},{16,4},{20,0},{24,12},{28,8},{1,21},{... | collective-permute-start | bytes 147464 | tf_op jit(solution)/shard_map/ppermute | solution.py:390
  12.3 0.5 %collective-permute-start.4 = (bf16[48,512]{1,0:T(8,128)(2,1)S(1)}, bf16[48,512]{1,0:T(8,128)(2,1)S(1)}, u32[]{:S(2)}, u32[]{:S(2)}) collective-permute-start(bf16[48,512]{1,0:T(8,128)(2,1)S(1)} %get-tuple-element.22), channel_id=1, source_target_pairs={{0,16},{4,20},{8,12},{12,8},{16,0},{20,4},{24,28},{28,24},{1,17},{... | collective-permute-start | bytes 147464 | tf_op jit(solution)/shard_map/ppermute | solution.py:390
  12.8 1.5 %collective-permute-start.5 = (bf16[48,512]{1,0:T(8,128)(2,1)S(1)}, bf16[48,512]{1,0:T(8,128)(2,1)S(1)}, u32[]{:S(2)}, u32[]{:S(2)}) collective-permute-start(bf16[48,512]{1,0:T(8,128)(2,1)S(1)} %get-tuple-element.21), channel_id=1, source_target_pairs={{0,4},{4,0},{8,24},{12,28},{16,20},{20,16},{24,8},{28,12},{1,5},{5... | collective-permute-start | bytes 147464 | tf_op jit(solution)/shard_map/ppermute | solution.py:390
  14.3 0.0 collective-permute-done.partner_ref
  14.3 1.3 %fold_operator.1.operator_ref = bf16[2,256,256]{2,1,0:T(8,128)(2,1)S(1)} custom-call(s32[1]{0:T(128)} %bitcast.index_ref, bf16[400,128]{1,0:T(8,128)(2,1)S(1)} %get-tuple-element.13.own_ref, bf16[400,128]{1,0:T(8,128)(2,1)S(1)} %collective-permute-done.partner_ref), custom_call_target="tpu_custom_call" | custom-call | tf_op jit(solution)/shard_map/fold_operator/pallas_call | solution.py:188
  15.6 0.2 %collective-permute-done.3.refs_0_ = bf16[48,512]{1,0:T(8,128)(2,1)S(1)} collective-permute-done((bf16[48,512]{1,0:T(8,128)(2,1)S(1)}, bf16[48,512]{1,0:T(8,128)(2,1)S(1)}, u32[]{:S(2)}, u32[]{:S(2)}) %collective-permute-start.3) | collective-permute-done | bytes 49184 | tf_op jit(solution)/shard_map/ppermute | solution.py:390
  15.9 0.9 %collective-permute-done.4.refs_1_ = bf16[48,512]{1,0:T(8,128)(2,1)S(1)} collective-permute-done((bf16[48,512]{1,0:T(8,128)(2,1)S(1)}, bf16[48,512]{1,0:T(8,128)(2,1)S(1)}, u32[]{:S(2)}, u32[]{:S(2)}) %collective-permute-start.4) | collective-permute-done | bytes 49184 | tf_op jit(solution)/shard_map/ppermute | solution.py:390
  16.7 0.1 collective-permute-done.5.refs_2_
  16.9 1.1 %form_image.1 = bf16[256,1024]{1,0:T(8,128)(2,1)} custom-call(s32[1]{0:T(128)} %bitcast.index_ref, bf16[2,256,256]{2,1,0:T(8,128)(2,1)S(1)} %fold_operator.1.operator_ref, bf16[2,48,512]{2,1,0:T(8,128)(2,1)S(1)} %constant_dynamic-update-slice_fusion.both_ref, bf16[48,512]{1,0:T(8,128)(2,1)S(1)} %collective-permute-done.3.refs_0_, ...), custom_call_target="tpu_custom_call" | custom-call | tf_op jit(solution)/shard_map/form_image/pallas_call | solution.py:363
  (3 shorter events, 0.0 us)
Async XLA Ops:
  0.0 8.9 %collective-permute-start.1 = (bf16[6,2,4096]{2,1,0:T(2,128)(2,1)}, bf16[6,2,4096]{2,1,0:T(2,128)(2,1)S(1)}, u32[]{:S(2)}, u32[]{:S(2)}) collective-permute-start(bf16[6,2,4096]{2,1,0:T(2,128)(2,1)} %bitcast.16), channel_id=1, source_target_pairs={{0,3},{1,0},{2,1},{3,2},{4,7},{5,4},{6,5},{7,6},{8,11},{9,8},{10,9... | collective-permute-start | bytes 294920 | tf_op jit(solution)/shard_map/ppermute | solution.py:395
  6.3 8.0 %collective-permute-start = (bf16[400,128]{1,0:T(8,128)(2,1)S(1)}, bf16[400,128]{1,0:T(8,128)(2,1)S(1)}, u32[]{:S(2)}, u32[]{:S(2)}) collective-permute-start(bf16[400,128]{1,0:T(8,128)(2,1)S(1)} %get-tuple-element.13.own_ref), channel_id=1, source_target_pairs={{0,4},{4,0},{1,5},{5,1},{2,6},{6,2},{3,7},{7,3},{8,12},{12,8},{9,1... | collective-permute-start | bytes 307208 | tf_op jit(solution)/shard_map/ppermute | solution.py:380
  9.4 1.3 %collective-permute-start.2 = (bf16[2,24,512]{2,1,0:T(8,128)(2,1)S(1)}, bf16[2,24,512]{2,1,0:T(8,128)(2,1)S(1)}, u32[]{:S(2)}, u32[]{:S(2)}) collective-permute-start(bf16[2,24,512]{2,1,0:T(8,128)(2,1)S(1)} %get-tuple-element.20), channel_id=1, source_target_pairs={{0,8},{8,0},{16,24},{24,16},{1,9},{9,1},{17,25},{25,17},{2,10},{10... | collective-permute-start | bytes 147464 | tf_op jit(solution)/shard_map/ppermute | solution.py:380
  10.8 5.1 %collective-permute-start.3 = (bf16[48,512]{1,0:T(8,128)(2,1)S(1)}, bf16[48,512]{1,0:T(8,128)(2,1)S(1)}, u32[]{:S(2)}, u32[]{:S(2)}) collective-permute-start(bf16[48,512]{1,0:T(8,128)(2,1)S(1)} %get-tuple-element.23), channel_id=1, source_target_pairs={{0,20},{4,16},{8,28},{12,24},{16,4},{20,0},{24,12},{28,8},{1,21},{... | collective-permute-start | bytes 147464 | tf_op jit(solution)/shard_map/ppermute | solution.py:390
  12.3 4.5 %collective-permute-start.4 = (bf16[48,512]{1,0:T(8,128)(2,1)S(1)}, bf16[48,512]{1,0:T(8,128)(2,1)S(1)}, u32[]{:S(2)}, u32[]{:S(2)}) collective-permute-start(bf16[48,512]{1,0:T(8,128)(2,1)S(1)} %get-tuple-element.22), channel_id=1, source_target_pairs={{0,16},{4,20},{8,12},{12,8},{16,0},{20,4},{24,28},{28,24},{1,17},{... | collective-permute-start | bytes 147464 | tf_op jit(solution)/shard_map/ppermute | solution.py:390
  12.8 4.1 %collective-permute-start.5 = (bf16[48,512]{1,0:T(8,128)(2,1)S(1)}, bf16[48,512]{1,0:T(8,128)(2,1)S(1)}, u32[]{:S(2)}, u32[]{:S(2)}) collective-permute-start(bf16[48,512]{1,0:T(8,128)(2,1)S(1)} %get-tuple-element.21), channel_id=1, source_target_pairs={{0,4},{4,0},{8,24},{12,28},{16,20},{20,16},{24,8},{28,12},{1,5},{5... | collective-permute-start | bytes 147464 | tf_op jit(solution)/shard_map/ppermute | solution.py:390

commit v16 on v14

--- a/solution.py
+++ b/solution.py
@@ -431,12 +431,16 @@
         echo, chirp, coef, band_start, band_width, weights, pulse_order, sections, group
     )
     has_next = (lax.axis_index("rng") < lax.axis_size("rng") - 1).astype(jnp.int32)
-    if subs == 2:
-        packed_partner = swap(packed, "sub", 1)
     early, late, table = begin_compression(echo, chirp, sections, group)
     place = section + sections * has_next
     keep, give = finish_compression(place, early, late, halo, table, group)
-    both = jnp.concatenate([keep, swap(give, "section", 1)], axis=1)
+    height = keep.shape[1]
+    both = jnp.zeros((2, 2 * height, keep.shape[2]), BF16)
+    both = lax.dynamic_update_slice(both, keep, (0, 0, 0))
+    given = swap(give, "section", 1)
+    both, packed = lax.optimization_barrier((both, packed))
+    packed_partner = swap(packed, "sub", 1) if subs == 2 else packed
+    both = lax.dynamic_update_slice(both, given, (0, height, 0))
     far = lax.dynamic_index_in_dim(both, section[0] % 2, 0, keepdims=False)
     if subs != 2:
         near = lax.dynamic_index_in_dim(both, 1 - section[0] % 2, 0, keepdims=False)

time: 18.1 us -> 17.8 us (0.983)
  waiting for transfers between devices: 2.45 us -> 2.1 us
    ppermute x2, waiting for transfers between devices: 1.21 us -> 0.16 us  [swap(): return lax.ppermute(value, axis, [(i, i ^ by) for i in range(count)])]
    ppermute x3, waiting for transfers between devices: 1.24 us -> 1.69 us  [swap_by(): return lax.ppermute(value, ('section', 'sub'), pairs)]
    ppermute x1, waiting for transfers between devices: 0.01 us -> 0.25 us  [from_next(): lax.ppermute(value, axis, [(i, (i - 1) % count) for i in range(count)])]
  transfers between devices with their start and end apart: 6 -> 6, of which waited for: 4 -> 5; matrix products, arithmetic and copies ran while one was open for 0% -> 0% of each run, Pallas kernels for 23% -> 20%
where the time goes in v16:
time: 17.8 us; the launch traced here: 17.6 us
  starting transfers between devices  10.3 us (58%)
  Pallas kernels  5.16 us (29%)
  waiting for transfers between devices  2.1 us (12%)
    ppermute x1, starting transfers between devices, from_next(): lax.ppermute(value, axis, [(i, (i - 1) % count) for i in range(count)])  5.05 us
    ppermute x3, starting transfers between devices, swap_by(): return lax.ppermute(value, ('section', 'sub'), pairs)  3.55 us
    ppermute x3, waiting for transfers between devices, swap_by(): return lax.ppermute(value, ('section', 'sub'), pairs)  1.69 us
    ppermute x2, starting transfers between devices, swap(): return lax.ppermute(value, axis, [(i, i ^ by) for i in range(count)])  1.66 us
    pallas_call x1, Pallas kernels, fold_operator(): pl.pallas_call(functools.partial(operator_kernel, dims=dims, sections=sec...  1.32 us
    pallas_call x1, Pallas kernels, prepare(): pl.pallas_call(functools.partial(prepare_kernel, sections=sections, group...  1.27 us
    pallas_call x1, Pallas kernels, form_image(): pl.pallas_call(functools.partial(image_kernel, group=group), out_shape=ja...  1.06 us
    pallas_call x1, Pallas kernels, begin_compression(): pl.pallas_call(functools.partial(begin_kernel, group=group), out_shape=(j...  0.99 us
  transfers between devices with their start and end apart: 6, of which 5 were waited for; matrix products, arithmetic and copies ran while one was open for 0% of the time, Pallas kernels for 20%

profile of v16, /device:TPU:0, one launch (start us, length us, event | category | flops | bytes accessed | tf_op | source)
XLA Modules:
  0.0 17.6 jit_solution(17911767347416370072)
XLA Ops:
  0.0 5.0 %collective-permute-start = (bf16[6,2,4096]{2,1,0:T(2,128)(2,1)}, bf16[6,2,4096]{2,1,0:T(2,128)(2,1)S(1)}, u32[]{:S(2)}, u32[]{:S(2)}) collective-permute-start(bf16[6,2,4096]{2,1,0:T(2,128)(2,1)} %bitcast.16), channel_id=1, source_target_pairs={{0,3},{1,0},{2,1},{3,2},{4,7},{5,4},{6,5},{7,6},{8,11},{9,8},{10,9... | collective-permute-start | bytes 294920 | tf_op jit(solution)/shard_map/ppermute | solution.py:415
  5.0 1.3 %prepare.1 = (bf16[6,2,4096]{2,1,0:T(2,128)(2,1)S(1)}, bf16[2,2048]{1,0:T(2,128)(2,1)S(1)}, bf16[400,128]{1,0:T(8,128)(2,1)S(1)}) custom-call(bf16[6,2,4096]{2,1,0:T(2,128)(2,1)} %bitcast.17, bf16[5,1,2,2,16,128]{5,4,3,2,1,0:T(8,128)(2,1)} %bitcast.18, s32[5,1,2,128]{3,2,1,0:T(2,128)} %refs_2_.1, s32[5,1,2,128]{3,2,1,0:T(2,128)} %refs_3_.1, ...), custom_call_target="tpu_custom_call" | custom-call | tf_op jit(solution)/shard_map/prepare/pallas_call | solution.py:72
  6.3 1.0 %begin_compression.1 = (bf16[2,24,512]{2,1,0:T(8,128)(2,1)S(1)}, f32[16,2048]{1,0:T(8,128)S(1)}, bf16[4352,256]{1,0:T(8,128)(2,1)S(1)}) custom-call(bf16[6,2,4096]{2,1,0:T(2,128)(2,1)S(1)} %get-tuple-element.15.echo_ref, bf16[2,2048]{1,0:T(2,128)(2,1)S(1)} %get-tuple-element.16.chirp_ref), custom_call_target="tpu_custom_call" | custom-call | tf_op jit(solution)/shard_map/begin_compression/pallas_call | solution.py:327
  7.3 0.3 %collective-permute-done.halo_ref = bf16[6,2,4096]{2,1,0:T(2,128)(2,1)S(1)} collective-permute-done((bf16[6,2,4096]{2,1,0:T(2,128)(2,1)}, bf16[6,2,4096]{2,1,0:T(2,128)(2,1)S(1)}, u32[]{:S(2)}, u32[]{:S(2)}) %collective-permute-start) | collective-permute-done | bytes 98336 | tf_op jit(solution)/shard_map/ppermute | solution.py:415
  7.6 0.5 %finish_compression.1 = (bf16[2,24,512]{2,1,0:T(8,128)(2,1)S(1)}, bf16[2,24,512]{2,1,0:T(8,128)(2,1)S(1)}) custom-call(s32[1]{0:T(128)S(6)} %add.17.index_ref, bf16[2,24,512]{2,1,0:T(8,128)(2,1)S(1)} %get-tuple-element.17.early_ref, f32[16,2048]{1,0:T(8,128)S(1)} %get-tuple-element.18.late_ref, bf16[6,2,4096]{2,1,0:T(2,128)(2,1)S(1)} %collective-permute-done.halo_ref, ...), custom_call_target="tpu_custom_call" | custom-call | tf_op jit(solution)/shard_map/finish_compression/pallas_call | solution.py:342
  8.1 0.1 collective-permute-start.2
  8.2 1.6 %collective-permute-start.1 = (bf16[400,128]{1,0:T(8,128)(2,1)S(1)}, bf16[400,128]{1,0:T(8,128)(2,1)S(1)}, u32[]{:S(2)}, u32[]{:S(2)}) collective-permute-start(bf16[400,128]{1,0:T(8,128)(2,1)S(1)} %get-tuple-element.22.own_ref), channel_id=1, source_target_pairs={{0,4},{4,0},{1,5},{5,1},{2,6},{6,2},{3,7},{7,3},{8,12},{12,8},{9,1... | collective-permute-start | bytes 307208 | tf_op jit(solution)/shard_map/ppermute | solution.py:400
  9.8 0.0 collective-permute-done.2
  9.8 2.1 %collective-permute-start.3 = (bf16[48,512]{1,0:T(8,128)(2,1)S(1)}, bf16[48,512]{1,0:T(8,128)(2,1)S(1)}, u32[]{:S(2)}, u32[]{:S(2)}) collective-permute-start(bf16[48,512]{1,0:T(8,128)(2,1)S(1)} %get-tuple-element.27), channel_id=1, source_target_pairs={{0,20},{4,16},{8,28},{12,24},{16,4},{20,0},{24,12},{28,8},{1,21},{... | collective-permute-start | bytes 147464 | tf_op jit(solution)/shard_map/ppermute | solution.py:410
  11.9 0.5 %collective-permute-start.4 = (bf16[48,512]{1,0:T(8,128)(2,1)S(1)}, bf16[48,512]{1,0:T(8,128)(2,1)S(1)}, u32[]{:S(2)}, u32[]{:S(2)}) collective-permute-start(bf16[48,512]{1,0:T(8,128)(2,1)S(1)} %get-tuple-element.26), channel_id=1, source_target_pairs={{0,16},{4,20},{8,12},{12,8},{16,0},{20,4},{24,28},{28,24},{1,17},{... | collective-permute-start | bytes 147464 | tf_op jit(solution)/shard_map/ppermute | solution.py:410
  12.5 0.9 %collective-permute-start.5 = (bf16[48,512]{1,0:T(8,128)(2,1)S(1)}, bf16[48,512]{1,0:T(8,128)(2,1)S(1)}, u32[]{:S(2)}, u32[]{:S(2)}) collective-permute-start(bf16[48,512]{1,0:T(8,128)(2,1)S(1)} %get-tuple-element.25), channel_id=1, source_target_pairs={{0,4},{4,0},{8,24},{12,28},{16,20},{20,16},{24,8},{28,12},{1,5},{5... | collective-permute-start | bytes 147464 | tf_op jit(solution)/shard_map/ppermute | solution.py:410
  13.4 0.2 collective-permute-done.1.partner_ref
  13.5 1.3 %fold_operator.1.operator_ref = bf16[2,256,256]{2,1,0:T(8,128)(2,1)S(1)} custom-call(s32[1]{0:T(128)} %bitcast.index_ref, bf16[400,128]{1,0:T(8,128)(2,1)S(1)} %get-tuple-element.22.own_ref, bf16[400,128]{1,0:T(8,128)(2,1)S(1)} %collective-permute-done.1.partner_ref), custom_call_target="tpu_custom_call" | custom-call | tf_op jit(solution)/shard_map/fold_operator/pallas_call | solution.py:188
  14.9 0.1 collective-permute-done.3.refs_0_
  14.9 1.2 %collective-permute-done.4.refs_1_ = bf16[48,512]{1,0:T(8,128)(2,1)S(1)} collective-permute-done((bf16[48,512]{1,0:T(8,128)(2,1)S(1)}, bf16[48,512]{1,0:T(8,128)(2,1)S(1)}, u32[]{:S(2)}, u32[]{:S(2)}) %collective-permute-start.4) | collective-permute-done | bytes 49184 | tf_op jit(solution)/shard_map/ppermute | solution.py:410
  16.1 0.4 %collective-permute-done.5.refs_2_ = bf16[48,512]{1,0:T(8,128)(2,1)S(1)} collective-permute-done((bf16[48,512]{1,0:T(8,128)(2,1)S(1)}, bf16[48,512]{1,0:T(8,128)(2,1)S(1)}, u32[]{:S(2)}, u32[]{:S(2)}) %collective-permute-start.5) | collective-permute-done | bytes 49184 | tf_op jit(solution)/shard_map/ppermute | solution.py:410
  16.6 1.1 %form_image.1 = bf16[256,1024]{1,0:T(8,128)(2,1)} custom-call(s32[1]{0:T(128)} %bitcast.index_ref, bf16[2,256,256]{2,1,0:T(8,128)(2,1)S(1)} %fold_operator.1.operator_ref, bf16[2,48,512]{2,1,0:T(8,128)(2,1)S(1)} %constant_dynamic-update-slice_fusion.both_ref, bf16[48,512]{1,0:T(8,128)(2,1)S(1)} %collective-permute-done.3.refs_0_, ...), custom_call_target="tpu_custom_call" | custom-call | tf_op jit(solution)/shard_map/form_image/pallas_call | solution.py:383
  (3 shorter events, 0.0 us)
Async XLA Ops:
  0.0 7.6 %collective-permute-start = (bf16[6,2,4096]{2,1,0:T(2,128)(2,1)}, bf16[6,2,4096]{2,1,0:T(2,128)(2,1)S(1)}, u32[]{:S(2)}, u32[]{:S(2)}) collective-permute-start(bf16[6,2,4096]{2,1,0:T(2,128)(2,1)} %bitcast.16), channel_id=1, source_target_pairs={{0,3},{1,0},{2,1},{3,2},{4,7},{5,4},{6,5},{7,6},{8,11},{9,8},{10,9... | collective-permute-start | bytes 294920 | tf_op jit(solution)/shard_map/ppermute | solution.py:415
  8.1 1.7 %collective-permute-start.2 = (bf16[2,24,512]{2,1,0:T(8,128)(2,1)S(1)}, bf16[2,24,512]{2,1,0:T(8,128)(2,1)S(1)}, u32[]{:S(2)}, u32[]{:S(2)}) collective-permute-start(bf16[2,24,512]{2,1,0:T(8,128)(2,1)S(1)} %get-tuple-element.24), channel_id=1, source_target_pairs={{0,8},{8,0},{16,24},{24,16},{1,9},{9,1},{17,25},{25,17},{2,10},{10... | collective-permute-start | bytes 147464 | tf_op jit(solution)/shard_map/ppermute | solution.py:400
  8.2 5.3 %collective-permute-start.1 = (bf16[400,128]{1,0:T(8,128)(2,1)S(1)}, bf16[400,128]{1,0:T(8,128)(2,1)S(1)}, u32[]{:S(2)}, u32[]{:S(2)}) collective-permute-start(bf16[400,128]{1,0:T(8,128)(2,1)S(1)} %get-tuple-element.22.own_ref), channel_id=1, source_target_pairs={{0,4},{4,0},{1,5},{5,1},{2,6},{6,2},{3,7},{7,3},{8,12},{12,8},{9,1... | collective-permute-start | bytes 307208 | tf_op jit(solution)/shard_map/ppermute | solution.py:400
  9.8 5.1 %collective-permute-start.3 = (bf16[48,512]{1,0:T(8,128)(2,1)S(1)}, bf16[48,512]{1,0:T(8,128)(2,1)S(1)}, u32[]{:S(2)}, u32[]{:S(2)}) collective-permute-start(bf16[48,512]{1,0:T(8,128)(2,1)S(1)} %get-tuple-element.27), channel_id=1, source_target_pairs={{0,20},{4,16},{8,28},{12,24},{16,4},{20,0},{24,12},{28,8},{1,21},{... | collective-permute-start | bytes 147464 | tf_op jit(solution)/shard_map/ppermute | solution.py:410
  11.9 4.2 %collective-permute-start.4 = (bf16[48,512]{1,0:T(8,128)(2,1)S(1)}, bf16[48,512]{1,0:T(8,128)(2,1)S(1)}, u32[]{:S(2)}, u32[]{:S(2)}) collective-permute-start(bf16[48,512]{1,0:T(8,128)(2,1)S(1)} %get-tuple-element.26), channel_id=1, source_target_pairs={{0,16},{4,20},{8,12},{12,8},{16,0},{20,4},{24,28},{28,24},{1,17},{... | collective-permute-start | bytes 147464 | tf_op jit(solution)/shard_map/ppermute | solution.py:410
  12.5 4.1 %collective-permute-start.5 = (bf16[48,512]{1,0:T(8,128)(2,1)S(1)}, bf16[48,512]{1,0:T(8,128)(2,1)S(1)}, u32[]{:S(2)}, u32[]{:S(2)}) collective-permute-start(bf16[48,512]{1,0:T(8,128)(2,1)S(1)} %get-tuple-element.25), channel_id=1, source_target_pairs={{0,4},{4,0},{8,24},{12,28},{16,20},{20,16},{24,8},{28,12},{1,5},{5... | collective-permute-start | bytes 147464 | tf_op jit(solution)/shard_map/ppermute | solution.py:410

commit v17 on v16

--- a/solution.py
+++ b/solution.py
@@ -168,15 +168,14 @@
         left.append(jnp.where(row < group // 2, pltpu.roll(turned, group - moved, 0), 0.0))
         right.append(jnp.where(row >= group // 2, pltpu.roll(turned, group // 2 - moved, 0), 0.0))
     pairs = sections // 2
-    first_core = section % 2 == 0
     for half, rest in enumerate((left, right)):
         sources = [jnp.concatenate([full[j], rest[j]], axis=0) for j in range(2 * sections)]
         quarters = [jnp.concatenate(sources[q * pairs : (q + 1) * pairs], axis=0) for q in range(4)]
         quarters = [
             quarters[0],
+            quarters[1],
             quarters[3],
-            jnp.where(first_core, quarters[1], quarters[2]),
-            jnp.where(first_core, quarters[2], quarters[1]),
+            quarters[2],
         ]
         high, low = split_two(jnp.concatenate(quarters, axis=0).T)
         out_ref[half] = jnp.concatenate([high, low], axis=1)
@@ -299,8 +298,8 @@
     for s in range(sections):
         stacked = early_ref[s] if s < ready else as_chunk(done, s - ready, chunk // LANE, group, pulses)
         slot = section ^ s
-        far_chunk, other_core = slot // 2, slot % 2
-        place = far_chunk ^ 1 ^ (section % 2) ^ other_core
+        other_core = slot % 2
+        place = 1 - slot // 2
 
         @pl.when(other_core == 0)
         def _():
@@ -349,12 +348,11 @@
     )(place, early, late, halo, table)
 
 
-def image_kernel(index_ref, operator_ref, both_ref, *refs, group):
+def image_kernel(operator_ref, both_ref, *refs, group):
     chunks, (out_ref, parts, sems) = refs[:-3], refs[-3:]
     count, _, tile = parts.shape
     width = both_ref.shape[2]
-    near = 1 - index_ref[0] % 2
-    held = [both_ref[near]] + [chunk[...] for chunk in chunks]
+    held = [both_ref[1]] + [chunk[...] for chunk in chunks]
     held = [value.astype(F32) for value in held]
     copies = []
     for i in range(count):
@@ -376,15 +374,14 @@
         copy.wait()
 
 
-def form_image(section, operator, both, chunks, group):
+def form_image(operator, both, chunks, group):
     height, half = operator.shape[1], both.shape[2]
     tile = 256 if half % 256 == 0 else half
     count = 2 * half // tile
     return pl.pallas_call(
         functools.partial(image_kernel, group=group),
         out_shape=jax.ShapeDtypeStruct((height, 2 * half), BF16),
-        in_specs=[pl.BlockSpec(memory_space=pltpu.SMEM)]
-        + [pl.BlockSpec(memory_space=pltpu.VMEM)] * (2 + len(chunks)),
+        in_specs=[pl.BlockSpec(memory_space=pltpu.VMEM)] * (2 + len(chunks)),
         out_specs=pl.BlockSpec(memory_space=pl.ANY),
         scratch_shapes=[
             pltpu.VMEM((count, height, tile), BF16),
@@ -392,7 +389,7 @@
         ],
         compiler_params=pltpu.CompilerParams(vmem_limit_bytes=16 * 1024 * 1024),
         name="form_image",
-    )(section, operator, both, *chunks)
+    )(operator, both, *chunks)
 
 
 def swap(value, axis, by):
@@ -441,18 +438,16 @@
     both, packed = lax.optimization_barrier((both, packed))
     packed_partner = swap(packed, "sub", 1) if subs == 2 else packed
     both = lax.dynamic_update_slice(both, given, (0, height, 0))
-    far = lax.dynamic_index_in_dim(both, section[0] % 2, 0, keepdims=False)
     if subs != 2:
-        near = lax.dynamic_index_in_dim(both, 1 - section[0] % 2, 0, keepdims=False)
-        chunks = [near, swap(far, "section", 2)]
+        chunks = [both[1], swap(both[0], "section", 2)]
         return merge_images(section, chunks, packed, dims, sections, group, pulses_each)
     chunks = [
-        swap_by(far, lambda s, a: (s ^ 2, a ^ 1)),
-        swap_by(both[0], lambda s, a: (s, a ^ 1) if s % 2 else (s ^ 2, a)),
-        swap_by(both[1], lambda s, a: (s ^ 2, a) if s % 2 else (s, a ^ 1)),
+        swap_by(both[0], lambda s, a: (s ^ 2, a)),
+        swap_by(both[0], lambda s, a: (s ^ 2, a ^ 1)),
+        swap_by(both[1], lambda s, a: (s, a ^ 1)),
     ]
     operator = fold_operator(section, packed, packed_partner, dims, sections, group, pulses_each)
-    image = form_image(section, operator, both, chunks, group)
+    image = form_image(operator, both, chunks, group)
     return image.reshape(2, beams, 1, image.shape[1])
 
 

time: 17.8 us -> 18.1 us (1.017)
  waiting for transfers between devices: 2.1 us -> 2.43 us
    ppermute x3, waiting for transfers between devices: 1.69 us -> 2.01 us  [swap_by(): return lax.ppermute(value, ('section', 'sub'), pairs)]
  transfers between devices with their start and end apart: 6 -> 6, of which waited for: 5 -> 4; matrix products, arithmetic and copies ran while one was open for 0% -> 0% of each run, Pallas kernels for 20% -> 20%
where the time goes in v17:
time: 18.1 us; the launch traced here: 17.9 us
  starting transfers between devices  10.3 us (57%)
  Pallas kernels  5.14 us (28%)
  waiting for transfers between devices  2.43 us (13%)
    ppermute x1, starting transfers between devices, from_next(): lax.ppermute(value, axis, [(i, (i - 1) % count) for i in range(count)])  5.05 us
    ppermute x3, starting transfers between devices, swap_by(): return lax.ppermute(value, ('section', 'sub'), pairs)  3.55 us
    ppermute x3, waiting for transfers between devices, swap_by(): return lax.ppermute(value, ('section', 'sub'), pairs)  2.01 us
    ppermute x2, starting transfers between devices, swap(): return lax.ppermute(value, axis, [(i, i ^ by) for i in range(count)])  1.66 us
    pallas_call x1, Pallas kernels, fold_operator(): pl.pallas_call(functools.partial(operator_kernel, dims=dims, sections=sec...  1.32 us
    pallas_call x1, Pallas kernels, prepare(): pl.pallas_call(functools.partial(prepare_kernel, sections=sections, group...  1.27 us
    pallas_call x1, Pallas kernels, form_image(): pl.pallas_call(functools.partial(image_kernel, group=group), out_shape=ja...  1.06 us
    pallas_call x1, Pallas kernels, begin_compression(): pl.pallas_call(functools.partial(begin_kernel, group=group), out_shape=(j...  0.99 us
  transfers between devices with their start and end apart: 6, of which 4 were waited for; matrix products, arithmetic and copies ran while one was open for 0% of the time, Pallas kernels for 20%

profile of v17, /device:TPU:0, one launch (start us, length us, event | category | flops | bytes accessed | tf_op | source)
XLA Modules:
  0.0 17.9 jit_solution(14879904026410630574)
XLA Ops:
  0.0 5.0 %collective-permute-start = (bf16[6,2,4096]{2,1,0:T(2,128)(2,1)}, bf16[6,2,4096]{2,1,0:T(2,128)(2,1)S(1)}, u32[]{:S(2)}, u32[]{:S(2)}) collective-permute-start(bf16[6,2,4096]{2,1,0:T(2,128)(2,1)} %bitcast.14), channel_id=1, source_target_pairs={{0,3},{1,0},{2,1},{3,2},{4,7},{5,4},{6,5},{7,6},{8,11},{9,8},{10,9... | collective-permute-start | bytes 294920 | tf_op jit(solution)/shard_map/ppermute | solution.py:412
  5.0 1.3 %prepare.1 = (bf16[6,2,4096]{2,1,0:T(2,128)(2,1)S(1)}, bf16[2,2048]{1,0:T(2,128)(2,1)S(1)}, bf16[400,128]{1,0:T(8,128)(2,1)S(1)}) custom-call(bf16[6,2,4096]{2,1,0:T(2,128)(2,1)} %bitcast.15, bf16[5,1,2,2,16,128]{5,4,3,2,1,0:T(8,128)(2,1)} %bitcast.16, s32[5,1,2,128]{3,2,1,0:T(2,128)} %refs_2_.1, s32[5,1,2,128]{3,2,1,0:T(2,128)} %refs_3_.1, ...), custom_call_target="tpu_custom_call" | custom-call | tf_op jit(solution)/shard_map/prepare/pallas_call | solution.py:72
  6.3 1.0 %begin_compression.1 = (bf16[2,24,512]{2,1,0:T(8,128)(2,1)S(1)}, f32[16,2048]{1,0:T(8,128)S(1)}, bf16[4352,256]{1,0:T(8,128)(2,1)S(1)}) custom-call(bf16[6,2,4096]{2,1,0:T(2,128)(2,1)S(1)} %get-tuple-element.15.echo_ref, bf16[2,2048]{1,0:T(2,128)(2,1)S(1)} %get-tuple-element.16.chirp_ref), custom_call_target="tpu_custom_call" | custom-call | tf_op jit(solution)/shard_map/begin_compression/pallas_call | solution.py:326
  7.3 0.2 %collective-permute-done.halo_ref = bf16[6,2,4096]{2,1,0:T(2,128)(2,1)S(1)} collective-permute-done((bf16[6,2,4096]{2,1,0:T(2,128)(2,1)}, bf16[6,2,4096]{2,1,0:T(2,128)(2,1)S(1)}, u32[]{:S(2)}, u32[]{:S(2)}) %collective-permute-start) | collective-permute-done | bytes 98336 | tf_op jit(solution)/shard_map/ppermute | solution.py:412
  7.6 0.5 %finish_compression.1 = (bf16[2,24,512]{2,1,0:T(8,128)(2,1)S(1)}, bf16[2,24,512]{2,1,0:T(8,128)(2,1)S(1)}) custom-call(s32[1]{0:T(128)S(6)} %add.9.index_ref, bf16[2,24,512]{2,1,0:T(8,128)(2,1)S(1)} %get-tuple-element.17.early_ref, f32[16,2048]{1,0:T(8,128)S(1)} %get-tuple-element.18.late_ref, bf16[6,2,4096]{2,1,0:T(2,128)(2,1)S(1)} %collective-permute-done.halo_ref, ...), custom_call_target="tpu_custom_call" | custom-call | tf_op jit(solution)/shard_map/finish_compression/pallas_call | solution.py:341
  8.1 0.1 collective-permute-start.2
  8.2 1.6 %collective-permute-start.1 = (bf16[400,128]{1,0:T(8,128)(2,1)S(1)}, bf16[400,128]{1,0:T(8,128)(2,1)S(1)}, u32[]{:S(2)}, u32[]{:S(2)}) collective-permute-start(bf16[400,128]{1,0:T(8,128)(2,1)S(1)} %get-tuple-element.22.own_ref), channel_id=1, source_target_pairs={{0,4},{4,0},{1,5},{5,1},{2,6},{6,2},{3,7},{7,3},{8,12},{12,8},{9,1... | collective-permute-start | bytes 307208 | tf_op jit(solution)/shard_map/ppermute | solution.py:397
  9.8 0.0 collective-permute-done.2
  9.8 1.6 %collective-permute-start.3 = (bf16[48,512]{1,0:T(8,128)(2,1)S(1)}, bf16[48,512]{1,0:T(8,128)(2,1)S(1)}, u32[]{:S(2)}, u32[]{:S(2)}) collective-permute-start(bf16[48,512]{1,0:T(8,128)(2,1)S(1)} %get-tuple-element.26), channel_id=1, source_target_pairs={{0,16},{4,20},{8,24},{12,28},{16,0},{20,4},{24,8},{28,12},{1,17},{... | collective-permute-start | bytes 147464 | tf_op jit(solution)/shard_map/ppermute | solution.py:407
  11.4 1.1 %collective-permute-start.4 = (bf16[48,512]{1,0:T(8,128)(2,1)S(1)}, bf16[48,512]{1,0:T(8,128)(2,1)S(1)}, u32[]{:S(2)}, u32[]{:S(2)}) collective-permute-start(bf16[48,512]{1,0:T(8,128)(2,1)S(1)} %get-tuple-element.26), channel_id=1, source_target_pairs={{0,20},{4,16},{8,28},{12,24},{16,4},{20,0},{24,12},{28,8},{1,21},{... | collective-permute-start | bytes 147464 | tf_op jit(solution)/shard_map/ppermute | solution.py:407
  12.5 0.9 %collective-permute-start.5 = (bf16[48,512]{1,0:T(8,128)(2,1)S(1)}, bf16[48,512]{1,0:T(8,128)(2,1)S(1)}, u32[]{:S(2)}, u32[]{:S(2)}) collective-permute-start(bf16[48,512]{1,0:T(8,128)(2,1)S(1)} %get-tuple-element.25), channel_id=1, source_target_pairs={{0,4},{4,0},{8,12},{12,8},{16,20},{20,16},{24,28},{28,24},{1,5},{5... | collective-permute-start | bytes 147464 | tf_op jit(solution)/shard_map/ppermute | solution.py:407
  13.3 0.2 collective-permute-done.1.partner_ref
  13.5 1.3 %fold_operator.1.operator_ref = bf16[2,256,256]{2,1,0:T(8,128)(2,1)S(1)} custom-call(s32[1]{0:T(128)} %bitcast.index_ref, bf16[400,128]{1,0:T(8,128)(2,1)S(1)} %get-tuple-element.22.own_ref, bf16[400,128]{1,0:T(8,128)(2,1)S(1)} %collective-permute-done.1.partner_ref), custom_call_target="tpu_custom_call" | custom-call | tf_op jit(solution)/shard_map/fold_operator/pallas_call | solution.py:187
  14.9 0.0 collective-permute-done.3.refs_0_
  14.9 1.5 %collective-permute-done.4.refs_1_ = bf16[48,512]{1,0:T(8,128)(2,1)S(1)} collective-permute-done((bf16[48,512]{1,0:T(8,128)(2,1)S(1)}, bf16[48,512]{1,0:T(8,128)(2,1)S(1)}, u32[]{:S(2)}, u32[]{:S(2)}) %collective-permute-start.4) | collective-permute-done | bytes 49184 | tf_op jit(solution)/shard_map/ppermute | solution.py:407
  16.4 0.5 %collective-permute-done.5.refs_2_ = bf16[48,512]{1,0:T(8,128)(2,1)S(1)} collective-permute-done((bf16[48,512]{1,0:T(8,128)(2,1)S(1)}, bf16[48,512]{1,0:T(8,128)(2,1)S(1)}, u32[]{:S(2)}, u32[]{:S(2)}) %collective-permute-start.5) | collective-permute-done | bytes 49184 | tf_op jit(solution)/shard_map/ppermute | solution.py:407
  16.9 1.1 %form_image.1 = bf16[256,1024]{1,0:T(8,128)(2,1)} custom-call(bf16[2,256,256]{2,1,0:T(8,128)(2,1)S(1)} %fold_operator.1.operator_ref, bf16[2,48,512]{2,1,0:T(8,128)(2,1)S(1)} %constant_dynamic-update-slice_fusion.both_ref, bf16[48,512]{1,0:T(8,128)(2,1)S(1)} %collective-permute-done.3.refs_0_, bf16[48,512]{1,0:T(8,128)(2,1)S(1)} %collective-permute-done.4.refs_1_, ...), custom_call_target="tpu_custom_call" | custom-call | tf_op jit(solution)/shard_map/form_image/pallas_call | solution.py:381
  (3 shorter events, 0.0 us)
Async XLA Ops:
  0.0 7.6 %collective-permute-start = (bf16[6,2,4096]{2,1,0:T(2,128)(2,1)}, bf16[6,2,4096]{2,1,0:T(2,128)(2,1)S(1)}, u32[]{:S(2)}, u32[]{:S(2)}) collective-permute-start(bf16[6,2,4096]{2,1,0:T(2,128)(2,1)} %bitcast.14), channel_id=1, source_target_pairs={{0,3},{1,0},{2,1},{3,2},{4,7},{5,4},{6,5},{7,6},{8,11},{9,8},{10,9... | collective-permute-start | bytes 294920 | tf_op jit(solution)/shard_map/ppermute | solution.py:412
  8.1 1.7 %collective-permute-start.2 = (bf16[2,24,512]{2,1,0:T(8,128)(2,1)S(1)}, bf16[2,24,512]{2,1,0:T(8,128)(2,1)S(1)}, u32[]{:S(2)}, u32[]{:S(2)}) collective-permute-start(bf16[2,24,512]{2,1,0:T(8,128)(2,1)S(1)} %get-tuple-element.24), channel_id=1, source_target_pairs={{0,8},{8,0},{16,24},{24,16},{1,9},{9,1},{17,25},{25,17},{2,10},{10... | collective-permute-start | bytes 147464 | tf_op jit(solution)/shard_map/ppermute | solution.py:397
  8.2 5.3 %collective-permute-start.1 = (bf16[400,128]{1,0:T(8,128)(2,1)S(1)}, bf16[400,128]{1,0:T(8,128)(2,1)S(1)}, u32[]{:S(2)}, u32[]{:S(2)}) collective-permute-start(bf16[400,128]{1,0:T(8,128)(2,1)S(1)} %get-tuple-element.22.own_ref), channel_id=1, source_target_pairs={{0,4},{4,0},{1,5},{5,1},{2,6},{6,2},{3,7},{7,3},{8,12},{12,8},{9,1... | collective-permute-start | bytes 307208 | tf_op jit(solution)/shard_map/ppermute | solution.py:397
  9.8 5.1 %collective-permute-start.3 = (bf16[48,512]{1,0:T(8,128)(2,1)S(1)}, bf16[48,512]{1,0:T(8,128)(2,1)S(1)}, u32[]{:S(2)}, u32[]{:S(2)}) collective-permute-start(bf16[48,512]{1,0:T(8,128)(2,1)S(1)} %get-tuple-element.26), channel_id=1, source_target_pairs={{0,16},{4,20},{8,24},{12,28},{16,0},{20,4},{24,8},{28,12},{1,17},{... | collective-permute-start | bytes 147464 | tf_op jit(solution)/shard_map/ppermute | solution.py:407
  11.4 5.0 %collective-permute-start.4 = (bf16[48,512]{1,0:T(8,128)(2,1)S(1)}, bf16[48,512]{1,0:T(8,128)(2,1)S(1)}, u32[]{:S(2)}, u32[]{:S(2)}) collective-permute-start(bf16[48,512]{1,0:T(8,128)(2,1)S(1)} %get-tuple-element.26), channel_id=1, source_target_pairs={{0,20},{4,16},{8,28},{12,24},{16,4},{20,0},{24,12},{28,8},{1,21},{... | collective-permute-start | bytes 147464 | tf_op jit(solution)/shard_map/ppermute | solution.py:407
  12.5 4.4 %collective-permute-start.5 = (bf16[48,512]{1,0:T(8,128)(2,1)S(1)}, bf16[48,512]{1,0:T(8,128)(2,1)S(1)}, u32[]{:S(2)}, u32[]{:S(2)}) collective-permute-start(bf16[48,512]{1,0:T(8,128)(2,1)S(1)} %get-tuple-element.25), channel_id=1, source_target_pairs={{0,4},{4,0},{8,12},{12,8},{16,20},{20,16},{24,28},{28,24},{1,5},{5... | collective-permute-start | bytes 147464 | tf_op jit(solution)/shard_map/ppermute | solution.py:407

commit v18 on v17

--- a/solution.py
+++ b/solution.py
@@ -173,8 +173,8 @@
         quarters = [jnp.concatenate(sources[q * pairs : (q + 1) * pairs], axis=0) for q in range(4)]
         quarters = [
             quarters[0],
+            quarters[3],
             quarters[1],
-            quarters[3],
             quarters[2],
         ]
         high, low = split_two(jnp.concatenate(quarters, axis=0).T)
@@ -442,8 +442,8 @@
         chunks = [both[1], swap(both[0], "section", 2)]
         return merge_images(section, chunks, packed, dims, sections, group, pulses_each)
     chunks = [
+        swap_by(both[0], lambda s, a: (s ^ 2, a ^ 1)),
         swap_by(both[0], lambda s, a: (s ^ 2, a)),
-        swap_by(both[0], lambda s, a: (s ^ 2, a ^ 1)),
         swap_by(both[1], lambda s, a: (s, a ^ 1)),
     ]
     operator = fold_operator(section, packed, packed_partner, dims, sections, group, pulses_each)

time: 18.1 us -> 17.7 us (0.978)
  waiting for transfers between devices: 2.43 us -> 2.11 us
    ppermute x3, waiting for transfers between devices: 2.01 us -> 1.69 us  [swap_by(): return lax.ppermute(value, ('section', 'sub'), pairs)]
  transfers between devices with their start and end apart: 6 -> 6, of which waited for: 4 -> 5; matrix products, arithmetic and copies ran while one was open for 0% -> 0% of each run, Pallas kernels for 20% -> 20%
where the time goes in v18:
time: 17.7 us; the launch traced here: 17.6 us
  starting transfers between devices  10.3 us (58%)
  Pallas kernels  5.15 us (29%)
  waiting for transfers between devices  2.11 us (12%)
    ppermute x1, starting transfers between devices, from_next(): lax.ppermute(value, axis, [(i, (i - 1) % count) for i in range(count)])  5.05 us
    ppermute x3, starting transfers between devices, swap_by(): return lax.ppermute(value, ('section', 'sub'), pairs)  3.55 us
    ppermute x3, waiting for transfers between devices, swap_by(): return lax.ppermute(value, ('section', 'sub'), pairs)  1.69 us
    ppermute x2, starting transfers between devices, swap(): return lax.ppermute(value, axis, [(i, i ^ by) for i in range(count)])  1.66 us
    pallas_call x1, Pallas kernels, fold_operator(): pl.pallas_call(functools.partial(operator_kernel, dims=dims, sections=sec...  1.32 us
    pallas_call x1, Pallas kernels, prepare(): pl.pallas_call(functools.partial(prepare_kernel, sections=sections, group...  1.27 us
    pallas_call x1, Pallas kernels, form_image(): pl.pallas_call(functools.partial(image_kernel, group=group), out_shape=ja...  1.06 us
    pallas_call x1, Pallas kernels, begin_compression(): pl.pallas_call(functools.partial(begin_kernel, group=group), out_shape=(j...  0.99 us
  transfers between devices with their start and end apart: 6, of which 5 were waited for; matrix products, arithmetic and copies ran while one was open for 0% of the time, Pallas kernels for 20%

profile of v18, /device:TPU:0, one launch (start us, length us, event | category | flops | bytes accessed | tf_op | source)
XLA Modules:
  0.0 17.6 jit_solution(5767172966064344735)
XLA Ops:
  0.0 5.0 %collective-permute-start = (bf16[6,2,4096]{2,1,0:T(2,128)(2,1)}, bf16[6,2,4096]{2,1,0:T(2,128)(2,1)S(1)}, u32[]{:S(2)}, u32[]{:S(2)}) collective-permute-start(bf16[6,2,4096]{2,1,0:T(2,128)(2,1)} %bitcast.14), channel_id=1, source_target_pairs={{0,3},{1,0},{2,1},{3,2},{4,7},{5,4},{6,5},{7,6},{8,11},{9,8},{10,9... | collective-permute-start | bytes 294920 | tf_op jit(solution)/shard_map/ppermute | solution.py:412
  5.0 1.3 %prepare.1 = (bf16[6,2,4096]{2,1,0:T(2,128)(2,1)S(1)}, bf16[2,2048]{1,0:T(2,128)(2,1)S(1)}, bf16[400,128]{1,0:T(8,128)(2,1)S(1)}) custom-call(bf16[6,2,4096]{2,1,0:T(2,128)(2,1)} %bitcast.15, bf16[5,1,2,2,16,128]{5,4,3,2,1,0:T(8,128)(2,1)} %bitcast.16, s32[5,1,2,128]{3,2,1,0:T(2,128)} %refs_2_.1, s32[5,1,2,128]{3,2,1,0:T(2,128)} %refs_3_.1, ...), custom_call_target="tpu_custom_call" | custom-call | tf_op jit(solution)/shard_map/prepare/pallas_call | solution.py:72
  6.3 1.0 %begin_compression.1 = (bf16[2,24,512]{2,1,0:T(8,128)(2,1)S(1)}, f32[16,2048]{1,0:T(8,128)S(1)}, bf16[4352,256]{1,0:T(8,128)(2,1)S(1)}) custom-call(bf16[6,2,4096]{2,1,0:T(2,128)(2,1)S(1)} %get-tuple-element.15.echo_ref, bf16[2,2048]{1,0:T(2,128)(2,1)S(1)} %get-tuple-element.16.chirp_ref), custom_call_target="tpu_custom_call" | custom-call | tf_op jit(solution)/shard_map/begin_compression/pallas_call | solution.py:326
  7.3 0.2 %collective-permute-done.halo_ref = bf16[6,2,4096]{2,1,0:T(2,128)(2,1)S(1)} collective-permute-done((bf16[6,2,4096]{2,1,0:T(2,128)(2,1)}, bf16[6,2,4096]{2,1,0:T(2,128)(2,1)S(1)}, u32[]{:S(2)}, u32[]{:S(2)}) %collective-permute-start) | collective-permute-done | bytes 98336 | tf_op jit(solution)/shard_map/ppermute | solution.py:412
  7.6 0.5 %finish_compression.1 = (bf16[2,24,512]{2,1,0:T(8,128)(2,1)S(1)}, bf16[2,24,512]{2,1,0:T(8,128)(2,1)S(1)}) custom-call(s32[1]{0:T(128)S(6)} %add.9.index_ref, bf16[2,24,512]{2,1,0:T(8,128)(2,1)S(1)} %get-tuple-element.17.early_ref, f32[16,2048]{1,0:T(8,128)S(1)} %get-tuple-element.18.late_ref, bf16[6,2,4096]{2,1,0:T(2,128)(2,1)S(1)} %collective-permute-done.halo_ref, ...), custom_call_target="tpu_custom_call" | custom-call | tf_op jit(solution)/shard_map/finish_compression/pallas_call | solution.py:341
  8.1 0.1 collective-permute-start.2
  8.2 1.6 %collective-permute-start.1 = (bf16[400,128]{1,0:T(8,128)(2,1)S(1)}, bf16[400,128]{1,0:T(8,128)(2,1)S(1)}, u32[]{:S(2)}, u32[]{:S(2)}) collective-permute-start(bf16[400,128]{1,0:T(8,128)(2,1)S(1)} %get-tuple-element.22.own_ref), channel_id=1, source_target_pairs={{0,4},{4,0},{1,5},{5,1},{2,6},{6,2},{3,7},{7,3},{8,12},{12,8},{9,1... | collective-permute-start | bytes 307208 | tf_op jit(solution)/shard_map/ppermute | solution.py:397
  9.8 0.0 collective-permute-done.2
  9.8 2.1 %collective-permute-start.3 = (bf16[48,512]{1,0:T(8,128)(2,1)S(1)}, bf16[48,512]{1,0:T(8,128)(2,1)S(1)}, u32[]{:S(2)}, u32[]{:S(2)}) collective-permute-start(bf16[48,512]{1,0:T(8,128)(2,1)S(1)} %get-tuple-element.26), channel_id=1, source_target_pairs={{0,20},{4,16},{8,28},{12,24},{16,4},{20,0},{24,12},{28,8},{1,21},{... | collective-permute-start | bytes 147464 | tf_op jit(solution)/shard_map/ppermute | solution.py:407
  11.9 0.5 %collective-permute-start.4 = (bf16[48,512]{1,0:T(8,128)(2,1)S(1)}, bf16[48,512]{1,0:T(8,128)(2,1)S(1)}, u32[]{:S(2)}, u32[]{:S(2)}) collective-permute-start(bf16[48,512]{1,0:T(8,128)(2,1)S(1)} %get-tuple-element.26), channel_id=1, source_target_pairs={{0,16},{4,20},{8,24},{12,28},{16,0},{20,4},{24,8},{28,12},{1,17},{... | collective-permute-start | bytes 147464 | tf_op jit(solution)/shard_map/ppermute | solution.py:407
  12.5 0.9 %collective-permute-start.5 = (bf16[48,512]{1,0:T(8,128)(2,1)S(1)}, bf16[48,512]{1,0:T(8,128)(2,1)S(1)}, u32[]{:S(2)}, u32[]{:S(2)}) collective-permute-start(bf16[48,512]{1,0:T(8,128)(2,1)S(1)} %get-tuple-element.25), channel_id=1, source_target_pairs={{0,4},{4,0},{8,12},{12,8},{16,20},{20,16},{24,28},{28,24},{1,5},{5... | collective-permute-start | bytes 147464 | tf_op jit(solution)/shard_map/ppermute | solution.py:407
  13.4 0.2 collective-permute-done.1.partner_ref
  13.5 1.3 %fold_operator.1.operator_ref = bf16[2,256,256]{2,1,0:T(8,128)(2,1)S(1)} custom-call(s32[1]{0:T(128)} %bitcast.index_ref, bf16[400,128]{1,0:T(8,128)(2,1)S(1)} %get-tuple-element.22.own_ref, bf16[400,128]{1,0:T(8,128)(2,1)S(1)} %collective-permute-done.1.partner_ref), custom_call_target="tpu_custom_call" | custom-call | tf_op jit(solution)/shard_map/fold_operator/pallas_call | solution.py:187
  14.9 0.2 collective-permute-done.3.refs_0_
  15.0 1.0 %collective-permute-done.4.refs_1_ = bf16[48,512]{1,0:T(8,128)(2,1)S(1)} collective-permute-done((bf16[48,512]{1,0:T(8,128)(2,1)S(1)}, bf16[48,512]{1,0:T(8,128)(2,1)S(1)}, u32[]{:S(2)}, u32[]{:S(2)}) %collective-permute-start.4) | collective-permute-done | bytes 49184 | tf_op jit(solution)/shard_map/ppermute | solution.py:407
  16.0 0.5 %collective-permute-done.5.refs_2_ = bf16[48,512]{1,0:T(8,128)(2,1)S(1)} collective-permute-done((bf16[48,512]{1,0:T(8,128)(2,1)S(1)}, bf16[48,512]{1,0:T(8,128)(2,1)S(1)}, u32[]{:S(2)}, u32[]{:S(2)}) %collective-permute-start.5) | collective-permute-done | bytes 49184 | tf_op jit(solution)/shard_map/ppermute | solution.py:407
  16.5 1.1 %form_image.1 = bf16[256,1024]{1,0:T(8,128)(2,1)} custom-call(bf16[2,256,256]{2,1,0:T(8,128)(2,1)S(1)} %fold_operator.1.operator_ref, bf16[2,48,512]{2,1,0:T(8,128)(2,1)S(1)} %constant_dynamic-update-slice_fusion.both_ref, bf16[48,512]{1,0:T(8,128)(2,1)S(1)} %collective-permute-done.3.refs_0_, bf16[48,512]{1,0:T(8,128)(2,1)S(1)} %collective-permute-done.4.refs_1_, ...), custom_call_target="tpu_custom_call" | custom-call | tf_op jit(solution)/shard_map/form_image/pallas_call | solution.py:381
  (3 shorter events, 0.0 us)
Async XLA Ops:
  0.0 7.6 %collective-permute-start = (bf16[6,2,4096]{2,1,0:T(2,128)(2,1)}, bf16[6,2,4096]{2,1,0:T(2,128)(2,1)S(1)}, u32[]{:S(2)}, u32[]{:S(2)}) collective-permute-start(bf16[6,2,4096]{2,1,0:T(2,128)(2,1)} %bitcast.14), channel_id=1, source_target_pairs={{0,3},{1,0},{2,1},{3,2},{4,7},{5,4},{6,5},{7,6},{8,11},{9,8},{10,9... | collective-permute-start | bytes 294920 | tf_op jit(solution)/shard_map/ppermute | solution.py:412
  8.1 1.7 %collective-permute-start.2 = (bf16[2,24,512]{2,1,0:T(8,128)(2,1)S(1)}, bf16[2,24,512]{2,1,0:T(8,128)(2,1)S(1)}, u32[]{:S(2)}, u32[]{:S(2)}) collective-permute-start(bf16[2,24,512]{2,1,0:T(8,128)(2,1)S(1)} %get-tuple-element.24), channel_id=1, source_target_pairs={{0,8},{8,0},{16,24},{24,16},{1,9},{9,1},{17,25},{25,17},{2,10},{10... | collective-permute-start | bytes 147464 | tf_op jit(solution)/shard_map/ppermute | solution.py:397
  8.2 5.3 %collective-permute-start.1 = (bf16[400,128]{1,0:T(8,128)(2,1)S(1)}, bf16[400,128]{1,0:T(8,128)(2,1)S(1)}, u32[]{:S(2)}, u32[]{:S(2)}) collective-permute-start(bf16[400,128]{1,0:T(8,128)(2,1)S(1)} %get-tuple-element.22.own_ref), channel_id=1, source_target_pairs={{0,4},{4,0},{1,5},{5,1},{2,6},{6,2},{3,7},{7,3},{8,12},{12,8},{9,1... | collective-permute-start | bytes 307208 | tf_op jit(solution)/shard_map/ppermute | solution.py:397
  9.8 5.2 %collective-permute-start.3 = (bf16[48,512]{1,0:T(8,128)(2,1)S(1)}, bf16[48,512]{1,0:T(8,128)(2,1)S(1)}, u32[]{:S(2)}, u32[]{:S(2)}) collective-permute-start(bf16[48,512]{1,0:T(8,128)(2,1)S(1)} %get-tuple-element.26), channel_id=1, source_target_pairs={{0,20},{4,16},{8,28},{12,24},{16,4},{20,0},{24,12},{28,8},{1,21},{... | collective-permute-start | bytes 147464 | tf_op jit(solution)/shard_map/ppermute | solution.py:407
  11.9 4.1 %collective-permute-start.4 = (bf16[48,512]{1,0:T(8,128)(2,1)S(1)}, bf16[48,512]{1,0:T(8,128)(2,1)S(1)}, u32[]{:S(2)}, u32[]{:S(2)}) collective-permute-start(bf16[48,512]{1,0:T(8,128)(2,1)S(1)} %get-tuple-element.26), channel_id=1, source_target_pairs={{0,16},{4,20},{8,24},{12,28},{16,0},{20,4},{24,8},{28,12},{1,17},{... | collective-permute-start | bytes 147464 | tf_op jit(solution)/shard_map/ppermute | solution.py:407
  12.5 4.1 %collective-permute-start.5 = (bf16[48,512]{1,0:T(8,128)(2,1)S(1)}, bf16[48,512]{1,0:T(8,128)(2,1)S(1)}, u32[]{:S(2)}, u32[]{:S(2)}) collective-permute-start(bf16[48,512]{1,0:T(8,128)(2,1)S(1)} %get-tuple-element.25), channel_id=1, source_target_pairs={{0,4},{4,0},{8,12},{12,8},{16,20},{20,16},{24,28},{28,24},{1,5},{5... | collective-permute-start | bytes 147464 | tf_op jit(solution)/shard_map/ppermute | solution.py:407
